TPU v7x, 128 devices: a whole 4x4x4 slice. The times are simulated.
128 devices in a mesh: shard: 8 (over y_lo, z), ctx: 4 (over x), tp: 4 (over y_hi, core).
Axes of the slice: x: 4, y: 4 (y_hi: 2, y_lo: 2; y = y_hi * 2 + y_lo), z: 4, core: 2. Of those that a mesh axis runs over, the one named last changes fastest.
Arguments:
- tokens: bfloat16 [20480, 768], P(('shard', 'ctx', 'tp')), may hold values from -6 to 6
- parents: int32 [8, 20], P('shard'), may hold values from -1 to 19, as said below
- query_weight: bfloat16 [768, 768], P('shard', 'tp'), may hold values from -0.21875 to 0.21875
- query_bias: float32 [768], P('tp'), may hold values from -3 to 3
- key_weight: bfloat16 [768, 768], P('shard', 'tp'), may hold values from -0.21875 to 0.21875
- value_weight: bfloat16 [768, 768], P('shard', 'tp'), may hold values from -0.21875 to 0.21875
- value_bias: float32 [768], P('tp'), may hold values from -3 to 3
- output_weight: bfloat16 [768, 768], P('tp', 'shard'), may hold values from -2 to 2
- output_bias: float32 [768], replicated, may hold values from -3 to 3
- first_gain: float32 [768], replicated, may hold values from 0.1 to 1.9
- first_shift: float32 [768], replicated, may hold values from -3 to 3
- inner_weight: bfloat16 [768, 3072], P('shard', 'tp'), may hold values from -0.21875 to 0.21875
- inner_bias: float32 [3072], P('tp'), may hold values from -3 to 3
- outer_weight: bfloat16 [3072, 768], P('tp', 'shard'), may hold values from -0.109375 to 0.109375
- outer_bias: float32 [768], replicated, may hold values from -3 to 3
- second_gain: float32 [768], replicated, may hold values from 0.1 to 1.9
- second_shift: float32 [768], replicated, may hold values from -3 to 3
- mask_logits: float32 [12, 512, 512], P('tp', 'shard'), may hold values from -6 to 6
- mask_noise: float32 [12, 512, 512], P('tp', 'shard'), may hold values from -5 to 5
- cotangent: bfloat16 [20480, 768], P(('shard', 'ctx', 'tp')), may hold values from -6 to 6
Outputs:
- result: bfloat16 [20480, 768], P(('shard', 'ctx', 'tp'))
- tokens_grad: float32 [20480, 768], P(('shard', 'ctx', 'tp'))
- query_weight_grad: float32 [768, 768], P('shard', 'tp')
- query_bias_grad: float32 [768], P('tp')
- key_weight_grad: float32 [768, 768], P('shard', 'tp')
- value_weight_grad: float32 [768, 768], P('shard', 'tp')
- value_bias_grad: float32 [768], P('tp')
- output_weight_grad: float32 [768, 768], P('tp', 'shard')
- output_bias_grad: float32 [768], replicated
- first_gain_grad: float32 [768], replicated
- first_shift_grad: float32 [768], replicated
- inner_weight_grad: float32 [768, 3072], P('shard', 'tp')
- inner_bias_grad: float32 [3072], P('tp')
- outer_weight_grad: float32 [3072, 768], P('tp', 'shard')
- outer_bias_grad: float32 [768], replicated
- second_gain_grad: float32 [768], replicated
- second_shift_grad: float32 [768], replicated
- mask_logits_grad: float32 [12, 512, 512], P('tp', 'shard')
Inputs may be any that keep to these rules, and one draw needn't show every extreme that they name: `parents`: each group's 20 segments form 1 trees: a chain of 8 trunk segments, 4 branch segments whose parent is the trunk's last, and 2 leaf segments under each branch. Writing L = 20 // 4, tree t holds, for every c, the L segments c * 20 // 4 + t * L to c * 20 // 4 + (t + 1) * L - 1.
All inputs are finite; a program needn't handle non-finite values.
Results may differ from a plain program's by a relative error of at most 0.023.
Values may be sent and summed in bfloat16 or wider, within the bound.
A program may use at most 192 MiB of HBM per device.

v0:
```python
import jax
import jax.numpy as jnp
from jax import lax
from jax.sharding import PartitionSpec as P

HEADS = 12
HEAD_DIM = 64
DEPTHS = 512
SEG_LEN = 128
TREE_SEGS = 20


def layer_norm(values, gain_vector, shift_vector):
    centre = jnp.mean(values, axis=-1, keepdims=True)
    spread = jnp.mean(jnp.square(values - centre), axis=-1, keepdims=True)
    return (values - centre) * lax.rsqrt(spread + 1e-05) * gain_vector + shift_vector


def gelu_exact(values):
    return jax.nn.gelu(values, approximate=False)


def tree_tables(parent_row):
    segment_count = parent_row.shape[0]
    segment_ids = jnp.arange(segment_count, dtype=jnp.int32)
    current = segment_ids
    reachable = current[:, None] == segment_ids[None, :]
    strict = jnp.zeros((segment_count,), jnp.int32)
    for climb in range(segment_count):
        safe_index = jnp.maximum(current, 0)
        upper = jnp.where(current >= 0, jnp.take(parent_row, safe_index), -1)
        reachable = reachable | (upper[:, None] == segment_ids[None, :])
        strict = strict + (upper >= 0).astype(jnp.int32)
        current = upper
    segment_tile = strict * SEG_LEN % DEPTHS // SEG_LEN
    return (reachable, segment_tile)


def gather_rows(values):
    return lax.all_gather(values, "tp", axis=0, tiled=True)


def sum_rows(values):
    return lax.psum_scatter(values, "tp", scatter_dimension=0, tiled=True)


def block_scores(query_heads, key_heads, tiles, reach_pair, query_hot, key_hot):
    heads_local = tiles.shape[0]
    query_segs = query_hot.shape[0]
    key_segs = key_hot.shape[0]
    plain_scores = jnp.einsum(
        "qhd,khd->hqk", query_heads, key_heads, preferred_element_type=jnp.float32
    ) * HEAD_DIM ** (-0.5)
    partial_bias = jnp.einsum(
        "hxpyq,by->hxpbq", tiles, key_hot, preferred_element_type=jnp.float32
    ).astype(jnp.bfloat16)
    mask_bias = jnp.einsum(
        "ax,hxpbq->hapbq", query_hot, partial_bias, preferred_element_type=jnp.float32
    )
    scores = plain_scores.reshape(heads_local, query_segs, SEG_LEN, key_segs, SEG_LEN) + mask_bias
    scores = jnp.where(reach_pair[None, :, None, :, None], scores, -1e30)
    return scores.reshape(heads_local, query_segs * SEG_LEN, key_segs * SEG_LEN)


def attend_forward(
    queries, key_trees, value_trees, tiles, reach_blocks, query_hots, key_hots, block_rows
):
    heads_local = tiles.shape[0]
    row_count, width = queries.shape
    head_size = width // heads_local
    trees = reach_blocks.shape[0]

    def one_block(inputs):
        query_block, key_block, value_block, reach_pair, query_hot, key_hot = inputs
        query_heads = query_block.reshape(block_rows, heads_local, head_size)
        key_heads = key_block.reshape(key_block.shape[0], heads_local, head_size)
        value_heads = value_block.reshape(value_block.shape[0], heads_local, head_size)
        scores = block_scores(query_heads, key_heads, tiles, reach_pair, query_hot, key_hot)
        row_peak = jnp.max(scores, axis=-1, keepdims=True)
        exponent = jnp.exp(scores - row_peak)
        row_total = jnp.sum(exponent, axis=-1, keepdims=True)
        soft_low = (exponent / row_total).astype(jnp.bfloat16)
        attended_block = jnp.einsum(
            "hqk,khd->qhd", soft_low, value_heads, preferred_element_type=jnp.float32
        )
        return (
            attended_block.reshape(block_rows, width).astype(jnp.bfloat16),
            row_peak[:, :, 0] + jnp.log(row_total[:, :, 0]),
        )

    attended, log_totals = lax.map(
        one_block,
        (
            queries.reshape(trees, block_rows, width),
            key_trees,
            value_trees,
            reach_blocks,
            query_hots,
            key_hots,
        ),
    )
    return (attended.reshape(row_count, width), log_totals)


def attend_backward(
    queries,
    key_trees,
    value_trees,
    tiles,
    reach_blocks,
    query_hots,
    key_hots,
    block_rows,
    log_totals,
    mixed_grad,
):
    heads_local = tiles.shape[0]
    row_count, width = queries.shape
    head_size = width // heads_local
    trees = reach_blocks.shape[0]
    score_scale = HEAD_DIM ** (-0.5)

    def one_block(table_acc, inputs):
        (
            query_block,
            grad_block,
            key_block,
            value_block,
            reach_pair,
            query_hot,
            key_hot,
            total_block,
        ) = inputs
        key_count = key_block.shape[0]
        query_heads = query_block.reshape(block_rows, heads_local, head_size)
        grad_heads = grad_block.reshape(block_rows, heads_local, head_size)
        key_heads = key_block.reshape(key_count, heads_local, head_size)
        value_heads = value_block.reshape(key_count, heads_local, head_size)
        scores = block_scores(query_heads, key_heads, tiles, reach_pair, query_hot, key_hot)
        soft = jnp.exp(scores - total_block[:, :, None])
        soft_low = soft.astype(jnp.bfloat16)
        soft_grad = jnp.einsum(
            "qhd,khd->hqk", grad_heads, value_heads, preferred_element_type=jnp.float32
        )
        value_grad = jnp.einsum(
            "hqk,qhd->khd", soft_low, grad_heads, preferred_element_type=jnp.float32
        ).reshape(key_count, width)
        score_grad = soft * (soft_grad - jnp.sum(soft * soft_grad, axis=-1, keepdims=True))
        score_low = score_grad.astype(jnp.bfloat16)
        query_grad = (
            jnp.einsum("hqk,khd->qhd", score_low, key_heads, preferred_element_type=jnp.float32)
            * score_scale
        )
        key_grad = (
            jnp.einsum(
                "hqk,qhd->khd", score_low, query_heads, preferred_element_type=jnp.float32
            ).reshape(key_count, width)
            * score_scale
        )
        score_tiles = score_low.reshape(
            heads_local, query_hot.shape[0], SEG_LEN, key_hot.shape[0], SEG_LEN
        )
        by_query = jnp.einsum(
            "hapbq,ax->hxpbq", score_tiles, query_hot, preferred_element_type=jnp.float32
        )
        by_both = jnp.einsum(
            "hxpbq,by->hxpyq",
            by_query,
            key_hot.astype(jnp.float32),
            precision=lax.Precision.HIGHEST,
        )
        table_acc = table_acc + by_both.reshape(heads_local, DEPTHS, DEPTHS)
        return (table_acc, (query_grad.reshape(block_rows, width), key_grad, value_grad))

    start_table = jnp.zeros((heads_local, DEPTHS, DEPTHS), jnp.float32)
    table_acc, block_grads = lax.scan(
        one_block,
        start_table,
        (
            queries.reshape(trees, block_rows, width),
            mixed_grad.reshape(trees, block_rows, width),
            key_trees,
            value_trees,
            reach_blocks,
            query_hots,
            key_hots,
            log_totals,
        ),
    )
    return (block_grads[0].reshape(row_count, width), block_grads[1], block_grads[2], table_acc)


def shards(
    tokens,
    parents,
    query_weight,
    query_bias,
    key_weight,
    value_weight,
    value_bias,
    output_weight,
    output_bias,
    first_gain,
    first_shift,
    inner_weight,
    inner_bias,
    outer_weight,
    outer_bias,
    second_gain,
    second_shift,
    mask_logits,
    mask_noise,
    cotangent,
):
    tp_count = lax.axis_size("tp")
    ctx_count = lax.axis_size("ctx")
    ctx_index = lax.axis_index("ctx")
    heads_local = HEADS // tp_count
    tile_count = DEPTHS // SEG_LEN
    relaxed_low = jax.nn.log_sigmoid(mask_logits + mask_noise).astype(jnp.bfloat16)
    weight_set = (
        lax.all_gather(query_weight, "shard", axis=0, tiled=True),
        lax.all_gather(key_weight, "shard", axis=0, tiled=True),
        lax.all_gather(value_weight, "shard", axis=0, tiled=True),
        lax.all_gather(inner_weight, "shard", axis=0, tiled=True),
        lax.all_gather(output_weight, "shard", axis=1, tiled=True),
        lax.all_gather(outer_weight, "shard", axis=1, tiled=True),
        lax.all_gather(relaxed_low, "shard", axis=1, tiled=True),
    )
    reachable, segment_tile = tree_tables(parents[0])
    full_rows = gather_rows(tokens)
    row_count = full_rows.shape[0]
    block_rows = SEG_LEN * TREE_SEGS // ctx_count
    trees = row_count // block_rows
    block_segs = block_rows // SEG_LEN
    local_segs = row_count // SEG_LEN
    tree_ids = jnp.arange(trees, dtype=jnp.int32)
    inner_ids = jnp.arange(block_segs, dtype=jnp.int32)
    ctx_ids = jnp.arange(ctx_count, dtype=jnp.int32)
    query_segs = ctx_index * local_segs + tree_ids[:, None] * block_segs + inner_ids[None, :]
    key_segs = (
        ctx_ids[None, :, None] * local_segs
        + tree_ids[:, None, None] * block_segs
        + inner_ids[None, None, :]
    ).reshape(trees, ctx_count * block_segs)
    reach_blocks = reachable[query_segs[:, :, None], key_segs[:, None, :]]
    tile_ids = jnp.arange(tile_count, dtype=jnp.int32)
    query_hots = (segment_tile[query_segs][..., None] == tile_ids).astype(jnp.bfloat16)
    key_hots = (segment_tile[key_segs][..., None] == tile_ids).astype(jnp.bfloat16)

    def by_tree(values):
        width = values.shape[1]
        return (
            values.reshape(ctx_count, trees, block_rows, width)
            .transpose(1, 0, 2, 3)
            .reshape(trees, ctx_count * block_rows, width)
        )

    def from_tree(values):
        width = values.shape[2]
        return (
            values.reshape(trees, ctx_count, block_rows, width)
            .transpose(1, 0, 2, 3)
            .reshape(ctx_count * row_count, width)
        )

    queries = (
        jnp.dot(full_rows, weight_set[0], preferred_element_type=jnp.float32) + query_bias
    ).astype(jnp.bfloat16)
    keys_local = jnp.dot(full_rows, weight_set[1], preferred_element_type=jnp.float32).astype(
        jnp.bfloat16
    )
    values_local = (
        jnp.dot(full_rows, weight_set[2], preferred_element_type=jnp.float32) + value_bias
    ).astype(jnp.bfloat16)
    keys_all, values_all = (
        lax.all_gather(keys_local, "ctx", axis=0, tiled=True),
        lax.all_gather(values_local, "ctx", axis=0, tiled=True),
    )
    tiles = weight_set[6].reshape(heads_local, tile_count, SEG_LEN, tile_count, SEG_LEN)
    attended, log_totals = attend_forward(
        queries,
        by_tree(keys_all),
        by_tree(values_all),
        tiles,
        reach_blocks,
        query_hots,
        key_hots,
        block_rows,
    )
    attn_sum = (
        sum_rows(jnp.dot(attended, weight_set[4], preferred_element_type=jnp.float32)) + output_bias
    )
    first_out, first_back = jax.vjp(
        layer_norm, tokens.astype(jnp.float32) + attn_sum, first_gain, first_shift
    )
    first_rows = gather_rows(first_out.astype(jnp.bfloat16))
    inner_pre = jnp.dot(first_rows, weight_set[3], preferred_element_type=jnp.float32) + inner_bias
    activated, gelu_back = jax.vjp(gelu_exact, inner_pre)
    act_low = activated.astype(jnp.bfloat16)
    outer_sum = (
        sum_rows(jnp.dot(act_low, weight_set[5], preferred_element_type=jnp.float32)) + outer_bias
    )
    second_out, second_back = jax.vjp(layer_norm, first_out + outer_sum, second_gain, second_shift)
    result = second_out.astype(jnp.bfloat16)
    weight_back = (
        lax.all_gather(query_weight, "shard", axis=0, tiled=True),
        lax.all_gather(key_weight, "shard", axis=0, tiled=True),
        lax.all_gather(value_weight, "shard", axis=0, tiled=True),
        lax.all_gather(inner_weight, "shard", axis=0, tiled=True),
        lax.all_gather(output_weight, "shard", axis=1, tiled=True),
        lax.all_gather(outer_weight, "shard", axis=1, tiled=True),
        lax.all_gather(relaxed_low, "shard", axis=1, tiled=True),
    )
    keys_back, values_back = (
        lax.all_gather(keys_local, "ctx", axis=0, tiled=True),
        lax.all_gather(values_local, "ctx", axis=0, tiled=True),
    )
    second_grad, second_gain_grad, second_shift_grad = second_back(cotangent.astype(jnp.float32))
    outer_low = second_grad.astype(jnp.bfloat16)
    outer_bias_grad = jnp.sum(outer_low.astype(jnp.float32), axis=0)
    outer_rows = gather_rows(outer_low)
    outer_weight_grad = jnp.einsum(
        "rf,rd->fd", act_low, outer_rows, preferred_element_type=jnp.float32
    )
    act_grad = jnp.einsum(
        "rd,fd->rf", outer_rows, weight_back[5], preferred_element_type=jnp.float32
    )
    inner_low = gelu_back(act_grad)[0].astype(jnp.bfloat16)
    inner_bias_grad = jnp.sum(inner_low.astype(jnp.float32), axis=0)
    inner_weight_grad = jnp.einsum(
        "rd,rf->df", first_rows, inner_low, preferred_element_type=jnp.float32
    )
    first_grad = (
        sum_rows(
            jnp.einsum("rf,df->rd", inner_low, weight_back[3], preferred_element_type=jnp.float32)
        )
        + second_grad
    )
    first_in_grad, first_gain_grad, first_shift_grad = first_back(first_grad)
    attn_low = first_in_grad.astype(jnp.bfloat16)
    output_bias_grad = jnp.sum(attn_low.astype(jnp.float32), axis=0)
    attn_rows = gather_rows(attn_low)
    output_weight_grad = jnp.einsum(
        "rh,rd->hd", attended, attn_rows, preferred_element_type=jnp.float32
    )
    mixed_grad = jnp.einsum(
        "rd,hd->rh", attn_rows, weight_back[4], preferred_element_type=jnp.float32
    ).astype(jnp.bfloat16)
    tiles_back = weight_back[6].reshape(heads_local, tile_count, SEG_LEN, tile_count, SEG_LEN)
    query_grad, key_tree_grad, value_tree_grad, table_grad = attend_backward(
        queries,
        by_tree(keys_back),
        by_tree(values_back),
        tiles_back,
        reach_blocks,
        query_hots,
        key_hots,
        block_rows,
        log_totals,
        mixed_grad,
    )
    key_part, value_part = (
        lax.psum_scatter(
            from_tree(key_tree_grad).astype(jnp.bfloat16), "ctx", scatter_dimension=0, tiled=True
        ).astype(jnp.float32),
        lax.psum_scatter(
            from_tree(value_tree_grad).astype(jnp.bfloat16), "ctx", scatter_dimension=0, tiled=True
        ).astype(jnp.float32),
    )
    query_low = query_grad.astype(jnp.bfloat16)
    key_low = key_part.astype(jnp.bfloat16)
    value_low = value_part.astype(jnp.bfloat16)
    query_bias_grad = jnp.sum(query_low.astype(jnp.float32), axis=0)
    value_bias_grad = jnp.sum(value_low.astype(jnp.float32), axis=0)
    query_weight_grad = jnp.einsum(
        "rd,rh->dh", full_rows, query_low, preferred_element_type=jnp.float32
    )
    key_weight_grad = jnp.einsum(
        "rd,rh->dh", full_rows, key_low, preferred_element_type=jnp.float32
    )
    value_weight_grad = jnp.einsum(
        "rd,rh->dh", full_rows, value_low, preferred_element_type=jnp.float32
    )
    token_terms = jnp.einsum(
        "rh,dh->rd", query_low, weight_back[0], preferred_element_type=jnp.float32
    )
    token_terms = token_terms + jnp.einsum(
        "rh,dh->rd", key_low, weight_back[1], preferred_element_type=jnp.float32
    )
    token_terms = token_terms + jnp.einsum(
        "rh,dh->rd", value_low, weight_back[2], preferred_element_type=jnp.float32
    )
    tokens_grad = sum_rows(token_terms) + first_in_grad
    shard_part = (
        lax.psum_scatter(
            query_weight_grad.astype(jnp.bfloat16), "shard", scatter_dimension=0, tiled=True
        ).astype(jnp.float32),
        lax.psum_scatter(
            key_weight_grad.astype(jnp.bfloat16), "shard", scatter_dimension=0, tiled=True
        ).astype(jnp.float32),
        lax.psum_scatter(
            value_weight_grad.astype(jnp.bfloat16), "shard", scatter_dimension=0, tiled=True
        ).astype(jnp.float32),
        lax.psum_scatter(
            inner_weight_grad.astype(jnp.bfloat16), "shard", scatter_dimension=0, tiled=True
        ).astype(jnp.float32),
        lax.psum_scatter(
            output_weight_grad.astype(jnp.bfloat16), "shard", scatter_dimension=1, tiled=True
        ).astype(jnp.float32),
        lax.psum_scatter(
            outer_weight_grad.astype(jnp.bfloat16), "shard", scatter_dimension=1, tiled=True
        ).astype(jnp.float32),
        lax.psum_scatter(
            table_grad.astype(jnp.bfloat16), "shard", scatter_dimension=1, tiled=True
        ).astype(jnp.float32),
    )
    reduced = (
        lax.psum(shard_part[0].astype(jnp.bfloat16), "ctx").astype(jnp.float32),
        lax.psum(shard_part[1].astype(jnp.bfloat16), "ctx").astype(jnp.float32),
        lax.psum(shard_part[2].astype(jnp.bfloat16), "ctx").astype(jnp.float32),
        lax.psum(shard_part[3].astype(jnp.bfloat16), "ctx").astype(jnp.float32),
        lax.psum(shard_part[4].astype(jnp.bfloat16), "ctx").astype(jnp.float32),
        lax.psum(shard_part[5].astype(jnp.bfloat16), "ctx").astype(jnp.float32),
        lax.psum(shard_part[6].astype(jnp.bfloat16), "ctx").astype(jnp.float32),
    )
    mask_logits_grad = reduced[6] * jax.nn.sigmoid(-(mask_logits + mask_noise))
    head_totals = lax.psum((query_bias_grad, value_bias_grad, inner_bias_grad), ("shard", "ctx"))
    row_totals = lax.psum(
        (
            output_bias_grad,
            outer_bias_grad,
            first_gain_grad,
            first_shift_grad,
            second_gain_grad,
            second_shift_grad,
        ),
        ("shard", "ctx", "tp"),
    )
    return (
        result,
        tokens_grad,
        reduced[0],
        head_totals[0],
        reduced[1],
        reduced[2],
        head_totals[1],
        reduced[4],
        row_totals[0],
        row_totals[2],
        row_totals[3],
        reduced[3],
        head_totals[2],
        reduced[5],
        row_totals[1],
        row_totals[4],
        row_totals[5],
        mask_logits_grad,
    )


def solution(mesh):
    in_specs = (
        P(("shard", "ctx", "tp"), None),
        P("shard", None),
        P("shard", "tp"),
        P("tp"),
        P("shard", "tp"),
        P("shard", "tp"),
        P("tp"),
        P("tp", "shard"),
        P(),
        P(),
        P(),
        P("shard", "tp"),
        P("tp"),
        P("tp", "shard"),
        P(),
        P(),
        P(),
        P("tp", "shard", None),
        P("tp", "shard", None),
        P(("shard", "ctx", "tp"), None),
    )
    out_specs = (
        P(("shard", "ctx", "tp"), None),
        P(("shard", "ctx", "tp"), None),
        P("shard", "tp"),
        P("tp"),
        P("shard", "tp"),
        P("shard", "tp"),
        P("tp"),
        P("tp", "shard"),
        P(),
        P(),
        P(),
        P("shard", "tp"),
        P("tp"),
        P("tp", "shard"),
        P(),
        P(),
        P(),
        P("tp", "shard", None),
    )
    return jax.shard_map(shards, mesh=mesh, in_specs=in_specs, out_specs=out_specs, check_vma=False)
```

profile of v0, /device:TPU:8, one launch (start us, length us, event | category | flops | bytes accessed | tf_op | source)
XLA Modules:
  0.0 1081.3 jit_solution(1416112534243558571)
XLA Ops:
  7.3 2.0 fusion.46
  24.6 2.0 gather_fusion
  28.3 15.7 %all_gather.48 = bf16[640,768]{1,0:T(8,128)(2,1)S(1)} all-gather(bf16[160,768]{1,0:T(8,128)(2,1)S(1)} %copy-done.24), channel_id=1, replica_groups=mesh['shard'=8,'ctx'=4,'tp'=4] {'tp'}, dimensions={0}, use_global_device_ids=true | all-gather | bytes 1228800 | tf_op jit(solution)/shard_map/all_gather | solution.py:40
  44.0 29.2 %all_gather.52 = bf16[768,192]{1,0:T(8,128)(2,1)S(1)} all-gather(bf16[96,192]{1,0:T(8,128)(2,1)S(1)} %copy-done.33), channel_id=1, replica_groups=mesh['shard'=8,'ctx'=4,'tp'=4] {'shard'}, dimensions={0}, use_global_device_ids=true | all-gather | bytes 331776 | tf_op jit(solution)/shard_map/all_gather | solution.py:223
  73.2 28.9 %all_gather.51 = bf16[768,192]{1,0:T(8,128)(2,1)S(1)} all-gather(bf16[96,192]{1,0:T(8,128)(2,1)S(1)} %copy-done.34), channel_id=1, replica_groups=mesh['shard'=8,'ctx'=4,'tp'=4] {'shard'}, dimensions={0}, use_global_device_ids=true | all-gather | bytes 331776 | tf_op jit(solution)/shard_map/all_gather | solution.py:222
  103.2 14.3 %all_gather.53 = bf16[2560,192]{0,1:T(8,128)(2,1)S(1)} all-gather(bf16[640,192]{0,1:T(8,128)(2,1)S(1)} %convolution_convert_fusion.7), channel_id=1, replica_groups=mesh['shard'=8,'ctx'=4,'tp'=4] {'ctx'}, dimensions={0}, use_global_device_ids=true | all-gather | bytes 1228800 | tf_op jit(solution)/shard_map/all_gather | solution.py:277
  118.5 8.3 broadcast_multiply_fusion
  126.7 21.9 %reshape.492 = f32[3,5,128,20,128]{4,3,2,1,0:T(8,128)} reshape(f32[3,640,2560]{2,1,0:T(8,128)} %broadcast_multiply_fusion) | data formatting | bytes 39321600 | tf_op jit(solution)/shard_map/while/body/eval_jaxpr/reshape | solution.py:60
  148.7 28.8 %all_gather.49 = bf16[768,192]{1,0:T(8,128)(2,1)S(1)} all-gather(bf16[96,192]{1,0:T(8,128)(2,1)S(1)} %copy-done.35), channel_id=1, replica_groups=mesh['shard'=8,'ctx'=4,'tp'=4] {'shard'}, dimensions={0}, use_global_device_ids=true | all-gather | bytes 331776 | tf_op jit(solution)/shard_map/all_gather | solution.py:224
  177.6 28.6 %all_gather.55 = bf16[192,768]{0,1:T(8,128)(2,1)S(1)} all-gather(bf16[192,96]{0,1:T(8,128)(2,1)S(1)} %copy.56), channel_id=1, replica_groups=mesh['shard'=8,'ctx'=4,'tp'=4] {'shard'}, dimensions={1}, use_global_device_ids=true | all-gather | bytes 331776 | tf_op jit(solution)/shard_map/all_gather | solution.py:226
  206.7 14.1 %all_gather.50 = bf16[2560,192]{0,1:T(8,128)(2,1)S(1)} all-gather(bf16[640,192]{0,1:T(8,128)(2,1)S(1)} %fusion.30), channel_id=1, replica_groups=mesh['shard'=8,'ctx'=4,'tp'=4] {'ctx'}, dimensions={0}, use_global_device_ids=true | all-gather | bytes 1228800 | tf_op jit(solution)/shard_map/all_gather | solution.py:278
  220.8 2.7 reshape.493
  223.6 5.1 convert_bitcast_fusion
  228.7 35.3 %fusion.114 = (f32[3,5,128]{1,2,0:T(8,128)S(1)}, f32[3,5,128,20,128]{4,1,3,2,0:T(8,128)}) fusion(s32[5]{0:T(128)S(1)} %gather_fusion.2, bf16[3,4,128,20,128]{4,3,2,1,0:T(8,128)(2,1)} %convert_bitcast_fusion, f32[3,5,128,20,128]{4,3,2,1,0:T(8,128)} %reshape.492, pred[5,20]{0,1:T(8,128)(4,1)S(1)} %copy.50), kind=kOutput, calls=%fused_computation.327 | convolution fusion | flops 54065300 | bytes 47193720 | tf_op jit(solution)/shard_map/while/body/eval_jaxpr/ax,hxpbq->hapbq/dot_general | solution.py:57
  264.1 14.1 %exponential_reduce_fusion = f32[3,5,128]{1,2,0:T(8,128)S(1)} fusion(f32[3,5,128,20,128]{4,1,3,2,0:T(8,128)} %get-tuple-element.225, f32[3,5,128]{1,2,0:T(8,128)S(1)} %get-tuple-element.224), kind=kLoop, calls=%fused_computation.25 | loop fusion | flops 9828480 | bytes 19676160 | tf_op jit(solution)/shard_map/while/body/eval_jaxpr/reduce_sum | solution.py:81
  278.2 4.9 copy-done.2
  283.1 9.5 copy.53
  292.6 22.4 %reshape.494 = f32[3,640,2560]{2,1,0:T(8,128)} reshape(f32[3,5,128,20,128]{4,3,2,1,0:T(8,128)} %copy.53) | data formatting | bytes 39321600 | tf_op jit(solution)/shard_map/while/body/eval_jaxpr/reshape | solution.py:62
  315.0 8.5 fusion.33
  323.6 1.8 fusion.115
  326.8 35.8 %reduce-scatter.26.cloned.1.call-done = f32[160,768]{1,0:T(8,128)} async-done(((f32[640,768]{1,0:T(8,128)}), f32[160,768]{1,0:T(8,128)}) %reduce-scatter.26.cloned.1.call-update) | async-done | bytes 491536 | tf_op jit(solution)/shard_map/reduce_scatter | solution.py:44
  364.2 10.8 all_gather.56
  375.0 28.2 %all-gather.6.cloned.1.call-done = bf16[768,768]{1,0:T(8,128)(2,1)} async-done(((bf16[96,768]{1,0:T(8,128)(2,1)}), bf16[768,768]{1,0:T(8,128)(2,1)}) %all-gather.6.cloned.1.call-update) | async-done | bytes 1179664 | tf_op jit(solution)/shard_map/all_gather | solution.py:225
  403.1 7.5 multiply_convert_fusion.1
  410.7 32.5 %all-gather.8.cloned.1.call-done = bf16[768,768]{0,1:T(8,128)(2,1)} async-done(((bf16[768,96]{0,1:T(8,128)(2,1)}), bf16[768,768]{0,1:T(8,128)(2,1)}) %all-gather.8.cloned.1.call-update) | async-done | bytes 1179664 | tf_op jit(solution)/shard_map/all_gather | solution.py:227
  443.1 3.8 fusion.116
  447.0 36.6 %reduce-scatter.28.cloned.1.call-done = f32[160,768]{1,0:T(8,128)} async-done(((f32[640,768]{1,0:T(8,128)}), f32[160,768]{1,0:T(8,128)}) %reduce-scatter.28.cloned.1.call-update) | async-done | bytes 491536 | tf_op jit(solution)/shard_map/reduce_scatter | solution.py:44
  486.2 10.8 all_gather.59
  499.4 2.3 fusion.117
  501.8 37.1 %reduce-scatter.30.cloned.1.call-done = f32[160,768]{1,0:T(8,128)} async-done(((f32[640,768]{1,0:T(8,128)}), f32[160,768]{1,0:T(8,128)}) %reduce-scatter.30.cloned.1.call-update) | async-done | bytes 491536 | tf_op jit(solution)/shard_map/reduce_scatter | solution.py:44
  538.9 2.2 multiply_reduce_fusion.1
  542.2 10.8 all_gather.60
  553.5 16.1 %multiply_reduce_fusion = (f32[3,640]{1,0:T(4,128)S(1)}, f32[3,640,2560]{2,1,0:T(8,128)}) fusion(f32[3,640,2560]{2,1,0:T(8,128)} %reshape.494, f32[3,640]{1,0:T(4,128)S(1)} %get-tuple-element.176, bf16[640,3,64]{0,2,1:T(8,128)(2,1)S(1)} %bitcast.161, bf16[2560,3,64]{0,2,1:T(8,128)(2,1)S(1)} %bitcast.159), kind=kOutput, calls=%fused_computation.27 | convolution fusion | flops 643889280 | bytes 40565760 | tf_op jit(solution)/shard_map/while/body/eval_jaxpr/qhd,khd->hqk/dot_general | solution.py:142
  569.6 9.9 fusion.15
  581.0 13.6 %multiply_convert_fusion = bf16[3,640,2560]{2,1,0:T(8,128)(2,1)S(1)} fusion(f32[3,640,2560]{2,1,0:T(8,128)} %get-tuple-element.228, f32[3,640,2560]{2,1,0:T(8,128)} %reshape.494, f32[3,640]{1,0:T(4,128)S(1)} %get-tuple-element.227, f32[3,640]{1,0:T(4,128)S(1)} %get-tuple-element.176), kind=kLoop, calls=%fused_computation.26 | loop fusion | flops 19660800 | bytes 49167360 | tf_op jit(solution)/shard_map/while/body/eval_jaxpr/convert_element_type | solution.py:149
  594.7 1.8 fusion.14
  596.5 1.9 copy-done.3
  601.4 7.1 convert_reduce_fusion.5
  612.3 20.2 %reduce-scatter.40.cloned.1.call-done = bf16[640,192]{1,0:T(8,128)(2,1)} async-done(((bf16[2560,192]{1,0:T(8,128)(2,1)}), bf16[640,192]{1,0:T(8,128)(2,1)}) %reduce-scatter.40.cloned.1.call-update) | async-done | bytes 245776
  635.0 3.4 convolution_convert_fusion
  638.7 3.4 convolution_convert_fusion.1
  642.2 17.2 %reshape.496 = bf16[3,5,128,20,128]{4,3,2,1,0:T(8,128)(2,1)} reshape(bf16[3,640,2560]{2,1,0:T(8,128)(2,1)} %copy-done.3) | data formatting | bytes 19660800 | tf_op jit(solution)/shard_map/while/body/eval_jaxpr/reshape | solution.py:160
  659.4 15.3 %fusion.11 = f32[3,4,128,20,128]{4,1,3,2,0:T(4,128)} fusion(bf16[3,5,128,20,128]{4,3,2,1,0:T(8,128)(2,1)} %reshape.496, s32[5]{0:T(128)S(1)} %gather_fusion.2), kind=kOutput, calls=%fused_computation.41 | convolution fusion | flops 39321620 | bytes 25559060 | tf_op jit(solution)/shard_map/while/body/eval_jaxpr/hapbq,ax->hxpbq/dot_general | solution.py:163
  674.7 12.2 %fusion.27 = bf16[3,4,128,4,128]{4,3,2,1,0:T(4,128)(2,1)S(1)} fusion(f32[3,4,128,20,128]{4,1,3,2,0:T(4,128)} %fusion.11, s32[20]{0:T(128)S(1)} %copy-done.40), kind=kOutput, calls=%fused_computation.67 | convolution fusion | flops 189530192 | bytes 17301584 | tf_op jit(solution)/shard_map/while/body/eval_jaxpr/hxpbq,by->hxpyq/dot_general | solution.py:166
  687.0 2.0 convert_element_type.327
  689.1 1.6 copy.77
  690.7 19.5 %reduce-scatter.44.cloned.1.call-done = bf16[96,192]{1,0:T(8,128)(2,1)} async-done(((bf16[768,192]{1,0:T(8,128)(2,1)}), bf16[96,192]{1,0:T(8,128)(2,1)}) %reduce-scatter.44.cloned.1.call-update) | async-done | bytes 36880
  710.2 1.5 copy.71
  711.7 37.4 %reduce-scatter.48.cloned.1.call-done = bf16[96,192]{1,0:T(8,128)(2,1)} async-done(((bf16[768,192]{1,0:T(8,128)(2,1)}), bf16[96,192]{1,0:T(8,128)(2,1)}) %reduce-scatter.48.cloned.1.call-update) | async-done | bytes 36880
  749.1 1.5 copy.75
  750.6 37.0 %reduce-scatter.46.cloned.1.call-done = bf16[96,192]{1,0:T(8,128)(2,1)} async-done(((bf16[768,192]{1,0:T(8,128)(2,1)}), bf16[96,192]{1,0:T(8,128)(2,1)}) %reduce-scatter.46.cloned.1.call-update) | async-done | bytes 36880
  789.9 38.5 %reduce-scatter.36.cloned.1.call-done = bf16[768,96]{0,1:T(8,128)(2,1)} async-done(((bf16[768,768]{0,1:T(8,128)(2,1)}), bf16[768,96]{0,1:T(8,128)(2,1)}) %reduce-scatter.36.cloned.1.call-update) | async-done | bytes 147472 | tf_op jit(solution)/shard_map/reduce_scatter | solution.py:411
  828.5 40.6 %reduce-scatter.34.cloned.1.call-done = bf16[96,768]{1,0:T(8,128)(2,1)} async-done(((bf16[768,768]{1,0:T(8,128)(2,1)}), bf16[96,768]{1,0:T(8,128)(2,1)}) %reduce-scatter.34.cloned.1.call-update) | async-done | bytes 147472 | tf_op jit(solution)/shard_map/reduce_scatter | solution.py:405
  869.0 42.1 %reduce-scatter.38.cloned.1.call-done = bf16[3,64,512]{2,1,0:T(8,128)(2,1)} async-done(((bf16[3,512,512]{2,1,0:T(8,128)(2,1)}), bf16[3,64,512]{2,1,0:T(8,128)(2,1)}) %reduce-scatter.38.cloned.1.call-update) | async-done | bytes 196624 | tf_op jit(solution)/shard_map/reduce_scatter | solution.py:414
  911.7 1.8 add_add_fusion
  913.6 65.0 %all-reduce = (f32[768]{0:T(1024)}, f32[768]{0:T(1024)}, f32[768]{0:T(1024)}, f32[768]{0:T(1024)}, f32[768]{0:T(1024)}, /*index=5*/f32[768]{0:T(1024)}) all-reduce(f32[768]{0:T(1024)S(1)} %get-tuple-element.171, f32[768]{0:T(1024)S(1)} %get-tuple-element.145, ...), channel_id=1, replica_groups=mesh['shard'=8,'ctx'=4,'tp'=4] {'shard','ctx','tp'}, use_global_device_ids=true, to_apply=%region_32.34 | all-reduce | flops 4608 | bytes 36864 | tf_op jit(solution)/shard_map/psum | solution.py:429
  979.0 82.2 %all-reduce.1 = (f32[192]{0:T(256)}, f32[192]{0:T(256)}, f32[768]{0:T(1024)}) all-reduce(f32[192]{0:T(256)S(1)} %reduce_sum.238, f32[192]{0:T(256)S(1)} %convert_reduce_fusion.4, f32[768]{0:T(1024)S(1)} %get-tuple-element.174), channel_id=1, replica_groups=mesh['shard'=8,'ctx'=4,'tp'=4] {'shard','ctx'}, use_global_device_ids=true, to_apply=%region_22.24 | all-reduce | flops 1152 | bytes 9216 | tf_op jit(solution)/shard_map/psum | solution.py:428
  1062.6 1.5 copy.59
  1064.1 1.5 copy.60
  1065.7 1.5 copy.61
  1067.2 1.6 convert_element_type.320
  1068.9 1.6 convert_element_type.323
  1070.5 1.8 divide_multiply_fusion
  1072.3 1.9 add.432
  (274 shorter events, 44.9 us)
Async XLA Ops:
  7.2 2.2 copy-start
  7.2 213.6 %all-gather.4.cloned.1.call-start = ((), (), s32[]{:S(2)}) async-start(), calls=%async_computation.13 | async-start | bytes 1769472 | tf_op jit(solution)/shard_map/all_gather | solution.py:228
  9.3 353.3 %reduce-scatter.26.cloned.1.call-start = ((), (), s32[]{:S(2)}) async-start(), calls=%async_computation.14 | async-start | bytes 2457600 | tf_op jit(solution)/shard_map/reduce_scatter | solution.py:44
  21.7 6.6 copy-start.24
  23.2 20.8 %copy-start.33 = (bf16[96,192]{1,0:T(8,128)(2,1)S(1)}, bf16[96,192]{1,0:T(8,128)(2,1)}, u32[]{:S(2)}) copy-start(bf16[96,192]{1,0:T(8,128)(2,1)} %param.26) | copy-start | bytes 110596
  24.1 49.1 %copy-start.34 = (bf16[96,192]{1,0:T(8,128)(2,1)S(1)}, bf16[96,192]{1,0:T(8,128)(2,1)}, u32[]{:S(2)}) copy-start(bf16[96,192]{1,0:T(8,128)(2,1)} %param.24) | copy-start | bytes 110596
  27.7 195.9 %copy-start.39 = (s32[20]{0:T(128)}, s32[20]{0:T(128)S(1)}, u32[]{:S(2)}) copy-start(s32[20]{0:T(128)S(1)} %gather_fusion.1) | copy-start | bytes 244
  28.3 74.3 %copy-start.44 = (f32[192]{0:T(256)S(1)}, f32[192]{0:T(256)}, u32[]{:S(2)}) copy-start(f32[192]{0:T(256)} %param.25) | copy-start | bytes 2308
  44.0 162.2 %copy-start.4 = (bf16[640,768]{1,0:T(8,128)(2,1)}, bf16[640,768]{1,0:T(8,128)(2,1)S(1)}, u32[]{:S(2)}) copy-start(bf16[640,768]{1,0:T(8,128)(2,1)S(1)} %all_gather.48) | copy-start | bytes 2949124
  73.2 44.2 %copy-start.16 = (bf16[768,192]{1,0:T(8,128)(2,1)}, bf16[768,192]{1,0:T(8,128)(2,1)S(1)}, u32[]{:S(2)}) copy-start(bf16[768,192]{1,0:T(8,128)(2,1)S(1)} %all_gather.52) | copy-start | bytes 884740
  102.1 15.3 %copy-start.14 = (bf16[768,192]{1,0:T(8,128)(2,1)}, bf16[768,192]{1,0:T(8,128)(2,1)S(1)}, u32[]{:S(2)}) copy-start(bf16[768,192]{1,0:T(8,128)(2,1)S(1)} %all_gather.51) | copy-start | bytes 884740
  103.2 14.3 %copy-start.8 = (bf16[640,192]{0,1:T(8,128)(2,1)}, bf16[640,192]{0,1:T(8,128)(2,1)S(1)}, u32[]{:S(2)}) copy-start(bf16[640,192]{0,1:T(8,128)(2,1)S(1)} %fusion.31) | copy-start | bytes 737284
  126.7 21.9 %copy-start.36 = (bf16[192,96]{1,0:T(8,128)(2,1)S(1)}, bf16[192,96]{1,0:T(8,128)(2,1)}, u32[]{:S(2)}) copy-start(bf16[192,96]{1,0:T(8,128)(2,1)} %param.29) | copy-start | bytes 110596
  126.7 22.0 %copy-start.35 = (bf16[96,192]{1,0:T(8,128)(2,1)S(1)}, bf16[96,192]{1,0:T(8,128)(2,1)}, u32[]{:S(2)}) copy-start(bf16[96,192]{1,0:T(8,128)(2,1)} %param.27) | copy-start | bytes 110596
  126.7 79.5 %copy-start.45 = (f32[192]{0:T(256)S(1)}, f32[192]{0:T(256)}, u32[]{:S(2)}) copy-start(f32[192]{0:T(256)} %param.28) | copy-start | bytes 2308
  177.6 29.1 %copy-start.12 = (bf16[768,192]{1,0:T(8,128)(2,1)}, bf16[768,192]{1,0:T(8,128)(2,1)S(1)}, u32[]{:S(2)}) copy-start(bf16[768,192]{1,0:T(8,128)(2,1)S(1)} %all_gather.49) | copy-start | bytes 884740
  220.8 94.2 %copy-start.10 = (bf16[2560,192]{0,1:T(8,128)(2,1)}, bf16[2560,192]{0,1:T(8,128)(2,1)S(1)}, u32[]{:S(2)}) copy-start(bf16[2560,192]{0,1:T(8,128)(2,1)S(1)} %all_gather.50) | copy-start | bytes 2949124
  264.1 19.0 %copy-start.2 = (f32[3,5,128,20,128]{4,1,3,2,0:T(8,128)S(1)}, f32[3,5,128,20,128]{4,1,3,2,0:T(8,128)}, u32[]{:S(2)}) copy-start(f32[3,5,128,20,128]{4,1,3,2,0:T(8,128)} %get-tuple-element.225) | copy-start | bytes 58982404
  323.6 39.0 %copy-start.25 = (bf16[160,768]{1,0:T(8,128)(2,1)S(1)}, bf16[160,768]{1,0:T(8,128)(2,1)}, u32[]{:S(2)}) copy-start(bf16[160,768]{1,0:T(8,128)(2,1)} %param.22) | copy-start | bytes 737284
  323.6 39.0 %copy-start.41 = (f32[768]{0:T(1024)S(1)}, f32[768]{0:T(1024)}, u32[]{:S(2)}) copy-start(f32[768]{0:T(1024)} %param.30) | copy-start | bytes 9220
  325.4 38.6 %copy-start.32 = (f32[768]{0:T(1024)S(1)}, f32[768]{0:T(1024)}, u32[]{:S(2)}) copy-start(f32[768]{0:T(1024)} %param.31) | copy-start | bytes 9220
  325.4 38.6 %copy-start.38 = (f32[768]{0:T(1024)S(1)}, f32[768]{0:T(1024)}, u32[]{:S(2)}) copy-start(f32[768]{0:T(1024)} %param.32) | copy-start | bytes 9220
  325.4 77.7 %all-gather.6.cloned.1.call-start = ((), (), s32[]{:S(2)}) async-start(), calls=%async_computation.15 | async-start | bytes 1327104 | tf_op jit(solution)/shard_map/all_gather | solution.py:225
  326.2 77.0 %copy-start.48 = (f32[768]{0:T(1024)S(1)}, f32[768]{0:T(1024)}, u32[]{:S(2)}) copy-start(f32[768]{0:T(1024)} %param.34) | copy-start | bytes 9220
  326.2 116.9 %all-gather.8.cloned.1.call-start = ((), (), s32[]{:S(2)}) async-start(), calls=%async_computation.16 | async-start | bytes 1327104 | tf_op jit(solution)/shard_map/all_gather | solution.py:227
  326.8 156.9 %reduce-scatter.28.cloned.1.call-start = ((), (), s32[]{:S(2)}) async-start(), calls=%async_computation.17 | async-start | bytes 2457600 | tf_op jit(solution)/shard_map/reduce_scatter | solution.py:44
  375.0 35.7 %copy-start.26 = (bf16[640,768]{1,0:T(8,128)(2,1)}, bf16[640,768]{1,0:T(8,128)(2,1)S(1)}, u32[]{:S(2)}) copy-start(bf16[640,768]{1,0:T(8,128)(2,1)S(1)} %all_gather.56) | copy-start | bytes 2949124
  446.9 36.7 %copy-start.42 = (f32[768]{0:T(1024)S(1)}, f32[768]{0:T(1024)}, u32[]{:S(2)}) copy-start(f32[768]{0:T(1024)} %param.36) | copy-start | bytes 9220
  446.9 38.4 %copy-start.19 = (bf16[160,768]{1,0:T(8,128)(2,1)S(1)}, bf16[160,768]{1,0:T(8,128)(2,1)}, u32[]{:S(2)}) copy-start(bf16[160,768]{1,0:T(8,128)(2,1)} %param.41) | copy-start | bytes 737284
  446.9 38.4 %copy-start.37 = (f32[768]{0:T(1024)S(1)}, f32[768]{0:T(1024)}, u32[]{:S(2)}) copy-start(f32[768]{0:T(1024)} %param.37) | copy-start | bytes 9220
  446.9 91.9 %reduce-scatter.30.cloned.1.call-start = ((), (), s32[]{:S(2)}) async-start(), calls=%async_computation.18 | async-start | bytes 2457600 | tf_op jit(solution)/shard_map/reduce_scatter | solution.py:44
  483.6 13.3 %copy-start.51 = (f32[640,768]{1,0:T(8,128)S(1)}, f32[640,768]{1,0:T(8,128)}, u32[]{:S(2)}) copy-start(f32[640,768]{1,0:T(8,128)} %get-tuple-element.226) | copy-start | bytes 5898244
  485.1 11.9 %copy-start.47 = (bf16[768,768]{0,1:T(8,128)(2,1)S(1)}, bf16[768,768]{0,1:T(8,128)(2,1)}, u32[]{:S(2)}) copy-start(bf16[768,768]{0,1:T(8,128)(2,1)} %all-gather.8.cloned.1.call-done) | copy-start | bytes 3538948
  485.1 11.8 %copy-start.50 = (f32[640,768]{1,0:T(8,128)S(1)}, f32[640,768]{1,0:T(8,128)}, u32[]{:S(2)}) copy-start(f32[640,768]{1,0:T(8,128)} %get-tuple-element.183) | copy-start | bytes 5898244
  497.0 2.5 copy-start.46
  501.7 37.1 %copy-start.43 = (f32[768]{0:T(1024)S(1)}, f32[768]{0:T(1024)}, u32[]{:S(2)}) copy-start(f32[768]{0:T(1024)} %param.38) | copy-start | bytes 9220
  501.7 108.2 %reduce-scatter.42.cloned.1.call-start = ((), (), s32[]{:S(2)}) async-start(), calls=%async_computation.24 | async-start | bytes 1638400
  541.3 12.3 %copy-start.11 = (bf16[2560,192]{0,1:T(8,128)(2,1)S(1)}, bf16[2560,192]{0,1:T(8,128)(2,1)}, u32[]{:S(2)}) copy-start(bf16[2560,192]{0,1:T(8,128)(2,1)} %copy-done.10) | copy-start | bytes 2949124
  580.9 51.7 %reduce-scatter.40.cloned.1.call-start = ((), (), s32[]{:S(2)}) async-start(), calls=%async_computation.23 | async-start | bytes 1638400
  581.0 13.7 %copy-start.9 = (bf16[640,192]{0,1:T(8,128)(2,1)S(1)}, bf16[640,192]{0,1:T(8,128)(2,1)}, u32[]{:S(2)}) copy-start(bf16[640,192]{0,1:T(8,128)(2,1)} %copy-done.8) | copy-start | bytes 737284
  594.6 3.8 copy-start.3
  599.9 89.3 %reduce-scatter.50.cloned.1.call-start = ((), (), s32[]{:S(2)}) async-start(), calls=%async_computation.28 | async-start | bytes 442368
  601.3 7.2 copy-start.5
  601.3 108.9 %reduce-scatter.44.cloned.1.call-start = ((), (), s32[]{:S(2)}) async-start(), calls=%async_computation.25 | async-start | bytes 442368
  609.8 139.3 %reduce-scatter.48.cloned.1.call-start = ((), (), s32[]{:S(2)}) async-start(), calls=%async_computation.27 | async-start | bytes 442368
  611.3 23.7 %copy-start.29 = (bf16[640,768]{1,0:T(8,128)(2,1)S(1)}, bf16[640,768]{1,0:T(8,128)(2,1)}, u32[]{:S(2)}) copy-start(bf16[640,768]{1,0:T(8,128)(2,1)} %copy-done.28) | copy-start | bytes 2949124
  612.3 175.3 %reduce-scatter.46.cloned.1.call-start = ((), (), s32[]{:S(2)}) async-start(), calls=%async_computation.26 | async-start | bytes 442368
  635.0 3.7 copy-start.27
  635.0 193.5 %reduce-scatter.36.cloned.1.call-start = ((), (), s32[]{:S(2)}) async-start(), calls=%async_computation.21 | async-start | bytes 1327104 | tf_op jit(solution)/shard_map/reduce_scatter | solution.py:411
  638.5 230.6 %reduce-scatter.34.cloned.1.call-start = ((), (), s32[]{:S(2)}) async-start(), calls=%async_computation.20 | async-start | bytes 1327104 | tf_op jit(solution)/shard_map/reduce_scatter | solution.py:405
  642.2 269.0 %reduce-scatter.38.cloned.1.call-start = ((), (), s32[]{:S(2)}) async-start(), calls=%async_computation.22 | async-start | bytes 1769472 | tf_op jit(solution)/shard_map/reduce_scatter | solution.py:414
  659.4 15.3 %copy-start.40 = (s32[20]{0:T(128)S(1)}, s32[20]{0:T(128)}, u32[]{:S(2)}) copy-start(s32[20]{0:T(128)} %copy-done.39) | copy-start | bytes 244
  687.0 102.4 %copy-start.15 = (bf16[768,192]{1,0:T(8,128)(2,1)S(1)}, bf16[768,192]{1,0:T(8,128)(2,1)}, u32[]{:S(2)}) copy-start(bf16[768,192]{1,0:T(8,128)(2,1)} %copy-done.14) | copy-start | bytes 884740
  689.0 222.2 %copy-start.17 = (bf16[768,192]{1,0:T(8,128)(2,1)S(1)}, bf16[768,192]{1,0:T(8,128)(2,1)}, u32[]{:S(2)}) copy-start(bf16[768,192]{1,0:T(8,128)(2,1)} %copy-done.16) | copy-start | bytes 884740
  689.0 222.2 %copy-start.23 = (bf16[640,192]{1,0:T(8,128)(2,1)S(1)}, bf16[640,192]{1,0:T(8,128)(2,1)}, u32[]{:S(2)}) copy-start(bf16[640,192]{1,0:T(8,128)(2,1)} %reduce-scatter.40.cloned.1.call-done) | copy-start | bytes 737284
  689.0 372.1 %all-reduce.7.cloned.1.call-start = ((), (), s32[]{:S(2)}) async-start(), calls=%async_computation.29 | async-start | bytes 393216 | tf_op jit(solution)/shard_map/psum | solution.py:419
  789.2 278.1 %all-reduce.9.cloned.1.call-start = ((), (), s32[]{:S(2)}) async-start(), calls=%async_computation.30 | async-start | bytes 983040 | tf_op jit(solution)/shard_map/psum | solution.py:422
  789.9 121.8 %copy-start.13 = (bf16[768,192]{1,0:T(8,128)(2,1)S(1)}, bf16[768,192]{1,0:T(8,128)(2,1)}, u32[]{:S(2)}) copy-start(bf16[768,192]{1,0:T(8,128)(2,1)} %copy-done.12) | copy-start | bytes 884740
  789.9 121.8 %copy-start.18 = (bf16[640,192]{1,0:T(8,128)(2,1)S(1)}, bf16[640,192]{1,0:T(8,128)(2,1)}, u32[]{:S(2)}) copy-start(bf16[640,192]{1,0:T(8,128)(2,1)} %reduce-scatter.42.cloned.1.call-done) | copy-start | bytes 737284
  911.2 161.2 %reduce-scatter.32.cloned.1.call-start = ((), (), s32[]{:S(2)}) async-start(), calls=%async_computation.19 | async-start | bytes 2457600 | tf_op jit(solution)/shard_map/reduce_scatter | solution.py:44
  913.5 157.0 %copy-start.21 = (f32[3,64,512]{2,1,0:T(8,128)S(1)}, f32[3,64,512]{2,1,0:T(8,128)}, u32[]{:S(2)}) copy-start(f32[3,64,512]{2,1,0:T(8,128)} %param.39) | copy-start | bytes 1179652
  913.5 157.0 %copy-start.22 = (f32[3,64,512]{2,1,0:T(8,128)S(1)}, f32[3,64,512]{2,1,0:T(8,128)}, u32[]{:S(2)}) copy-start(f32[3,64,512]{2,1,0:T(8,128)} %param.40) | copy-start | bytes 1179652
  913.5 158.8 %copy-start.20 = (f32[160,768]{1,0:T(8,128)S(1)}, f32[160,768]{1,0:T(8,128)}, u32[]{:S(2)}) copy-start(f32[160,768]{1,0:T(8,128)} %get-tuple-element.173) | copy-start | bytes 1474564
  1064.1 10.1 copy-start.1
  (6 other events, 8.4 us)
Sparse Core Ops, SparseCore 0:
  10.3 42.3 all-gather.3
  325.6 36.9 reduce-scatter.25
  364.3 38.7 all-gather.5
  404.7 38.3 all-gather.7
  447.1 36.5 reduce-scatter.27
  501.9 36.9 reduce-scatter.29
  581.1 24.8 reduce-scatter.41
  608.5 24.0 reduce-scatter.39
  635.1 36.4 reduce-scatter.49
  673.8 36.3 reduce-scatter.43
  712.7 36.3 reduce-scatter.47
  751.3 36.2 reduce-scatter.45
  790.1 38.2 reduce-scatter.35
  830.8 38.1 reduce-scatter.33
  871.4 39.6 reduce-scatter.37
  914.2 41.1 all-reduce.6
  957.8 43.4 all-reduce.8
  1004.0 37.3 reduce-scatter.31
where the time goes:
time: 1090 us; the launch traced here: 1080 us
  waiting for transfers between devices  407 us (37%)
  blocking collectives  339 us (31%)
  matrix products  152 us (14%)
  local copies, waits for them, and re-layouts  121 us (11%)
  other arithmetic  46.3 us (4%)
  between operations  15.4 us (1%)
    unnamed x24, waiting for transfers between devices  116 us
    reduce_scatter x4, waiting for transfers between devices, sum_rows(): return lax.psum_scatter(values, 'tp', scatter_dimension=0, tiled=True)  109 us
    psum x1, blocking collectives, shards(): lax.psum((query_bias_grad, value_bias_grad, inner_bias_grad), ('shard', '...  82.2 us
    psum x1, blocking collectives, shards(): lax.psum((output_bias_grad, outer_bias_grad, first_gain_grad, first_shift...  65 us
    all_gather x4, blocking collectives, gather_rows(): return lax.all_gather(values, 'tp', axis=0, tiled=True)  48 us
    reduce_scatter x1, waiting for transfers between devices, shards(): lax.psum_scatter(table_grad.astype(jnp.bfloat16), 'shard', scatter_dimens...  42.1 us
    reduce_scatter x1, waiting for transfers between devices, shards(): lax.psum_scatter(inner_weight_grad.astype(jnp.bfloat16), 'shard', scatter...  40.6 us
    reduce_scatter x1, waiting for transfers between devices, shards(): lax.psum_scatter(outer_weight_grad.astype(jnp.bfloat16), 'shard', scatter...  38.5 us
  transfers between devices with their start and end apart: 18, of which 12 were waited for; matrix products, arithmetic and copies ran while one was open for 15% of the time, Pallas kernels for 0%

commit v1 on v0

--- a/solution.py
+++ b/solution.py
@@ -1,13 +1,398 @@
 import jax
 import jax.numpy as jnp
 from jax import lax
+from jax.experimental import pallas as pl
+from jax.experimental.pallas import tpu as pltpu
 from jax.sharding import PartitionSpec as P
 
-HEADS = 12
+MESH = pl.DeviceIdType.MESH
+BF = jnp.bfloat16
+F32 = jnp.float32
+HEADS_DEV = 3
 HEAD_DIM = 64
+WIDE = 128
+SEG = 128
+SEGS = 20
+PATH = 10
+KEYS = PATH * SEG
+D = 768
+QK = 192
+QKW = 384
+ROWS = 160
+CTX_ROWS = 640
+TREE = 2560
 DEPTHS = 512
-SEG_LEN = 128
-TREE_SEGS = 20
+MIB = 2**20
+VM = pl.BlockSpec(memory_space=pltpu.VMEM)
+SM = pl.BlockSpec(memory_space=pltpu.SMEM)
+
+
+def place():
+    shard = lax.axis_index("shard")
+    tp = lax.axis_index("tp")
+    return {
+        "x": lax.axis_index("ctx"),
+        "yl": lax.div(shard, 4),
+        "z": lax.rem(shard, 4),
+        "yh": lax.div(tp, 2),
+        "core": lax.rem(tp, 2),
+    }
+
+
+def ident(at, **moved):
+    to = {**at, **moved}
+    return {"shard": to["yl"] * 4 + to["z"], "ctx": to["x"], "tp": to["yh"] * 2 + to["core"]}
+
+
+def around(value, step):
+    return lax.rem(value + step, 4)
+
+
+def greet(devices):
+    barrier = pltpu.get_barrier_semaphore()
+    for device in devices:
+        pl.semaphore_signal(barrier, inc=1, device_id=device, device_id_type=MESH)
+    pl.semaphore_wait(barrier, len(devices))
+
+
+class Mail:
+    def __init__(self, send, recv):
+        self.send, self.recv, self.used, self.sent = send, recv, 0, []
+
+    def post(self, src, dst, device):
+        copy = pltpu.make_async_remote_copy(
+            src_ref=src,
+            dst_ref=dst,
+            send_sem=self.send.at[self.used],
+            recv_sem=self.recv.at[self.used],
+            device_id=device,
+            device_id_type=MESH,
+        )
+        self.used += 1
+        copy.start()
+        self.sent.append(copy)
+        return copy
+
+    def close(self):
+        for copy in self.sent:
+            copy.wait_send()
+
+
+def nn(a, b):
+    return jnp.dot(a, b, preferred_element_type=F32)
+
+
+def nt(a, b):
+    return lax.dot_general(a, b, (((1,), (1,)), ((), ())), preferred_element_type=F32)
+
+
+def spread(kind=BF):
+    rows = lax.broadcasted_iota(jnp.int32, (QK, QKW), 0)
+    cols = lax.broadcasted_iota(jnp.int32, (QK, QKW), 1)
+    head, lane = cols // WIDE, cols % WIDE
+    return ((head * HEAD_DIM + lane == rows) & (lane < HEAD_DIM)).astype(kind)
+
+
+def project_kernel(
+    tok,
+    wq,
+    wk,
+    wv,
+    qb,
+    vb,
+    logits,
+    noise,
+    q_out,
+    k_out,
+    v_out,
+    rows_out,
+    tab,
+    xs,
+    ws,
+    wide,
+    send,
+    recv,
+):
+    at = place()
+    x, yl, z, yh, core = at["x"], at["yl"], at["z"], at["yh"], at["core"]
+    shard, tp = yl * 4 + z, yh * 2 + core
+    sib = ident(at, core=1 - core)
+    far = ident(at, yh=1 - yh)
+    low = ident(at, yl=1 - yl)
+    zs = [ident(at, z=around(z, k)) for k in (1, 2, 3)]
+    xp = [ident(at, x=around(x, k)) for k in (1, 2, 3)]
+    xs[x, tp] = tok[...]
+    for j, w in enumerate((wq, wk, wv)):
+        ws[shard, j] = w[...]
+    masks = logits[...] + noise[...]
+    tab[:, shard] = jax.nn.log_sigmoid(masks).astype(BF)
+    greet([sib, far, low, *zs, *xp])
+    mail = Mail(send, recv)
+
+    def block(kx, other):
+        return xs.at[around(x, 4 - kx), (1 - yh if other else yh) * 2 + core]
+
+    def pass_on(src, device):
+        return mail.post(src, src, device)
+
+    first_far = pass_on(block(0, False), far)
+    own_low = [pass_on(ws.at[shard], low), pass_on(tab.at[0, shard], low)]
+    own_x = [pass_on(block(0, False), d) for d in xp]
+    own_z = [pass_on(ws.at[shard], d) for d in zs]
+    own_z0 = [pass_on(tab.at[0, shard], d) for d in zs]
+    own_z1 = [pass_on(tab.at[pl.ds(1, 2), shard], d) for d in zs]
+    to_low = [pass_on(tab.at[pl.ds(1, 2), shard], low)]
+    to_sib = [pass_on(block(0, False), sib)]
+    first_far.wait_recv()
+    far_x = [pass_on(block(0, True), d) for d in xp]
+    to_sib.append(pass_on(block(0, True), sib))
+    for copy in own_low:
+        copy.wait_recv()
+    mate = (1 - yl) * 4 + z
+    low_z = [pass_on(ws.at[mate], d) for d in zs]
+    low_z0 = [pass_on(tab.at[0, mate], d) for d in zs]
+    for k in (1, 3, 2):
+        own_x[k - 1].wait_recv()
+        to_sib.append(pass_on(block(k, False), sib))
+    for k in (1, 3, 2):
+        own_z1[k - 1].wait_recv()
+        to_low.append(pass_on(tab.at[pl.ds(1, 2), yl * 4 + around(z, 4 - k)], low))
+    for k in (1, 3, 2):
+        far_x[k - 1].wait_recv()
+        to_sib.append(pass_on(block(k, True), sib))
+    for copy in own_z + own_z0 + low_z + to_sib:
+        copy.wait_recv()
+
+    hots = spread()
+    hots32 = spread(F32)
+    for j in range(3):
+        whole = ws[:, j].reshape(D, QK)
+        wide[:, j * QKW : (j + 1) * QKW] = nn(whole, hots).astype(BF)
+    q_add = jnp.dot(qb[...], hots32, precision=lax.Precision.HIGHEST)
+    v_add = jnp.dot(vb[...], hots32, precision=lax.Precision.HIGHEST)
+
+    @pl.loop(0, 16)
+    def _(i):
+        rows = xs[lax.div(i, 4), lax.rem(i, 4)]
+        both = nn(rows, wide[:, QKW:])
+        k_out[pl.ds(i * ROWS, ROWS), :] = both[:, :QKW].astype(BF)
+        v_out[pl.ds(i * ROWS, ROWS), :] = (both[:, QKW:] + v_add).astype(BF)
+
+    @pl.loop(0, 4)
+    def _(i):
+        rows = xs[x, i]
+        rows_out[pl.ds(i * ROWS, ROWS), :] = rows
+        q_out[pl.ds(i * ROWS, ROWS), :] = (nn(rows, wide[:, :QKW]) + q_add).astype(BF)
+
+    for copy in low_z0 + to_low:
+        copy.wait_recv()
+    mail.close()
+
+
+def project(tokens, wq, wk, wv, qb, vb, logits, noise):
+    shape = jax.ShapeDtypeStruct
+    posts = 2 + 1 + 3 + 9 + 1 + 8 + 3 + 6 + 3
+    return pl.pallas_call(
+        project_kernel,
+        out_shape=(
+            shape((CTX_ROWS, QKW), BF),
+            shape((TREE, QKW), BF),
+            shape((TREE, QKW), BF),
+            shape((CTX_ROWS, D), BF),
+            shape((HEADS_DEV, 8, 64, DEPTHS), BF),
+        ),
+        in_specs=[VM] * 8,
+        out_specs=[VM] * 5,
+        scratch_shapes=[
+            pltpu.VMEM((4, 4, ROWS, D), BF),
+            pltpu.VMEM((8, 3, 96, QK), BF),
+            pltpu.VMEM((D, 3 * QKW), BF),
+            pltpu.SemaphoreType.DMA((posts,)),
+            pltpu.SemaphoreType.DMA((posts,)),
+        ],
+        compiler_params=pltpu.CompilerParams(
+            collective_id=1, has_side_effects=True, vmem_limit_bytes=56 * MIB
+        ),
+        name="project",
+    )(tokens, wq, wk, wv, qb.reshape(1, QK), vb.reshape(1, QK), logits, noise)
+
+
+def climb(parents, seg, trail):
+    trail[0] = seg
+    depth = jnp.int32(0)
+    here = seg
+    for i in range(1, PATH):
+        up = parents[0, here]
+        found = up >= 0
+        here = jnp.where(found, up, here)
+        trail[i] = here
+        depth = depth + found.astype(jnp.int32)
+    return depth
+
+
+def on_path(trail, depth, j):
+    return trail[jnp.maximum(depth - j, 0)]
+
+
+def attend_kernel(parents, q, k, v, tab, o_out, p_out, trail, kp, vp):
+    a = pl.program_id(0)
+    seg = lax.axis_index("ctx") * 5 + a
+    depth = climb(parents, seg, trail)
+    for j in range(PATH):
+        rows = pl.ds(pl.multiple_of(on_path(trail, depth, j) * SEG, SEG), SEG)
+        kp[pl.ds(j * SEG, SEG), :] = k[rows, :]
+        vp[pl.ds(j * SEG, SEG), :] = v[rows, :]
+    tile = pl.ds(pl.multiple_of(lax.rem(depth, 4) * SEG, SEG), SEG)
+    outs = []
+    for h in range(HEADS_DEV):
+        head = slice(h * WIDE, (h + 1) * WIDE)
+        mine = q[:, head] * jnp.asarray(HEAD_DIM**-0.5, BF)
+        bias = tab[h, tile, :].astype(F32)
+        scores = nt(mine, kp[:, head])
+        parts = []
+        for j in range(PATH):
+            cols = slice((j % 4) * SEG, (j % 4 + 1) * SEG)
+            part = scores[:, j * SEG : (j + 1) * SEG] + bias[:, cols]
+            parts.append(jnp.where(j <= depth, part, -1e30))
+        scores = jnp.concatenate(parts, axis=1)
+        peak = jnp.max(scores, axis=1, keepdims=True)
+        raised = jnp.exp(scores - peak)
+        total = jnp.sum(raised, axis=1, keepdims=True)
+        soft = (raised * (1.0 / total)).astype(BF)
+        p_out[0, h] = soft
+        outs.append(nn(soft, vp[:, head]).astype(BF))
+    o_out[...] = nt(jnp.concatenate(outs, axis=1), spread()).astype(BF)
+
+
+def whole(shape):
+    return pl.BlockSpec(shape, lambda a: (0,) * len(shape))
+
+
+def attend(parents, q, k, v, tab):
+    shape = jax.ShapeDtypeStruct
+    return pl.pallas_call(
+        attend_kernel,
+        grid=(5,),
+        out_shape=(
+            shape((CTX_ROWS, QK), BF),
+            shape((5, HEADS_DEV, SEG, KEYS), BF),
+        ),
+        in_specs=[
+            SM,
+            pl.BlockSpec((SEG, QKW), lambda a: (a, 0)),
+            whole((TREE, QKW)),
+            whole((TREE, QKW)),
+            whole((HEADS_DEV, DEPTHS, DEPTHS)),
+        ],
+        out_specs=(
+            pl.BlockSpec((SEG, QK), lambda a: (a, 0)),
+            pl.BlockSpec((1, HEADS_DEV, SEG, KEYS), lambda a: (a, 0, 0, 0)),
+        ),
+        scratch_shapes=[
+            pltpu.SMEM((PATH,), jnp.int32),
+            pltpu.VMEM((KEYS, QKW), BF),
+            pltpu.VMEM((KEYS, QKW), BF),
+        ],
+        compiler_params=pltpu.CompilerParams(vmem_limit_bytes=56 * MIB),
+        cost_estimate=pl.CostEstimate(
+            flops=2 * 2 * 15 * SEG * KEYS * WIDE, bytes_accessed=12 * MIB, transcendentals=15 * SEG * KEYS
+        ),
+        name="attend",
+    )(parents, q, k, v, tab)
+
+
+def attend_back_kernel(
+    parents, q, k, v, o, g, p, dq_out, dk_out, dv_out, tab_out, trail, kp, vp, dk, dv, dtab
+):
+    a = pl.program_id(0)
+    seg = lax.axis_index("ctx") * 5 + a
+
+    @pl.when(a == 0)
+    def _():
+        dk[...] = jnp.zeros_like(dk)
+        dv[...] = jnp.zeros_like(dv)
+        dtab[...] = jnp.zeros_like(dtab)
+
+    depth = climb(parents, seg, trail)
+    starts = [pl.multiple_of(on_path(trail, depth, j) * SEG, SEG) for j in range(PATH)]
+    for j in range(PATH):
+        kp[pl.ds(j * SEG, SEG), :] = k[pl.ds(starts[j], SEG), :]
+        vp[pl.ds(j * SEG, SEG), :] = v[pl.ds(starts[j], SEG), :]
+    tile = pl.ds(pl.multiple_of(lax.rem(depth, 4) * SEG, SEG), SEG)
+    hots = spread()
+    g_wide = nn(g[...], hots).astype(BF)
+    o_wide = nn(o[...], hots)
+    scale = HEAD_DIM**-0.5
+    outs = []
+    for h in range(HEADS_DEV):
+        head = slice(h * WIDE, (h + 1) * WIDE)
+        mine, grad = q[:, head], g_wide[:, head]
+        soft = p[0, h]
+        inner = jnp.sum(grad.astype(F32) * o_wide[:, head], axis=1, keepdims=True)
+        ds = soft.astype(F32) * (nt(grad, vp[:, head]) - inner)
+        low = ds.astype(BF)
+        outs.append((nn(low, kp[:, head]) * scale).astype(BF))
+        mine_t = (mine.astype(F32).T[:HEAD_DIM] * scale).astype(BF)
+        grad_t = grad.astype(F32).T[:HEAD_DIM].astype(BF)
+        dk_part = nn(mine_t, low)
+        dv_part = nn(grad_t, soft)
+        for j in range(PATH):
+            cols = slice(j * SEG, (j + 1) * SEG)
+            dk[h, :, pl.ds(starts[j], SEG)] += dk_part[:, cols]
+            dv[h, :, pl.ds(starts[j], SEG)] += dv_part[:, cols]
+        down = low.astype(F32)
+        dtab[h, tile, 0:256] += down[:, 0:256] + down[:, 512:768] + down[:, 1024:1280]
+        dtab[h, tile, 256:512] += down[:, 256:512] + down[:, 768:1024]
+    dq_out[...] = nt(jnp.concatenate(outs, axis=1), hots).astype(BF)
+
+    @pl.when(a == 4)
+    def _():
+        for h in range(HEADS_DEV):
+            dk_out[pl.ds(h * HEAD_DIM, HEAD_DIM), :] = dk[h].astype(BF)
+            dv_out[pl.ds(h * HEAD_DIM, HEAD_DIM), :] = dv[h].astype(BF)
+            tab_out[h] = dtab[h].astype(BF)
+
+
+def attend_back(parents, q, k, v, o, g, p):
+    shape = jax.ShapeDtypeStruct
+    return pl.pallas_call(
+        attend_back_kernel,
+        grid=(5,),
+        out_shape=(
+            shape((CTX_ROWS, QK), BF),
+            shape((QK, TREE), BF),
+            shape((QK, TREE), BF),
+            shape((HEADS_DEV, DEPTHS, DEPTHS), BF),
+        ),
+        in_specs=[
+            SM,
+            pl.BlockSpec((SEG, QKW), lambda a: (a, 0)),
+            whole((TREE, QKW)),
+            whole((TREE, QKW)),
+            pl.BlockSpec((SEG, QK), lambda a: (a, 0)),
+            pl.BlockSpec((SEG, QK), lambda a: (a, 0)),
+            pl.BlockSpec((1, HEADS_DEV, SEG, KEYS), lambda a: (a, 0, 0, 0)),
+        ],
+        out_specs=(
+            pl.BlockSpec((SEG, QK), lambda a: (a, 0)),
+            whole((QK, TREE)),
+            whole((QK, TREE)),
+            whole((HEADS_DEV, DEPTHS, DEPTHS)),
+        ),
+        scratch_shapes=[
+            pltpu.SMEM((PATH,), jnp.int32),
+            pltpu.VMEM((KEYS, QKW), BF),
+            pltpu.VMEM((KEYS, QKW), BF),
+            pltpu.VMEM((HEADS_DEV, HEAD_DIM, TREE), F32),
+            pltpu.VMEM((HEADS_DEV, HEAD_DIM, TREE), F32),
+            pltpu.VMEM((HEADS_DEV, DEPTHS, DEPTHS), F32),
+        ],
+        compiler_params=pltpu.CompilerParams(vmem_limit_bytes=56 * MIB),
+        cost_estimate=pl.CostEstimate(
+            flops=5 * 2 * 15 * SEG * KEYS * WIDE, bytes_accessed=20 * MIB, transcendentals=0
+        ),
+        name="attend_back",
+    )(parents, q, k, v, o, g, p)
 
 
 def layer_norm(values, gain_vector, shift_vector):
@@ -212,82 +597,14 @@
     mask_noise,
     cotangent,
 ):
-    tp_count = lax.axis_size("tp")
-    ctx_count = lax.axis_size("ctx")
-    ctx_index = lax.axis_index("ctx")
-    heads_local = HEADS // tp_count
-    tile_count = DEPTHS // SEG_LEN
     relaxed_low = jax.nn.log_sigmoid(mask_logits + mask_noise).astype(jnp.bfloat16)
-    weight_set = (
-        lax.all_gather(query_weight, "shard", axis=0, tiled=True),
-        lax.all_gather(key_weight, "shard", axis=0, tiled=True),
-        lax.all_gather(value_weight, "shard", axis=0, tiled=True),
+    queries, keys_all, values_all, full_rows, table = project(tokens, query_weight, key_weight, value_weight, query_bias, value_bias, mask_logits, mask_noise)
+    table = table.reshape(HEADS_DEV, DEPTHS, DEPTHS)
+    attended, soft = attend(parents, queries, keys_all, values_all, table)
+    weight_set = (None,None,None,
         lax.all_gather(inner_weight, "shard", axis=0, tiled=True),
         lax.all_gather(output_weight, "shard", axis=1, tiled=True),
-        lax.all_gather(outer_weight, "shard", axis=1, tiled=True),
-        lax.all_gather(relaxed_low, "shard", axis=1, tiled=True),
-    )
-    reachable, segment_tile = tree_tables(parents[0])
-    full_rows = gather_rows(tokens)
-    row_count = full_rows.shape[0]
-    block_rows = SEG_LEN * TREE_SEGS // ctx_count
-    trees = row_count // block_rows
-    block_segs = block_rows // SEG_LEN
-    local_segs = row_count // SEG_LEN
-    tree_ids = jnp.arange(trees, dtype=jnp.int32)
-    inner_ids = jnp.arange(block_segs, dtype=jnp.int32)
-    ctx_ids = jnp.arange(ctx_count, dtype=jnp.int32)
-    query_segs = ctx_index * local_segs + tree_ids[:, None] * block_segs + inner_ids[None, :]
-    key_segs = (
-        ctx_ids[None, :, None] * local_segs
-        + tree_ids[:, None, None] * block_segs
-        + inner_ids[None, None, :]
-    ).reshape(trees, ctx_count * block_segs)
-    reach_blocks = reachable[query_segs[:, :, None], key_segs[:, None, :]]
-    tile_ids = jnp.arange(tile_count, dtype=jnp.int32)
-    query_hots = (segment_tile[query_segs][..., None] == tile_ids).astype(jnp.bfloat16)
-    key_hots = (segment_tile[key_segs][..., None] == tile_ids).astype(jnp.bfloat16)
-
-    def by_tree(values):
-        width = values.shape[1]
-        return (
-            values.reshape(ctx_count, trees, block_rows, width)
-            .transpose(1, 0, 2, 3)
-            .reshape(trees, ctx_count * block_rows, width)
-        )
-
-    def from_tree(values):
-        width = values.shape[2]
-        return (
-            values.reshape(trees, ctx_count, block_rows, width)
-            .transpose(1, 0, 2, 3)
-            .reshape(ctx_count * row_count, width)
-        )
-
-    queries = (
-        jnp.dot(full_rows, weight_set[0], preferred_element_type=jnp.float32) + query_bias
-    ).astype(jnp.bfloat16)
-    keys_local = jnp.dot(full_rows, weight_set[1], preferred_element_type=jnp.float32).astype(
-        jnp.bfloat16
-    )
-    values_local = (
-        jnp.dot(full_rows, weight_set[2], preferred_element_type=jnp.float32) + value_bias
-    ).astype(jnp.bfloat16)
-    keys_all, values_all = (
-        lax.all_gather(keys_local, "ctx", axis=0, tiled=True),
-        lax.all_gather(values_local, "ctx", axis=0, tiled=True),
-    )
-    tiles = weight_set[6].reshape(heads_local, tile_count, SEG_LEN, tile_count, SEG_LEN)
-    attended, log_totals = attend_forward(
-        queries,
-        by_tree(keys_all),
-        by_tree(values_all),
-        tiles,
-        reach_blocks,
-        query_hots,
-        key_hots,
-        block_rows,
-    )
+        lax.all_gather(outer_weight, "shard", axis=1, tiled=True))
     attn_sum = (
         sum_rows(jnp.dot(attended, weight_set[4], preferred_element_type=jnp.float32)) + output_bias
     )
@@ -312,10 +629,6 @@
         lax.all_gather(outer_weight, "shard", axis=1, tiled=True),
         lax.all_gather(relaxed_low, "shard", axis=1, tiled=True),
     )
-    keys_back, values_back = (
-        lax.all_gather(keys_local, "ctx", axis=0, tiled=True),
-        lax.all_gather(values_local, "ctx", axis=0, tiled=True),
-    )
     second_grad, second_gain_grad, second_shift_grad = second_back(cotangent.astype(jnp.float32))
     outer_low = second_grad.astype(jnp.bfloat16)
     outer_bias_grad = jnp.sum(outer_low.astype(jnp.float32), axis=0)
@@ -347,30 +660,9 @@
     mixed_grad = jnp.einsum(
         "rd,hd->rh", attn_rows, weight_back[4], preferred_element_type=jnp.float32
     ).astype(jnp.bfloat16)
-    tiles_back = weight_back[6].reshape(heads_local, tile_count, SEG_LEN, tile_count, SEG_LEN)
-    query_grad, key_tree_grad, value_tree_grad, table_grad = attend_backward(
-        queries,
-        by_tree(keys_back),
-        by_tree(values_back),
-        tiles_back,
-        reach_blocks,
-        query_hots,
-        key_hots,
-        block_rows,
-        log_totals,
-        mixed_grad,
-    )
-    key_part, value_part = (
-        lax.psum_scatter(
-            from_tree(key_tree_grad).astype(jnp.bfloat16), "ctx", scatter_dimension=0, tiled=True
-        ).astype(jnp.float32),
-        lax.psum_scatter(
-            from_tree(value_tree_grad).astype(jnp.bfloat16), "ctx", scatter_dimension=0, tiled=True
-        ).astype(jnp.float32),
-    )
-    query_low = query_grad.astype(jnp.bfloat16)
-    key_low = key_part.astype(jnp.bfloat16)
-    value_low = value_part.astype(jnp.bfloat16)
+    query_low, key_t, value_t, table_grad = attend_back(parents, queries, keys_all, values_all, attended, mixed_grad, soft)
+    key_low = lax.psum_scatter(key_t.T, "ctx", scatter_dimension=0, tiled=True)
+    value_low = lax.psum_scatter(value_t.T, "ctx", scatter_dimension=0, tiled=True)
     query_bias_grad = jnp.sum(query_low.astype(jnp.float32), axis=0)
     value_bias_grad = jnp.sum(value_low.astype(jnp.float32), axis=0)
     query_weight_grad = jnp.einsum(

time: 1090 us -> 818 us (0.75)
  the two profiles are of different devices: /device:TPU:8 before, /device:TPU:1 now
where the time goes in v1:
time: 818 us; the launch traced here: 803 us
  waiting for transfers between devices  376 us (46%)
  blocking collectives  271 us (33%)
  Pallas kernels  73 us (9%)
  matrix products  36.3 us (4%)
  other arithmetic  19.5 us (2%)
  between operations  15.9 us (2%)
  local copies, waits for them, and re-layouts  10.4 us (1%)
    reduce_scatter x4, waiting for transfers between devices, sum_rows(): return lax.psum_scatter(values, 'tp', scatter_dimension=0, tiled=True)  114 us
    psum x1, blocking collectives, shards(): lax.psum((output_bias_grad, outer_bias_grad, first_gain_grad, first_shift...  71.1 us
    psum x1, blocking collectives, shards(): lax.psum((query_bias_grad, value_bias_grad, inner_bias_grad), ('shard', '...  67 us
    pallas_call x1, Pallas kernels, project(): pl.pallas_call(project_kernel, out_shape=(shape((CTX_ROWS, QKW), BF), sha...  46.4 us
    unnamed x20, waiting for transfers between devices  41.7 us
    reduce_scatter x1, waiting for transfers between devices, shards(): lax.psum_scatter(table_grad.astype(jnp.bfloat16), 'shard', scatter_dimens...  41.6 us
    reduce_scatter x1, waiting for transfers between devices, shards(): lax.psum_scatter(outer_weight_grad.astype(jnp.bfloat16), 'shard', scatter...  40.8 us
    reduce_scatter x1, waiting for transfers between devices, shards(): lax.psum_scatter(inner_weight_grad.astype(jnp.bfloat16), 'shard', scatter...  39.1 us
  transfers between devices with their start and end apart: 17, of which 11 were waited for; matrix products, arithmetic and copies ran while one was open for 5% of the time, Pallas kernels for 0%

profile of v1, /device:TPU:1, one launch (start us, length us, event | category | flops | bytes accessed | tf_op | source)
XLA Modules:
  0.0 803.2 jit_solution(11276650562914937863)
XLA Ops:
  8.1 0.9 copy.41
  9.0 24.9 %all_gather.30 = bf16[192,768]{0,1:T(8,128)(2,1)S(1)} all-gather(bf16[192,96]{0,1:T(8,128)(2,1)S(1)} %copy.41), channel_id=1, replica_groups=mesh['shard'=8,'ctx'=4,'tp'=4] {'shard'}, dimensions={1}, use_global_device_ids=true | all-gather | bytes 331776 | tf_op jit(solution)/shard_map/all_gather | solution.py:606
  33.9 46.4 %project.1 = (bf16[640,384]{1,0:T(8,128)(2,1)}, bf16[2560,384]{1,0:T(8,128)(2,1)}, bf16[2560,384]{1,0:T(8,128)(2,1)}, bf16[640,768]{1,0:T(8,128)(2,1)}, bf16[3,8,64,512]{3,2,1,0:T(8,128)(2,1)}) custom-call(bf16[160,768]{1,0:T(8,128)(2,1)} %tok.1, bf16[96,192]{1,0:T(8,128)(2,1)} %wq.1, bf16[96,192]{1,0:T(8,128)(2,1)} %wk.1, bf16[96,192]{1,0:T(8,128)(2,1)} %wv.1, ...), custom_call_target="tpu_custom_call" | custom-call | tf_op jit(solution)/shard_map/project/pallas_call | solution.py:195
  80.3 13.3 %attend.1 = (bf16[640,192]{1,0:T(8,128)(2,1)}, bf16[5,3,128,1280]{3,2,1,0:T(8,128)(2,1)}) custom-call(s32[1,20]{1,0:T(1,128)} %parents.3, bf16[640,384]{1,0:T(8,128)(2,1)} %get-tuple-element.29.q, bf16[2560,384]{1,0:T(8,128)(2,1)} %get-tuple-element.30.k, bf16[2560,384]{1,0:T(8,128)(2,1)} %get-tuple-element.31.v, bf16[3,512,512]{2,1,0:T(8,128)(2,1)} %bitcast.40), custom_call_target="tpu_custom_call" | custom-call | flops 1258291200 | bytes 12582912 | tf_op jit(solution)/shard_map/attend/pallas_call | solution.py:273
  93.6 2.8 fusion.23
  96.5 0.5 all-gather.3.cloned.1.call-update
  97.1 0.5 all-gather.5.cloned.1.call-update
  97.7 36.1 %reduce-scatter.20.cloned.1.call-done = f32[160,768]{1,0:T(8,128)} async-done(((f32[640,768]{1,0:T(8,128)}), f32[160,768]{1,0:T(8,128)}) %reduce-scatter.20.cloned.1.call-update) | async-done | bytes 491536 | tf_op jit(solution)/shard_map/reduce_scatter | solution.py:429
  133.8 1.2 fusion.22
  135.0 0.2 multiply_reduce_fusion.3
  135.4 13.0 %all_gather.31 = bf16[640,768]{1,0:T(8,128)(2,1)S(1)} all-gather(bf16[160,768]{1,0:T(8,128)(2,1)S(1)} %fusion.13), channel_id=1, replica_groups=mesh['shard'=8,'ctx'=4,'tp'=4] {'tp'}, dimensions={0}, use_global_device_ids=true | all-gather | bytes 1228800 | tf_op jit(solution)/shard_map/all_gather | solution.py:425
  148.4 7.5 multiply_convert_fusion
  156.0 27.1 %all-gather.5.cloned.1.call-done = bf16[768,768]{0,1:T(8,128)(2,1)} async-done(((bf16[768,96]{0,1:T(8,128)(2,1)}), bf16[768,768]{0,1:T(8,128)(2,1)}) %all-gather.5.cloned.1.call-update) | async-done | bytes 1179664 | tf_op jit(solution)/shard_map/all_gather | solution.py:607
  183.1 3.8 fusion.24
  187.0 41.9 %reduce-scatter.22.cloned.1.call-done = f32[160,768]{1,0:T(8,128)} async-done(((f32[640,768]{1,0:T(8,128)}), f32[160,768]{1,0:T(8,128)}) %reduce-scatter.22.cloned.1.call-update) | async-done | bytes 491536 | tf_op jit(solution)/shard_map/reduce_scatter | solution.py:429
  228.9 1.4 fusion.20
  230.6 0.3 fusion.12
  231.0 0.2 multiply_reduce_fusion.6
  231.4 11.3 %all_gather.34 = bf16[640,768]{1,0:T(8,128)(2,1)S(1)} all-gather(bf16[160,768]{1,0:T(8,128)(2,1)S(1)} %get-tuple-element.65), channel_id=1, replica_groups=mesh['shard'=8,'ctx'=4,'tp'=4] {'tp'}, dimensions={0}, use_global_device_ids=true | all-gather | bytes 1228800 | tf_op jit(solution)/shard_map/all_gather | solution.py:425
  242.7 1.5 convert_reduce_fusion
  244.2 0.9 copy-done.25
  245.2 2.3 fusion.25
  247.5 0.2 reduce-scatter.40.cloned.1.call-start
  247.7 36.4 %reduce-scatter.24.cloned.1.call-done = f32[160,768]{1,0:T(8,128)} async-done(((f32[640,768]{1,0:T(8,128)}), f32[160,768]{1,0:T(8,128)}) %reduce-scatter.24.cloned.1.call-update) | async-done | bytes 491536 | tf_op jit(solution)/shard_map/reduce_scatter | solution.py:429
  284.1 2.1 multiply_reduce_fusion
  286.3 0.2 multiply_reduce_fusion.4
  286.7 11.3 %all_gather.35 = bf16[640,768]{1,0:T(8,128)(2,1)S(1)} all-gather(bf16[160,768]{1,0:T(8,128)(2,1)S(1)} %get-tuple-element.67), channel_id=1, replica_groups=mesh['shard'=8,'ctx'=4,'tp'=4] {'tp'}, dimensions={0}, use_global_device_ids=true | all-gather | bytes 1228800 | tf_op jit(solution)/shard_map/all_gather | solution.py:425
  298.0 0.5 convolution_convert_fusion.6
  298.5 0.9 copy.42.g
  299.4 13.4 %attend_back.1 = (bf16[640,192]{1,0:T(8,128)(2,1)}, bf16[192,2560]{1,0:T(8,128)(2,1)}, bf16[192,2560]{1,0:T(8,128)(2,1)}, bf16[3,512,512]{2,1,0:T(8,128)(2,1)}) custom-call(s32[1,20]{1,0:T(1,128)} %parents.3, bf16[640,384]{1,0:T(8,128)(2,1)} %get-tuple-element.29.q, bf16[2560,384]{1,0:T(8,128)(2,1)} %get-tuple-element.30.k, ...), custom_call_target="tpu_custom_call" | custom-call | flops 3145728000 | bytes 20971520 | tf_op jit(solution)/shard_map/attend_back/pallas_call | solution.py:358
  312.8 2.4 copy.43
  315.3 2.4 copy.45
  317.8 0.4 convolution_convert_fusion.5
  318.2 0.9 copy.47
  319.2 2.5 convolution_convert_fusion.4
  321.8 15.6 %reduce-scatter.40.cloned.1.call-done = bf16[640,192]{1,0:T(8,128)(2,1)} async-done(((bf16[2560,192]{1,0:T(8,128)(2,1)}), bf16[640,192]{1,0:T(8,128)(2,1)}) %reduce-scatter.40.cloned.1.call-update) | async-done | bytes 245776
  337.4 2.2 convolution_convert_fusion.3
  339.7 24.4 %reduce-scatter.42.cloned.1.call-done = bf16[640,192]{1,0:T(8,128)(2,1)} async-done(((bf16[2560,192]{1,0:T(8,128)(2,1)}), bf16[640,192]{1,0:T(8,128)(2,1)}) %reduce-scatter.42.cloned.1.call-update) | async-done | bytes 245776
  364.0 2.2 convolution_convert_fusion.2
  366.4 3.5 convolution_convert_fusion.1
  369.9 2.2 convolution_convert_fusion
  372.2 0.5 reduce-scatter.38.cloned.1.call-update
  372.9 25.8 %all_gather.36 = bf16[768,192]{1,0:T(8,128)(2,1)} all-gather(bf16[96,192]{1,0:T(8,128)(2,1)S(1)} %copy-done.11), channel_id=1, replica_groups=mesh['shard'=8,'ctx'=4,'tp'=4] {'shard'}, dimensions={0}, use_global_device_ids=true | all-gather | bytes 331776 | tf_op jit(solution)/shard_map/all_gather | solution.py:624
  398.7 22.7 %all_gather.37 = bf16[768,192]{1,0:T(8,128)(2,1)S(1)} all-gather(bf16[96,192]{1,0:T(8,128)(2,1)S(1)} %copy-done.12), channel_id=1, replica_groups=mesh['shard'=8,'ctx'=4,'tp'=4] {'shard'}, dimensions={0}, use_global_device_ids=true | all-gather | bytes 331776 | tf_op jit(solution)/shard_map/all_gather | solution.py:625
  421.4 23.5 %all_gather.38 = bf16[768,192]{1,0:T(8,128)(2,1)S(1)} all-gather(bf16[96,192]{1,0:T(8,128)(2,1)S(1)} %copy-done.13), channel_id=1, replica_groups=mesh['shard'=8,'ctx'=4,'tp'=4] {'shard'}, dimensions={0}, use_global_device_ids=true | all-gather | bytes 331776 | tf_op jit(solution)/shard_map/all_gather | solution.py:626
  445.0 1.5 copy.48
  446.5 32.9 %reduce-scatter.30.cloned.1.call-done = bf16[96,192]{1,0:T(8,128)(2,1)} async-done(((bf16[768,192]{1,0:T(8,128)(2,1)}), bf16[96,192]{1,0:T(8,128)(2,1)}) %reduce-scatter.30.cloned.1.call-update) | async-done | bytes 36880 | tf_op jit(solution)/shard_map/reduce_scatter | solution.py:691
  479.4 38.7 %reduce-scatter.32.cloned.1.call-done = bf16[96,192]{1,0:T(8,128)(2,1)} async-done(((bf16[768,192]{1,0:T(8,128)(2,1)}), bf16[96,192]{1,0:T(8,128)(2,1)}) %reduce-scatter.32.cloned.1.call-update) | async-done | bytes 36880 | tf_op jit(solution)/shard_map/reduce_scatter | solution.py:694
  518.1 1.6 fusion.26
  519.7 39.1 %reduce-scatter.34.cloned.1.call-done = bf16[96,768]{1,0:T(8,128)(2,1)} async-done(((bf16[768,768]{1,0:T(8,128)(2,1)}), bf16[96,768]{1,0:T(8,128)(2,1)}) %reduce-scatter.34.cloned.1.call-update) | async-done | bytes 147472 | tf_op jit(solution)/shard_map/reduce_scatter | solution.py:697
  558.7 40.8 %reduce-scatter.36.cloned.1.call-done = bf16[768,96]{0,1:T(8,128)(2,1)} async-done(((bf16[768,768]{0,1:T(8,128)(2,1)}), bf16[768,96]{0,1:T(8,128)(2,1)}) %reduce-scatter.36.cloned.1.call-update) | async-done | bytes 147472 | tf_op jit(solution)/shard_map/reduce_scatter | solution.py:703
  599.6 41.6 %reduce-scatter.38.cloned.1.call-done = bf16[3,64,512]{2,1,0:T(8,128)(2,1)} async-done(((bf16[3,512,512]{2,1,0:T(8,128)(2,1)}), bf16[3,64,512]{2,1,0:T(8,128)(2,1)}) %reduce-scatter.38.cloned.1.call-update) | async-done | bytes 196624 | tf_op jit(solution)/shard_map/reduce_scatter | solution.py:706
  641.2 1.5 fusion.27
  642.7 1.8 add_add_fusion
  644.6 71.1 %all-reduce = (f32[768]{0:T(1024)}, f32[768]{0:T(1024)}, f32[768]{0:T(1024)}, f32[768]{0:T(1024)}, f32[768]{0:T(1024)}, /*index=5*/f32[768]{0:T(1024)}) all-reduce(f32[768]{0:T(1024)S(1)} %get-tuple-element.66, f32[768]{0:T(1024)S(1)} %get-tuple-element.40, ...), channel_id=1, replica_groups=mesh['shard'=8,'ctx'=4,'tp'=4] {'shard','ctx','tp'}, use_global_device_ids=true, to_apply=%region_29.0 | all-reduce | flops 4608 | bytes 36864 | tf_op jit(solution)/shard_map/psum | solution.py:721
  716.1 67.0 %all-reduce.1 = (f32[192]{0:T(256)}, f32[192]{0:T(256)}, f32[768]{0:T(1024)}) all-reduce(f32[192]{0:T(256)S(1)} %convert_reduce_fusion.2, f32[192]{0:T(256)S(1)} %convert_reduce_fusion.5, f32[768]{0:T(1024)S(1)} %get-tuple-element.69), channel_id=1, replica_groups=mesh['shard'=8,'ctx'=4,'tp'=4] {'shard','ctx'}, use_global_device_ids=true, to_apply=%region_19.0 | all-reduce | flops 1152 | bytes 9216 | tf_op jit(solution)/shard_map/psum | solution.py:720
  783.1 1.4 convert_element_type.105
  784.6 1.4 convert_element_type.108
  786.0 1.4 convert_element_type.110
  787.5 1.4 convert_element_type.113
  788.9 1.6 convert_element_type.116
  790.6 1.6 convert_element_type.119
  792.2 1.8 divide_multiply_fusion
  794.0 1.9 add.159
  (106 shorter events, 2.4 us)
Async XLA Ops:
  8.0 125.8 %reduce-scatter.20.cloned.1.call-start = ((), (), s32[]{:S(2)}) async-start(), calls=%async_computation.13 | async-start | bytes 2457600 | tf_op jit(solution)/shard_map/reduce_scatter | solution.py:429
  93.6 40.2 %copy-start.10 = (bf16[160,768]{1,0:T(8,128)(2,1)S(1)}, bf16[160,768]{1,0:T(8,128)(2,1)}, u32[]{:S(2)}) copy-start(bf16[160,768]{1,0:T(8,128)(2,1)} %tok.1) | copy-start | bytes 737284
  93.6 40.2 %copy-start.17 = (f32[768]{0:T(1024)S(1)}, f32[768]{0:T(1024)}, u32[]{:S(2)}) copy-start(f32[768]{0:T(1024)} %param.28) | copy-start | bytes 9220
  96.4 38.8 %copy-start.14 = (f32[768]{0:T(1024)S(1)}, f32[768]{0:T(1024)}, u32[]{:S(2)}) copy-start(f32[768]{0:T(1024)} %param.29) | copy-start | bytes 9220
  96.4 38.8 %copy-start.16 = (f32[768]{0:T(1024)S(1)}, f32[768]{0:T(1024)}, u32[]{:S(2)}) copy-start(f32[768]{0:T(1024)} %param.30) | copy-start | bytes 9220
  96.5 52.0 %all-gather.3.cloned.1.call-start = ((), (), s32[]{:S(2)}) async-start(), calls=%async_computation.14 | async-start | bytes 1327104 | tf_op jit(solution)/shard_map/all_gather | solution.py:605
  97.0 51.4 %copy-start.23 = (f32[768]{0:T(1024)S(1)}, f32[768]{0:T(1024)}, u32[]{:S(2)}) copy-start(f32[768]{0:T(1024)} %param.32) | copy-start | bytes 9220
  97.1 86.0 %all-gather.5.cloned.1.call-start = ((), (), s32[]{:S(2)}) async-start(), calls=%async_computation.15 | async-start | bytes 1327104 | tf_op jit(solution)/shard_map/all_gather | solution.py:607
  97.6 131.2 %reduce-scatter.22.cloned.1.call-start = ((), (), s32[]{:S(2)}) async-start(), calls=%async_computation.16 | async-start | bytes 2457600 | tf_op jit(solution)/shard_map/reduce_scatter | solution.py:429
  186.9 42.0 %copy-start.18 = (f32[768]{0:T(1024)S(1)}, f32[768]{0:T(1024)}, u32[]{:S(2)}) copy-start(f32[768]{0:T(1024)} %param.34) | copy-start | bytes 9220
  186.9 43.7 %copy-start = (bf16[160,768]{1,0:T(8,128)(2,1)S(1)}, bf16[160,768]{1,0:T(8,128)(2,1)}, u32[]{:S(2)}) copy-start(bf16[160,768]{1,0:T(8,128)(2,1)} %param.39) | copy-start | bytes 737284
  186.9 43.7 %copy-start.15 = (f32[768]{0:T(1024)S(1)}, f32[768]{0:T(1024)}, u32[]{:S(2)}) copy-start(f32[768]{0:T(1024)} %param.35) | copy-start | bytes 9220
  186.9 97.2 %reduce-scatter.24.cloned.1.call-start = ((), (), s32[]{:S(2)}) async-start(), calls=%async_computation.17 | async-start | bytes 2457600 | tf_op jit(solution)/shard_map/reduce_scatter | solution.py:429
  228.9 13.8 %copy-start.27 = (f32[640,768]{1,0:T(8,128)S(1)}, f32[640,768]{1,0:T(8,128)}, u32[]{:S(2)}) copy-start(f32[640,768]{1,0:T(8,128)} %get-tuple-element.79) | copy-start | bytes 5898244
  230.3 12.4 %copy-start.21 = (bf16[768,768]{0,1:T(8,128)(2,1)S(1)}, bf16[768,768]{0,1:T(8,128)(2,1)}, u32[]{:S(2)}) copy-start(bf16[768,768]{0,1:T(8,128)(2,1)} %all-gather.5.cloned.1.call-done) | copy-start | bytes 3538948
  230.4 12.3 %copy-start.26 = (f32[640,768]{1,0:T(8,128)S(1)}, f32[640,768]{1,0:T(8,128)}, u32[]{:S(2)}) copy-start(f32[640,768]{1,0:T(8,128)} %get-tuple-element.75) | copy-start | bytes 5898244
  242.7 1.5 copy-start.8
  242.7 2.5 copy-start.20
  244.2 1.0 copy-start.25
  247.5 36.7 %copy-start.19 = (f32[768]{0:T(1024)S(1)}, f32[768]{0:T(1024)}, u32[]{:S(2)}) copy-start(f32[768]{0:T(1024)} %param.36) | copy-start | bytes 9220
  247.5 89.9 %reduce-scatter.40.cloned.1.call-start = ((), (), s32[]{:S(2)}) async-start(), calls=%async_computation.25 | async-start | bytes 1638400
  315.2 2.6 copy-start.7
  315.2 48.8 %reduce-scatter.42.cloned.1.call-start = ((), (), s32[]{:S(2)}) async-start(), calls=%async_computation.26 | async-start | bytes 1638400
  317.7 1.5 copy-start.5
  317.7 127.3 %reduce-scatter.44.cloned.1.call-start = ((), (), s32[]{:S(2)}) async-start(), calls=%async_computation.27 | async-start | bytes 442368
  318.2 19.2 %copy-start.22 = (bf16[640,768]{1,0:T(8,128)(2,1)S(1)}, bf16[640,768]{1,0:T(8,128)(2,1)}, u32[]{:S(2)}) copy-start(bf16[640,768]{1,0:T(8,128)(2,1)} %get-tuple-element.38) | copy-start | bytes 2949124
  319.2 127.3 %reduce-scatter.28.cloned.1.call-start = ((), (), s32[]{:S(2)}) async-start(), calls=%async_computation.19 | async-start | bytes 442368 | tf_op jit(solution)/shard_map/reduce_scatter | solution.py:688
  321.7 157.6 %reduce-scatter.30.cloned.1.call-start = ((), (), s32[]{:S(2)}) async-start(), calls=%async_computation.20 | async-start | bytes 442368 | tf_op jit(solution)/shard_map/reduce_scatter | solution.py:691
  339.6 178.4 %reduce-scatter.32.cloned.1.call-start = ((), (), s32[]{:S(2)}) async-start(), calls=%async_computation.21 | async-start | bytes 442368 | tf_op jit(solution)/shard_map/reduce_scatter | solution.py:694
  366.3 3.6 copy-start.9
  366.3 3.6 copy-start.24
  366.3 192.4 %reduce-scatter.34.cloned.1.call-start = ((), (), s32[]{:S(2)}) async-start(), calls=%async_computation.22 | async-start | bytes 1327104 | tf_op jit(solution)/shard_map/reduce_scatter | solution.py:697
  369.9 229.7 %reduce-scatter.36.cloned.1.call-start = ((), (), s32[]{:S(2)}) async-start(), calls=%async_computation.23 | async-start | bytes 1327104 | tf_op jit(solution)/shard_map/reduce_scatter | solution.py:703
  372.1 0.8 copy-start.11
  372.1 26.6 %copy-start.12 = (bf16[96,192]{1,0:T(8,128)(2,1)S(1)}, bf16[96,192]{1,0:T(8,128)(2,1)}, u32[]{:S(2)}) copy-start(bf16[96,192]{1,0:T(8,128)(2,1)} %wk.1) | copy-start | bytes 110596
  372.1 49.3 %copy-start.13 = (bf16[96,192]{1,0:T(8,128)(2,1)S(1)}, bf16[96,192]{1,0:T(8,128)(2,1)}, u32[]{:S(2)}) copy-start(bf16[96,192]{1,0:T(8,128)(2,1)} %wv.1) | copy-start | bytes 110596
  372.1 269.0 %reduce-scatter.38.cloned.1.call-start = ((), (), s32[]{:S(2)}) async-start(), calls=%async_computation.24 | async-start | bytes 1769472 | tf_op jit(solution)/shard_map/reduce_scatter | solution.py:706
  372.7 410.4 %all-reduce.7.cloned.1.call-start = ((), (), s32[]{:S(2)}) async-start(), calls=%async_computation.28 | async-start | bytes 393216 | tf_op jit(solution)/shard_map/psum | solution.py:711
  518.1 270.9 %all-reduce.9.cloned.1.call-start = ((), (), s32[]{:S(2)}) async-start(), calls=%async_computation.29 | async-start | bytes 983040 | tf_op jit(solution)/shard_map/psum | solution.py:714
  641.2 152.8 %reduce-scatter.26.cloned.1.call-start = ((), (), s32[]{:S(2)}) async-start(), calls=%async_computation.18 | async-start | bytes 2457600 | tf_op jit(solution)/shard_map/reduce_scatter | solution.py:429
  641.2 1.5 copy-start.3
  644.5 71.2 %copy-start.6 = (bf16[640,192]{1,0:T(8,128)(2,1)S(1)}, bf16[640,192]{1,0:T(8,128)(2,1)}, u32[]{:S(2)}) copy-start(bf16[640,192]{1,0:T(8,128)(2,1)} %get-tuple-element.35) | copy-start | bytes 737284
  644.5 71.3 %copy-start.4 = (bf16[640,192]{1,0:T(8,128)(2,1)S(1)}, bf16[640,192]{1,0:T(8,128)(2,1)}, u32[]{:S(2)}) copy-start(bf16[640,192]{1,0:T(8,128)(2,1)} %reduce-scatter.42.cloned.1.call-done) | copy-start | bytes 737284
  644.5 147.7 %copy-start.1 = (f32[3,64,512]{2,1,0:T(8,128)S(1)}, f32[3,64,512]{2,1,0:T(8,128)}, u32[]{:S(2)}) copy-start(f32[3,64,512]{2,1,0:T(8,128)} %logits.1) | copy-start | bytes 1179652
  644.5 147.7 %copy-start.2 = (f32[3,64,512]{2,1,0:T(8,128)S(1)}, f32[3,64,512]{2,1,0:T(8,128)}, u32[]{:S(2)}) copy-start(f32[3,64,512]{2,1,0:T(8,128)} %noise.1) | copy-start | bytes 1179652
Sparse Core Ops, SparseCore 0:
  96.6 37.1 reduce-scatter.19
  187.1 41.7 reduce-scatter.21
  247.6 36.4 reduce-scatter.23
  644.7 41.6 reduce-scatter.25
Sparse Core Ops, SparseCore 1:
  98.7 44.0 all-gather.2
  144.3 38.7 all-gather.4
  315.3 22.0 reduce-scatter.39
  339.9 24.0 reduce-scatter.41
  366.4 34.0 reduce-scatter.43
  403.5 36.6 reduce-scatter.27
  443.0 36.3 reduce-scatter.29
  481.7 36.2 reduce-scatter.31
  520.3 38.4 reduce-scatter.33
  561.1 38.3 reduce-scatter.35
  601.8 39.3 reduce-scatter.37
  644.3 43.5 all-reduce.6
  690.4 42.9 all-reduce.8

commit v2 on v1

v2 whole, which is shorter than its diff:
```python
import jax
import jax.numpy as jnp
from jax import lax
from jax.experimental import pallas as pl
from jax.experimental.pallas import tpu as pltpu
from jax.sharding import PartitionSpec as P

MESH = pl.DeviceIdType.MESH
BF = jnp.bfloat16
F32 = jnp.float32
HEADS_DEV = 3
HEAD_DIM = 64
WIDE = 128
SEG = 128
SEGS = 20
PATH = 10
KEYS = PATH * SEG
D = 768
QK = 192
QKW = 384
ROWS = 160
CTX_ROWS = 640
TREE = 2560
DEPTHS = 512
MIB = 2**20
VM = pl.BlockSpec(memory_space=pltpu.VMEM)
SM = pl.BlockSpec(memory_space=pltpu.SMEM)


def place():
    shard = lax.axis_index("shard")
    tp = lax.axis_index("tp")
    return {
        "x": lax.axis_index("ctx"),
        "yl": lax.div(shard, 4),
        "z": lax.rem(shard, 4),
        "yh": lax.div(tp, 2),
        "core": lax.rem(tp, 2),
    }


def ident(at, **moved):
    to = {**at, **moved}
    return {"shard": to["yl"] * 4 + to["z"], "ctx": to["x"], "tp": to["yh"] * 2 + to["core"]}


def around(value, step):
    return lax.rem(value + step, 4)


def greet(devices):
    barrier = pltpu.get_barrier_semaphore()
    for device in devices:
        pl.semaphore_signal(barrier, inc=1, device_id=device, device_id_type=MESH)
    pl.semaphore_wait(barrier, len(devices))


class Mail:
    def __init__(self, send, recv):
        self.send, self.recv, self.used, self.sent = send, recv, 0, []

    def post(self, src, dst, device):
        copy = pltpu.make_async_remote_copy(
            src_ref=src,
            dst_ref=dst,
            send_sem=self.send.at[self.used],
            recv_sem=self.recv.at[self.used],
            device_id=device,
            device_id_type=MESH,
        )
        self.used += 1
        copy.start()
        self.sent.append(copy)
        return copy

    def done(self, copy):
        copy.wait()
        self.sent = [kept for kept in self.sent if kept is not copy]

    def close(self):
        for copy in self.sent:
            copy.wait_send()


def nn(a, b):
    return jnp.dot(a, b, preferred_element_type=F32)


def nt(a, b):
    return lax.dot_general(a, b, (((1,), (1,)), ((), ())), preferred_element_type=F32)


def spread(kind=BF):
    rows = lax.broadcasted_iota(jnp.int32, (QK, QKW), 0)
    cols = lax.broadcasted_iota(jnp.int32, (QK, QKW), 1)
    head, lane = cols // WIDE, cols % WIDE
    return ((head * HEAD_DIM + lane == rows) & (lane < HEAD_DIM)).astype(kind)


def project_kernel(
    tok,
    wq,
    wk,
    wv,
    qb,
    vb,
    logits,
    noise,
    q_out,
    k_out,
    v_out,
    rows_out,
    tab,
    ws,
    xs,
    wide,
    send,
    recv,
):
    at = place()
    x, yl, z, yh, core = at["x"], at["yl"], at["z"], at["yh"], at["core"]
    shard, tp = yl * 4 + z, yh * 2 + core
    sib = ident(at, core=1 - core)
    far = ident(at, yh=1 - yh)
    low = ident(at, yl=1 - yl)
    zs = [ident(at, z=around(z, k)) for k in (1, 2, 3)]
    xp = [ident(at, x=around(x, k)) for k in (1, 2, 3)]
    xs[x, tp] = tok[...]
    for j, w in enumerate((wq, wk, wv)):
        ws[shard, j] = w[...]
    masks = logits[...] + noise[...]
    tab[:, shard] = jax.nn.log_sigmoid(masks).astype(BF)
    greet([sib, far, low, *zs, *xp])
    mail = Mail(send, recv)

    def block(kx, other):
        return xs.at[around(x, 4 - kx), (1 - yh if other else yh) * 2 + core]

    def pass_on(src, device):
        return mail.post(src, src, device)

    first_far = pass_on(block(0, False), far)
    own_low = [pass_on(ws.at[shard], low), pass_on(tab.at[0, shard], low)]
    own_x = [pass_on(block(0, False), d) for d in xp]
    own_z = [pass_on(ws.at[shard], d) for d in zs]
    own_z0 = [pass_on(tab.at[0, shard], d) for d in zs]
    own_z1 = [pass_on(tab.at[pl.ds(1, 2), shard], d) for d in zs]
    to_low = [pass_on(tab.at[pl.ds(1, 2), shard], low)]
    to_sib = [pass_on(block(0, False), sib)]
    first_far.wait_recv()
    far_x = [pass_on(block(0, True), d) for d in xp]
    to_sib.append(pass_on(block(0, True), sib))
    for copy in own_low:
        copy.wait_recv()
    mate = (1 - yl) * 4 + z
    low_z = [pass_on(ws.at[mate], d) for d in zs]
    low_z0 = [pass_on(tab.at[0, mate], d) for d in zs]
    for k in (1, 3, 2):
        own_x[k - 1].wait_recv()
        to_sib.append(pass_on(block(k, False), sib))
    for k in (1, 3, 2):
        own_z1[k - 1].wait_recv()
        to_low.append(pass_on(tab.at[pl.ds(1, 2), yl * 4 + around(z, 4 - k)], low))
    for k in (1, 3, 2):
        far_x[k - 1].wait_recv()
        to_sib.append(pass_on(block(k, True), sib))
    for copy in own_z + own_z0 + low_z + to_sib:
        copy.wait_recv()

    hots = spread()
    hots32 = spread(F32)
    for j in range(3):
        whole = ws[:, j].reshape(D, QK)
        wide[:, j * QKW : (j + 1) * QKW] = nn(whole, hots).astype(BF)
    q_add = jnp.dot(qb[...], hots32, precision=lax.Precision.HIGHEST)
    v_add = jnp.dot(vb[...], hots32, precision=lax.Precision.HIGHEST)

    @pl.loop(0, 16)
    def _(i):
        rows = xs[lax.div(i, 4), lax.rem(i, 4)]
        both = nn(rows, wide[:, QKW:])
        k_out[pl.ds(i * ROWS, ROWS), :] = both[:, :QKW].astype(BF)
        v_out[pl.ds(i * ROWS, ROWS), :] = (both[:, QKW:] + v_add).astype(BF)

    @pl.loop(0, 4)
    def _(i):
        rows = xs[x, i]
        rows_out[pl.ds(i * ROWS, ROWS), :] = rows
        q_out[pl.ds(i * ROWS, ROWS), :] = (nn(rows, wide[:, :QKW]) + q_add).astype(BF)

    for copy in low_z0 + to_low:
        copy.wait_recv()
    mail.close()


def project(tokens, wq, wk, wv, qb, vb, logits, noise):
    shape = jax.ShapeDtypeStruct
    posts = 2 + 1 + 3 + 9 + 1 + 8 + 3 + 6 + 3
    return pl.pallas_call(
        project_kernel,
        out_shape=(
            shape((CTX_ROWS, QKW), BF),
            shape((TREE, QKW), BF),
            shape((TREE, QKW), BF),
            shape((CTX_ROWS, D), BF),
            shape((HEADS_DEV, 8, 64, DEPTHS), BF),
            shape((8, 3, 96, QK), BF),
        ),
        in_specs=[VM] * 8,
        out_specs=[VM] * 6,
        scratch_shapes=[
            pltpu.VMEM((4, 4, ROWS, D), BF),
            pltpu.VMEM((D, 3 * QKW), BF),
            pltpu.SemaphoreType.DMA((posts,)),
            pltpu.SemaphoreType.DMA((posts,)),
        ],
        compiler_params=pltpu.CompilerParams(
            collective_id=1, has_side_effects=True, vmem_limit_bytes=56 * MIB
        ),
        name="project",
    )(tokens, wq, wk, wv, qb.reshape(1, QK), vb.reshape(1, QK), logits, noise)


def climb(parents, seg, trail):
    trail[0] = seg
    depth = jnp.int32(0)
    here = seg
    for i in range(1, PATH):
        up = parents[0, here]
        found = up >= 0
        here = jnp.where(found, up, here)
        trail[i] = here
        depth = depth + found.astype(jnp.int32)
    return depth


def on_path(trail, depth, j):
    return trail[jnp.maximum(depth - j, 0)]


def attend_kernel(parents, q, k, v, tab, o_out, p_out, trail, kp, vp):
    a = pl.program_id(0)
    seg = lax.axis_index("ctx") * 5 + a
    depth = climb(parents, seg, trail)
    for j in range(PATH):
        rows = pl.ds(pl.multiple_of(on_path(trail, depth, j) * SEG, SEG), SEG)
        kp[pl.ds(j * SEG, SEG), :] = k[rows, :]
        vp[pl.ds(j * SEG, SEG), :] = v[rows, :]
    tile = pl.ds(pl.multiple_of(lax.rem(depth, 4) * SEG, SEG), SEG)
    outs = []
    for h in range(HEADS_DEV):
        head = slice(h * WIDE, (h + 1) * WIDE)
        mine = q[:, head] * jnp.asarray(HEAD_DIM**-0.5, BF)
        bias = tab[h, tile, :].astype(F32)
        scores = nt(mine, kp[:, head])
        parts = []
        for j in range(PATH):
            cols = slice((j % 4) * SEG, (j % 4 + 1) * SEG)
            part = scores[:, j * SEG : (j + 1) * SEG] + bias[:, cols]
            parts.append(jnp.where(j <= depth, part, -1e30))
        scores = jnp.concatenate(parts, axis=1)
        peak = jnp.max(scores, axis=1, keepdims=True)
        raised = jnp.exp(scores - peak)
        total = jnp.sum(raised, axis=1, keepdims=True)
        soft = (raised * (1.0 / total)).astype(BF)
        p_out[0, h] = soft
        outs.append(nn(soft, vp[:, head]).astype(BF))
    o_out[...] = nt(jnp.concatenate(outs, axis=1), spread()).astype(BF)


def whole(shape):
    return pl.BlockSpec(shape, lambda a: (0,) * len(shape))


def attend(parents, q, k, v, tab):
    shape = jax.ShapeDtypeStruct
    return pl.pallas_call(
        attend_kernel,
        grid=(5,),
        out_shape=(
            shape((CTX_ROWS, QK), BF),
            shape((5, HEADS_DEV, SEG, KEYS), BF),
        ),
        in_specs=[
            SM,
            pl.BlockSpec((SEG, QKW), lambda a: (a, 0)),
            whole((TREE, QKW)),
            whole((TREE, QKW)),
            whole((HEADS_DEV, DEPTHS, DEPTHS)),
        ],
        out_specs=(
            pl.BlockSpec((SEG, QK), lambda a: (a, 0)),
            pl.BlockSpec((1, HEADS_DEV, SEG, KEYS), lambda a: (a, 0, 0, 0)),
        ),
        scratch_shapes=[
            pltpu.SMEM((PATH,), jnp.int32),
            pltpu.VMEM((KEYS, QKW), BF),
            pltpu.VMEM((KEYS, QKW), BF),
        ],
        compiler_params=pltpu.CompilerParams(vmem_limit_bytes=56 * MIB),
        cost_estimate=pl.CostEstimate(
            flops=2 * 2 * 15 * SEG * KEYS * WIDE, bytes_accessed=12 * MIB, transcendentals=15 * SEG * KEYS
        ),
        name="attend",
    )(parents, q, k, v, tab)


def attend_back_kernel(
    parents, q, k, v, o, g, p, dq_out, dk_out, dv_out, tab_out, trail, kp, vp, dk, dv, dtab
):
    a = pl.program_id(0)
    seg = lax.axis_index("ctx") * 5 + a

    @pl.when(a == 0)
    def _():
        dk[...] = jnp.zeros_like(dk)
        dv[...] = jnp.zeros_like(dv)
        dtab[...] = jnp.zeros_like(dtab)

    depth = climb(parents, seg, trail)
    starts = [pl.multiple_of(on_path(trail, depth, j) * SEG, SEG) for j in range(PATH)]
    for j in range(PATH):
        kp[pl.ds(j * SEG, SEG), :] = k[pl.ds(starts[j], SEG), :]
        vp[pl.ds(j * SEG, SEG), :] = v[pl.ds(starts[j], SEG), :]
    tile = pl.ds(pl.multiple_of(lax.rem(depth, 4) * SEG, SEG), SEG)
    hots = spread()
    g_wide = nn(g[...], hots).astype(BF)
    o_wide = nn(o[...], hots)
    scale = HEAD_DIM**-0.5
    outs = []
    for h in range(HEADS_DEV):
        head = slice(h * WIDE, (h + 1) * WIDE)
        mine, grad = q[:, head], g_wide[:, head]
        soft = p[0, h]
        inner = jnp.sum(grad.astype(F32) * o_wide[:, head], axis=1, keepdims=True)
        ds = soft.astype(F32) * (nt(grad, vp[:, head]) - inner)
        low = ds.astype(BF)
        outs.append((nn(low, kp[:, head]) * scale).astype(BF))
        mine_t = (mine.astype(F32).T[:HEAD_DIM] * scale).astype(BF)
        grad_t = grad.astype(F32).T[:HEAD_DIM].astype(BF)
        dk_part = nn(mine_t, low)
        dv_part = nn(grad_t, soft)
        for j in range(PATH):
            cols = slice(j * SEG, (j + 1) * SEG)
            dk[h, :, pl.ds(starts[j], SEG)] += dk_part[:, cols]
            dv[h, :, pl.ds(starts[j], SEG)] += dv_part[:, cols]
        down = low.astype(F32)
        dtab[h, tile, 0:256] += down[:, 0:256] + down[:, 512:768] + down[:, 1024:1280]
        dtab[h, tile, 256:512] += down[:, 256:512] + down[:, 768:1024]
    dq_out[...] = nt(jnp.concatenate(outs, axis=1), hots).astype(BF)

    @pl.when(a == 4)
    def _():
        for h in range(HEADS_DEV):
            dk_out[pl.ds(h * HEAD_DIM, HEAD_DIM), :] = dk[h].astype(BF)
            dv_out[pl.ds(h * HEAD_DIM, HEAD_DIM), :] = dv[h].astype(BF)
            tab_out[h] = dtab[h].astype(BF)


def attend_back(parents, q, k, v, o, g, p):
    shape = jax.ShapeDtypeStruct
    return pl.pallas_call(
        attend_back_kernel,
        grid=(5,),
        out_shape=(
            shape((CTX_ROWS, QK), BF),
            shape((QK, TREE), BF),
            shape((QK, TREE), BF),
            shape((HEADS_DEV, DEPTHS, DEPTHS), BF),
        ),
        in_specs=[
            SM,
            pl.BlockSpec((SEG, QKW), lambda a: (a, 0)),
            whole((TREE, QKW)),
            whole((TREE, QKW)),
            pl.BlockSpec((SEG, QK), lambda a: (a, 0)),
            pl.BlockSpec((SEG, QK), lambda a: (a, 0)),
            pl.BlockSpec((1, HEADS_DEV, SEG, KEYS), lambda a: (a, 0, 0, 0)),
        ],
        out_specs=(
            pl.BlockSpec((SEG, QK), lambda a: (a, 0)),
            whole((QK, TREE)),
            whole((QK, TREE)),
            whole((HEADS_DEV, DEPTHS, DEPTHS)),
        ),
        scratch_shapes=[
            pltpu.SMEM((PATH,), jnp.int32),
            pltpu.VMEM((KEYS, QKW), BF),
            pltpu.VMEM((KEYS, QKW), BF),
            pltpu.VMEM((HEADS_DEV, HEAD_DIM, TREE), F32),
            pltpu.VMEM((HEADS_DEV, HEAD_DIM, TREE), F32),
            pltpu.VMEM((HEADS_DEV, DEPTHS, DEPTHS), F32),
        ],
        compiler_params=pltpu.CompilerParams(vmem_limit_bytes=56 * MIB),
        cost_estimate=pl.CostEstimate(
            flops=5 * 2 * 15 * SEG * KEYS * WIDE, bytes_accessed=20 * MIB, transcendentals=0
        ),
        name="attend_back",
    )(parents, q, k, v, o, g, p)


def tn(a, b):
    return lax.dot_general(a, b, (((0,), (0,)), ((), ())), preferred_element_type=F32)


def unit(n):
    rows = lax.broadcasted_iota(jnp.int32, (n, n), 0)
    cols = lax.broadcasted_iota(jnp.int32, (n, n), 1)
    return (rows == cols).astype(BF)


def y_peers(at):
    spots = []
    for k in (1, 2, 3):
        y = around(at["yh"] * 2 + at["yl"], k)
        spots.append((lax.div(y, 2), lax.rem(y, 2)))
    return spots


def normed(values):
    centre = jnp.mean(values, axis=1, keepdims=True)
    off = values - centre
    inverse = lax.rsqrt(jnp.mean(off * off, axis=1, keepdims=True) + 1e-5)
    return off * inverse, inverse


def normed_back(grad, gain, n, inverse):
    e = grad * gain
    return inverse * (e - jnp.mean(e, axis=1, keepdims=True) - n * jnp.mean(e * n, axis=1, keepdims=True))


def total(values):
    return jnp.sum(values, axis=0, keepdims=True)


def middle_kernel(
    o,
    tok,
    cot,
    wo,
    wi,
    wout,
    bo,
    g1,
    s1,
    bi,
    bout,
    g2,
    s2,
    result,
    dh1_out,
    g_out,
    grads,
    grads_o,
    vec,
    w,
    wt,
    o2,
    bias,
    part,
    got,
    rows,
    act,
    slope,
    du,
    y1s,
    n1s,
    dh2s,
    leave,
    send,
    recv,
):
    at = place()
    x, yl, z, yh, core = at["x"], at["yl"], at["z"], at["yh"], at["core"]
    sib = ident(at, core=1 - core)
    far = ident(at, yh=1 - yh)
    xp = [ident(at, x=around(x, k)) for k in (1, 2, 3)]
    zp = [ident(at, z=around(z, k)) for k in (1, 2, 3)]
    yp = [ident(at, yh=a, yl=b) for a, b in y_peers(at)]
    yz = [
        ident(at, yh=a, yl=b, z=around(z, k)) for a, b in y_peers(at) for k in (1, 2, 3)
    ]
    w[yh, yl, z, :, 0:D] = wi[...]
    w[yh, yl, z, :, D : 2 * D] = nt(unit(96), wout[...]).astype(BF)
    wt[yh, yl, z] = nt(unit(96), wo[...]).astype(BF)
    bias[yh] = bi[...]
    o2[yh] = o[pl.ds(yh * 320, 320), :]
    greet([sib, *xp, *zp, *yp, *yz])
    mail = Mail(send, recv)

    def pass_on(src, device):
        return mail.post(src, src, device)

    def waits(copies):
        for copy in copies:
            copy.wait_recv()

    q = pl.multiple_of(x * 128, 128)
    q1, q2 = pl.ds(512 + q, 128), pl.ds(1024 + q, 128)
    all_o = [mail.post(o.at[pl.ds((1 - yh) * 320, 320)], o2.at[yh], far)]
    all_o += [pass_on(wt.at[yh, yl, z], d) for d in yp + zp + yz]
    one_z = [pass_on(w.at[yh, yl, z, :, q1], d) for d in zp]
    two_y = [pass_on(w.at[yh, yl, z, :, q2], d) for d in yp]
    zero_y = [pass_on(w.at[yh, yl, z, :, pl.ds(0, 512)], d) for d in yp]
    bias_far = pass_on(bias.at[yh], far)
    waits(one_z)
    one_x = [pass_on(w.at[yh, yl, :, :, q1], d) for d in xp]
    waits(two_y)
    two_z = [pass_on(w.at[:, :, z, :, q2], d) for d in zp]
    waits(zero_y)
    zero_z = [pass_on(w.at[:, :, z, :, pl.ds(0, 512)], d) for d in zp]
    waits(two_z)
    two_x = [pass_on(w.at[:, :, :, :, q2], d) for d in xp]
    waits(one_x)
    one_y = [pass_on(w.at[yh, yl, :, :, pl.ds(512, 512)], d) for d in yp]
    waits(all_o)

    mine, other = pl.ds(core * ROWS, ROWS), pl.ds((1 - core) * ROWS, ROWS)

    def trade_sum(slot):
        mail.done(mail.post(part.at[other], got.at[slot], sib))
        return part[mine, :] + got[slot]

    def trade_rows(slot, values):
        rows[slot, mine, :] = values
        copy = pass_on(rows.at[slot, mine], sib)
        copy.wait_recv()

    for half in range(2):
        cols = slice(half * 384, (half + 1) * 384)
        part[:, cols] = nt(o2[0], wt[0, half].reshape(384, QK)) + nt(
            o2[1], wt[1, half].reshape(384, QK)
        )
    n1, inv1 = normed(tok[...].astype(F32) + trade_sum(0) + bo[...])
    n1s[...] = n1
    y1 = n1 * g1[...] + s1[...]
    y1s[...] = y1
    trade_rows(0, y1.astype(BF))
    waits([bias_far, *zero_z, *one_y, *two_x])

    @pl.loop(0, 6)
    def _(i):
        which, col = lax.div(i, 3), pl.multiple_of(lax.rem(i, 3) * 256, 256)
        weight = w[which, :, :, :, pl.ds(col, 256)].reshape(D, 256)
        u = nn(rows[0], weight) + bias[which, :, pl.ds(col, 256)]
        phi = 0.5 * (1.0 + lax.erf(u * 0.7071067811865476))
        act[which, :, pl.ds(col, 256)] = (u * phi).astype(BF)
        slope[which, :, pl.ds(col, 256)] = phi + u * (jnp.exp(-0.5 * u * u) * 0.3989422804014327)

    for half in range(2):
        cols = slice(half * 384, (half + 1) * 384)
        part[:, cols] = nt(act[0], w[0, half, :, :, D:].reshape(384, D)) + nt(
            act[1], w[1, half, :, :, D:].reshape(384, D)
        )
    n2, inv2 = normed(y1s[...] + trade_sum(1) + bout[...])
    result[...] = (n2 * g2[...] + s2[...]).astype(BF)
    c = cot[...].astype(F32)
    vec[4:5, :] = total(c * n2)
    vec[5:6, :] = total(c)
    dh2 = normed_back(c, g2[...], n2, inv2)
    dh2s[...] = dh2
    df = dh2.astype(BF)
    vec[1:2, :] = total(df.astype(F32))
    trade_rows(1, df)

    @pl.loop(0, 6)
    def _(i):
        which, col = lax.div(i, 3), pl.multiple_of(lax.rem(i, 3) * 256, 256)
        later = pl.multiple_of(col + D, 256)
        weight = w[which, :, :, :, pl.ds(later, 256)].reshape(D, 256)
        low = (nn(rows[1], weight) * slope[which, :, pl.ds(col, 256)]).astype(BF)
        du[which, :, pl.ds(col, 256)] = low
        vec[pl.ds(6 + which, 1), pl.ds(col, 256)] = total(low.astype(F32))

    for half in range(2):
        cols = slice(half * 384, (half + 1) * 384)
        part[:, cols] = nt(du[0], w[0, half, :, :, :D].reshape(384, D)) + nt(
            du[1], w[1, half, :, :, :D].reshape(384, D)
        )
    dy1 = trade_sum(2) + dh2s[...]
    n1 = n1s[...]
    vec[2:3, :] = total(dy1 * n1)
    vec[3:4, :] = total(dy1)
    dh1 = normed_back(dy1, g1[...], n1, inv1)
    dh1_out[...] = dh1
    da = dh1.astype(BF)
    vec[0:1, :] = total(da.astype(F32))
    trade_rows(2, da)
    to_far = nn(rows[2], wt[1 - yh].reshape(D, QK))
    leave[...] = to_far.astype(BF)
    back = mail.post(leave, g_out.at[pl.ds(yh * 320, 320)], far)
    g_out[pl.ds(yh * 320, 320), :] = nn(rows[2], wt[yh].reshape(D, QK)).astype(BF)
    for which in range(2):
        grads_o[which] = tn(rows[2], o2[which]).astype(BF).reshape(2, 4, 96, QK)

    @pl.loop(0, 6)
    def _(i):
        which, col = lax.div(i, 3), pl.multiple_of(lax.rem(i, 3) * 256, 256)
        later = pl.multiple_of(col + D, 256)
        first = tn(rows[0], du[which, :, pl.ds(col, 256)]).astype(BF)
        grads[which, :, :, :, pl.ds(col, 256)] = first.reshape(2, 4, 96, 256)
        last = tn(rows[1], act[which, :, pl.ds(col, 256)]).astype(BF)
        grads[which, :, :, :, pl.ds(later, 256)] = last.reshape(2, 4, 96, 256)

    back.wait_recv()
    mail.close()


def middle(o, tok, cot, wo, wi, wout, bo, g1, s1, bi, bout, g2, s2):
    shape = jax.ShapeDtypeStruct
    posts = 1 + 15 + 1 + 3 * 8 + 3 + 3 + 1
    line = lambda v: v.reshape(1, D)
    return pl.pallas_call(
        middle_kernel,
        out_shape=(
            shape((ROWS, D), BF),
            shape((ROWS, D), F32),
            shape((CTX_ROWS, QK), BF),
            shape((2, 2, 4, 96, 2 * D), BF),
            shape((2, 2, 4, 96, QK), BF),
            shape((8, D), F32),
        ),
        in_specs=[VM] * 13,
        out_specs=[VM] * 6,
        scratch_shapes=[
            pltpu.VMEM((2, 2, 4, 96, 2 * D), BF),
            pltpu.VMEM((2, 2, 4, 96, QK), BF),
            pltpu.VMEM((2, 320, QK), BF),
            pltpu.VMEM((2, 1, D), F32),
            pltpu.VMEM((320, D), F32),
            pltpu.VMEM((3, ROWS, D), F32),
            pltpu.VMEM((3, 320, D), BF),
            pltpu.VMEM((2, 320, D), BF),
            pltpu.VMEM((2, 320, D), F32),
            pltpu.VMEM((2, 320, D), BF),
            pltpu.VMEM((ROWS, D), F32),
            pltpu.VMEM((ROWS, D), F32),
            pltpu.VMEM((ROWS, D), F32),
            pltpu.VMEM((320, QK), BF),
            pltpu.SemaphoreType.DMA((posts,)),
            pltpu.SemaphoreType.DMA((posts,)),
        ],
        compiler_params=pltpu.CompilerParams(
            collective_id=2, has_side_effects=True, vmem_limit_bytes=56 * MIB
        ),
        name="middle",
    )(o, tok, cot, wo, wi, wout, *map(line, (bo, g1, s1, bi, bout, g2, s2)))


def collect_kernel(
    dq,
    dk_t,
    dv_t,
    dtab,
    g,
    go,
    x_rows,
    ws,
    dh1,
    vec,
    f,
    fo,
    fq,
    ft,
    tg_out,
    vsum,
    r_dk,
    r_dv,
    r0z,
    s0z,
    r0y,
    s0y,
    r0x,
    r1y,
    s1y,
    r1x,
    s1x,
    r1z,
    r2x,
    s2x,
    r2z,
    s2z,
    r2y,
    t0z,
    u0z,
    t0y,
    u0y,
    t0x,
    t1y,
    u1y,
    t1x,
    u1x,
    t1z,
    t2x,
    u2x,
    t2z,
    u2z,
    t2y,
    roz,
    soz,
    roy,
    rox,
    gq,
    rqz,
    sqz,
    rqy,
    rqx,
    tgp,
    r_sib,
    s_far,
    r_far,
    v_own,
    vx,
    vz,
    vy,
    vc,
    send,
    recv,
):
    at = place()
    x, yl, z, yh, core = at["x"], at["yl"], at["z"], at["yh"], at["core"]
    y = yh * 2 + yl
    sib = ident(at, core=1 - core)
    far = ident(at, yh=1 - yh)
    low = ident(at, yl=1 - yl)
    steps = (1, 2, 3)
    xp = [ident(at, x=around(x, k)) for k in steps]
    zp = [ident(at, z=around(z, k)) for k in steps]
    ys = y_peers(at)
    yp = [ident(at, yh=a, yl=b) for a, b in ys]
    greet([sib, *xp, *zp, *yp])
    mail = Mail(send, recv)

    def lanes(base, k):
        return pl.ds(pl.multiple_of(base + around(x, k) * 128, 128), 128)

    def scatter(view, landing, peers):
        return [mail.post(view(k), landing.at[k - 1], peers[k - 1]) for k in steps]

    def gathered(copies, own, landing):
        for copy in copies:
            copy.wait_recv()
        return own.astype(F32) + landing[0].astype(F32) + landing[1].astype(F32) + landing[2].astype(F32)

    def paired(copy, own, landing):
        copy.wait_recv()
        return own.astype(F32) + landing[...].astype(F32)

    def share(slots, me, peers):
        return [mail.post(slots.at[me], slots.at[me], d) for d in peers]

    def summed(copies, slots):
        for copy in copies:
            copy.wait_recv()
        return (
            slots[0].astype(F32) + slots[1].astype(F32) + slots[2].astype(F32) + slots[3].astype(F32)
        )

    def tree_cols(k):
        return pl.ds(pl.multiple_of(around(x, k) * CTX_ROWS, 128), CTX_ROWS)

    c_dk = scatter(lambda k: dk_t.at[:, tree_cols(k)], r_dk, xp)
    c_dv = scatter(lambda k: dv_t.at[:, tree_cols(k)], r_dv, xp)
    c0z = scatter(lambda k: g.at[:, :, around(z, k), :, pl.ds(0, 512)], r0z, zp)
    c1y = scatter(lambda k: g.at[ys[k - 1][0], ys[k - 1][1], :, :, pl.ds(512, 512)], r1y, yp)
    c2x = scatter(lambda k: g.at[:, :, :, :, lanes(1024, k)], r2x, xp)
    d0z = scatter(lambda k: dtab.at[0, :, around(z, k)], t0z, zp)
    d1y = mail.post(dtab.at[1, 1 - yl], t1y, low)
    d2x = scatter(lambda k: dtab.at[2, :, :, :, lanes(0, k)], t2x, xp)
    coz = scatter(lambda k: go.at[:, :, around(z, k)], roz, zp)

    def project_grad(j, values):
        gq[j] = tn(x_rows[...], values).astype(BF).reshape(2, 4, 96, QK)
        return scatter(lambda k: gq.at[j, :, around(z, k)], rqz.at[j], zp)

    def weight(j):
        return ws[:, j].reshape(D, QK)

    q_low = dq[...]
    cqz = [project_grad(0, q_low)]
    tgp[...] = nt(q_low, weight(0))
    v_own[...] = jnp.zeros_like(v_own)
    v_own[0:8, :] = vec[...]
    v_own[pl.ds(8 + yh, 1), 0:QK] = total(q_low.astype(F32))
    k_low = gathered(c_dk, dk_t[:, tree_cols(0)], r_dk).T.astype(BF)
    v_low = gathered(c_dv, dv_t[:, tree_cols(0)], r_dv).T.astype(BF)
    v_own[pl.ds(10 + yh, 1), 0:QK] = total(v_low.astype(F32))
    vx[x] = v_own[...]
    c_vx = share(vx, x, xp)
    tgp[...] += nt(k_low, weight(1)) + nt(v_low, weight(2))

    def block(a, b):
        return pl.ds((a * 2 + b) * ROWS, ROWS)

    c_sib = [mail.post(tgp.at[block(a, 1 - core)], r_sib.at[a], sib) for a in range(2)]
    cqz.append(project_grad(1, k_low))
    cqz.append(project_grad(2, v_low))
    for copy in c_sib:
        copy.wait_recv()
    s_far[...] = (tgp[block(1 - yh, core), :] + r_sib[1 - yh]).astype(BF)
    c_far = mail.post(s_far, r_far, far)

    u0z[...] = gathered(d0z, dtab[0, :, z], t0z).astype(BF)
    d0y = mail.post(u0z.at[1 - yl], t0y, low)
    u1y[...] = paired(d1y, dtab[1, yl], t1y).astype(BF)
    d1x = scatter(lambda k: u1y.at[:, :, lanes(0, k)], t1x, xp)
    soz[...] = gathered(coz, go[:, :, z], roz).astype(BF)
    coy = scatter(lambda k: soz.at[ys[k - 1][0], ys[k - 1][1]], roy, yp)
    s0z[...] = gathered(c0z, g[:, :, z, :, 0:512], r0z).astype(BF)
    c0y = scatter(lambda k: s0z.at[ys[k - 1][0], ys[k - 1][1]], r0y, yp)
    s1y[...] = gathered(c1y, g[yh, yl, :, :, 512:1024], r1y).astype(BF)
    c1x = scatter(lambda k: s1y.at[:, :, lanes(0, k)], r1x, xp)
    s2x[...] = gathered(c2x, g[:, :, :, :, lanes(1024, 0)], r2x).astype(BF)
    c2z = scatter(lambda k: s2x.at[:, :, around(z, k)], r2z, zp)
    u2x[...] = gathered(d2x, dtab[2, :, :, :, lanes(0, 0)], t2x).astype(BF)
    d2z = scatter(lambda k: u2x.at[:, around(z, k)], t2z, zp)
    cqy = []
    for j in range(3):
        sqz[j] = gathered(cqz[j], gq[j, :, z], rqz.at[j]).astype(BF)
        cqy.append(mail.post(sqz.at[j, 1 - yl], rqy.at[j], low))
    vz[z] = summed(c_vx, vx)
    c_vz = share(vz, z, zp)

    c_far.wait_recv()
    tg_out[...] = tgp[block(yh, core), :] + r_sib[yh] + r_far[...].astype(F32) + dh1[...]
    u0y[...] = paired(d0y, u0z[yl], t0y).astype(BF)
    d0x = scatter(lambda k: u0y.at[:, lanes(0, k)], t0x, xp)
    rox[x] = gathered(coy, soz[yh, yl], roy).astype(BF)
    cox = share(rox, x, xp)
    s0y[...] = gathered(c0y, s0z[yh, yl], r0y).astype(BF)
    c0x = scatter(lambda k: s0y.at[:, lanes(0, k)], r0x, xp)
    s1x[...] = gathered(c1x, s1y[:, :, lanes(0, 0)], r1x).astype(BF)
    c1z = scatter(lambda k: s1x.at[around(z, k)], r1z, zp)
    s2z[...] = gathered(c2z, s2x[:, :, z], r2z).astype(BF)
    c2y = scatter(lambda k: s2z.at[ys[k - 1][0], ys[k - 1][1]], r2y, yp)
    u1x[...] = gathered(d1x, u1y[:, :, lanes(0, 0)], t1x).astype(BF)
    d1z = scatter(lambda k: u1x.at[around(z, k)], t1z, zp)
    u2z[...] = gathered(d2z, u2x[:, z], t2z).astype(BF)
    d2y = mail.post(u2z.at[1 - yl], t2y, low)
    cqx = []
    for j in range(3):
        rqx[j, x] = paired(cqy[j], sqz[j, yl], rqy.at[j]).astype(BF)
        cqx.append(share(rqx.at[j], x, xp))
    vy[y] = summed(c_vz, vz)
    c_vy = share(vy, y, yp)

    late = []

    def settle(ref, base, values):
        ref[:, lanes(base, 0)] = values.astype(BF)
        view = ref.at[:, lanes(base, 0)]
        late.extend(mail.post(view, view, d) for d in xp)

    settle(f, 0, gathered(c0x, s0y[:, lanes(0, 0)], r0x))
    settle(f, 512, gathered(c1z, s1x[z], r1z))
    settle(f, 1024, gathered(c2y, s2z[yh, yl], r2y))
    settle(ft.at[0], 0, gathered(d0x, u0y[:, lanes(0, 0)], t0x))
    settle(ft.at[1], 0, gathered(d1z, u1x[z], t1z))
    settle(ft.at[2], 0, paired(d2y, u2z[yl], t2y))
    vc[0] = summed(c_vy, vy)
    c_vc = mail.post(vc.at[0], vc.at[1], sib)
    fo[...] = summed(cox, rox)
    for j in range(3):
        fq[j] = summed(cqx[j], rqx.at[j])
    c_vc.wait_recv()
    vsum[...] = vc[0]
    vsum[0:6, :] = vc[0, 0:6, :] + vc[1, 0:6, :]
    for copy in late:
        copy.wait_recv()
    mail.close()


def collect(dq, dk_t, dv_t, dtab, g, go, x_rows, ws, dh1, vec):
    shape = jax.ShapeDtypeStruct
    posts = 6 + 9 + 3 + 1 + 3 + 3 + 9 + 3 + 2 + 1 + 1 + 3 + 3 + 3 + 3 + 3 + 3 + 3 + 3 + 3
    posts += 3 + 3 + 3 + 3 + 3 + 1 + 9 + 3 + 18 + 1 + 8
    buf = lambda *dims: pltpu.VMEM(dims, BF)
    buf32 = lambda *dims: pltpu.VMEM(dims, F32)
    return pl.pallas_call(
        collect_kernel,
        out_shape=(
            shape((96, 2 * D), BF),
            shape((96, QK), F32),
            shape((3, 96, QK), F32),
            shape((HEADS_DEV, 64, DEPTHS), BF),
            shape((ROWS, D), F32),
            shape((16, D), F32),
        ),
        in_specs=[VM] * 10,
        out_specs=[VM] * 6,
        scratch_shapes=[
            buf(3, QK, CTX_ROWS),
            buf(3, QK, CTX_ROWS),
            buf(3, 2, 2, 96, 512),
            buf(2, 2, 96, 512),
            buf(3, 96, 512),
            buf(96, 512),
            buf(3, 96, 128),
            buf(3, 4, 96, 512),
            buf(4, 96, 512),
            buf(3, 4, 96, 128),
            buf(4, 96, 128),
            buf(3, 96, 128),
            buf(3, 2, 2, 4, 96, 128),
            buf(2, 2, 4, 96, 128),
            buf(3, 2, 2, 96, 128),
            buf(2, 2, 96, 128),
            buf(3, 96, 128),
            buf(3, 2, 64, 512),
            buf(2, 64, 512),
            buf(64, 512),
            buf(64, 512),
            buf(3, 64, 128),
            buf(4, 64, 512),
            buf(4, 64, 512),
            buf(3, 4, 64, 128),
            buf(4, 64, 128),
            buf(3, 64, 128),
            buf(3, 2, 4, 64, 128),
            buf(2, 4, 64, 128),
            buf(3, 2, 64, 128),
            buf(2, 64, 128),
            buf(64, 128),
            buf(3, 2, 2, 96, QK),
            buf(2, 2, 96, QK),
            buf(3, 96, QK),
            buf(4, 96, QK),
            buf(3, 2, 4, 96, QK),
            buf(3, 3, 2, 96, QK),
            buf(3, 2, 96, QK),
            buf(3, 96, QK),
            buf(3, 4, 96, QK),
            buf32(CTX_ROWS, D),
            buf32(2, ROWS, D),
            buf(ROWS, D),
            buf(ROWS, D),
            buf32(16, D),
            buf32(4, 16, D),
            buf32(4, 16, D),
            buf32(4, 16, D),
            buf32(2, 16, D),
            pltpu.SemaphoreType.DMA((posts,)),
            pltpu.SemaphoreType.DMA((posts,)),
        ],
        compiler_params=pltpu.CompilerParams(
            collective_id=3, has_side_effects=True, vmem_limit_bytes=56 * MIB
        ),
        name="collect",
    )(dq, dk_t, dv_t, dtab, g, go, x_rows, ws, dh1, vec)


def finish_kernel(
    f,
    fo,
    fq,
    ft,
    tg,
    vsum,
    res,
    logits,
    noise,
    res_out,
    tg_out,
    gwq,
    gwk,
    gwv,
    gwo,
    gwi,
    gwout,
    mask,
    lines,
    narrow,
):
    res_out[...] = res[...]
    tg_out[...] = tg[...]
    gwq[...], gwk[...], gwv[...] = fq[0], fq[1], fq[2]
    gwo[...] = fo[...].T
    gwi[...] = f[:, :D].astype(F32)
    gwout[...] = f[:, D:].astype(F32).T
    mask[...] = ft[...].astype(F32) * jax.nn.sigmoid(-(logits[...] + noise[...]))
    yh = lax.div(lax.axis_index("tp"), 2)
    lines[...] = vsum[...]
    lines[6:7, :] = vsum[pl.ds(6 + yh, 1), :]
    narrow[0:1, :] = vsum[pl.ds(8 + yh, 1), 0:QK]
    narrow[1:2, :] = vsum[pl.ds(10 + yh, 1), 0:QK]


def finish(f, fo, fq, ft, tg, vsum, res, logits, noise):
    shape = jax.ShapeDtypeStruct
    return pl.pallas_call(
        finish_kernel,
        out_shape=(
            shape((ROWS, D), BF),
            shape((ROWS, D), F32),
            shape((96, QK), F32),
            shape((96, QK), F32),
            shape((96, QK), F32),
            shape((QK, 96), F32),
            shape((96, D), F32),
            shape((D, 96), F32),
            shape((HEADS_DEV, 64, DEPTHS), F32),
            shape((16, D), F32),
            shape((8, QK), F32),
        ),
        in_specs=[VM] * 9,
        out_specs=[VM] * 11,
        compiler_params=pltpu.CompilerParams(vmem_limit_bytes=56 * MIB),
        name="finish",
    )(f, fo, fq, ft, tg, vsum, res, logits, noise)


def shards(
    tokens,
    parents,
    query_weight,
    query_bias,
    key_weight,
    value_weight,
    value_bias,
    output_weight,
    output_bias,
    first_gain,
    first_shift,
    inner_weight,
    inner_bias,
    outer_weight,
    outer_bias,
    second_gain,
    second_shift,
    mask_logits,
    mask_noise,
    cotangent,
):
    q, k, v, rows, table, ws = project(
        tokens,
        query_weight,
        key_weight,
        value_weight,
        query_bias,
        value_bias,
        mask_logits,
        mask_noise,
    )
    table = table.reshape(HEADS_DEV, DEPTHS, DEPTHS)
    o, soft = attend(parents, q, k, v, table)
    result, dh1, dout, grads, grads_o, vec = middle(
        o,
        tokens,
        cotangent,
        output_weight,
        inner_weight,
        outer_weight,
        output_bias,
        first_gain,
        first_shift,
        inner_bias,
        outer_bias,
        second_gain,
        second_shift,
    )
    dq, dk_t, dv_t, dtab = attend_back(parents, q, k, v, o, dout, soft)
    dtab = dtab.reshape(HEADS_DEV, 2, 4, 64, DEPTHS)
    out = collect(dq, dk_t, dv_t, dtab, grads, grads_o, rows, ws, dh1, vec)
    result, tg, gwq, gwk, gwv, gwo, gwi, gwout, mask, lines, narrow = finish(
        *out, result, mask_logits, mask_noise
    )
    return (
        result,
        tg,
        gwq,
        narrow[0],
        gwk,
        gwv,
        narrow[1],
        gwo,
        lines[0],
        lines[2],
        lines[3],
        gwi,
        lines[6],
        gwout,
        lines[1],
        lines[4],
        lines[5],
        mask,
    )


def solution(mesh):
    in_specs = (
        P(("shard", "ctx", "tp"), None),
        P("shard", None),
        P("shard", "tp"),
        P("tp"),
        P("shard", "tp"),
        P("shard", "tp"),
        P("tp"),
        P("tp", "shard"),
        P(),
        P(),
        P(),
        P("shard", "tp"),
        P("tp"),
        P("tp", "shard"),
        P(),
        P(),
        P(),
        P("tp", "shard", None),
        P("tp", "shard", None),
        P(("shard", "ctx", "tp"), None),
    )
    out_specs = (
        P(("shard", "ctx", "tp"), None),
        P(("shard", "ctx", "tp"), None),
        P("shard", "tp"),
        P("tp"),
        P("shard", "tp"),
        P("shard", "tp"),
        P("tp"),
        P("tp", "shard"),
        P(),
        P(),
        P(),
        P("shard", "tp"),
        P("tp"),
        P("tp", "shard"),
        P(),
        P(),
        P(),
        P("tp", "shard", None),
    )
    return jax.shard_map(shards, mesh=mesh, in_specs=in_specs, out_specs=out_specs, check_vma=False)
```

time: 818 us -> 245 us (0.30); the launches traced: 803 us -> 243 us
  waiting for transfers between devices: 376 us -> 0 us
  blocking collectives: 271 us -> 0 us
  Pallas kernels: 73 us -> 227 us
  matrix products: 36.3 us -> 0 us
  other arithmetic: 19.5 us -> 0 us
  between operations: 15.9 us -> 0.69 us
    reduce_scatter x10 -> x0, waiting for transfers between devices: 307 us -> none  [the longest x4 114 us: sum_rows(): return lax.psum_scatter(values, 'tp', scatter_dimension=0, tiled=True)]
    pallas_call x0 -> x3, Pallas kernels: none -> 155 us  [the longest x1 82 us: collect(): pl.pallas_call(collect_kernel, out_shape=(shape((96, 2 * D), BF), shape((...]
    psum x2 -> x0, blocking collectives: 138 us -> none  [the longest x1 71.1 us: shards(): lax.psum((output_bias_grad, outer_bias_grad, first_gain_grad, first_shift...]
    all_gather x7 -> x0, blocking collectives: 133 us -> none  [the longest x3 35.6 us: gather_rows(): return lax.all_gather(values, 'tp', axis=0, tiled=True)]
    unnamed x20 -> x0, waiting for transfers between devices: 41.7 us -> none
    dot_general x15 -> x0, matrix products: 36.3 us -> none  [the longest x1 7.54 us: shards(): jnp.dot(first_rows, weight_set[3], preferred_element_type=jnp.float32)]
    all_gather x2 -> x0, waiting for transfers between devices: 27.1 us -> none  [the longest x1 27.1 us: shards(): lax.all_gather(outer_weight, 'shard', axis=1, tiled=True)]
    convert_element_type x7 -> x0, other arithmetic: 9.22 us -> none  [the longest x1 1.64 us: shards(): lax.psum(shard_part[3].astype(jnp.bfloat16), 'ctx').astype(jnp.float32)]
  transfers between devices with their start and end apart: 17 -> 0, of which waited for: 11 -> 0; matrix products, arithmetic and copies ran while one was open for 5% -> 0% of each run, Pallas kernels for 0% -> 0%
where the time goes in v2:
time: 245 us; the launch traced here: 243 us
  Pallas kernels  227 us (93%)
  local copies, waits for them, and re-layouts  15.5 us (6%)
    pallas_call x1, Pallas kernels, collect(): pl.pallas_call(collect_kernel, out_shape=(shape((96, 2 * D), BF), shape((...  82 us
    pallas_call x1, Pallas kernels, middle(): pl.pallas_call(middle_kernel, out_shape=(shape((ROWS, D), BF), shape((ROW...  70 us
    pallas_call x1, Pallas kernels, project(): pl.pallas_call(project_kernel, out_shape=(shape((CTX_ROWS, QKW), BF), sha...  44.8 us
    pallas_call x1, Pallas kernels, attend_back(): pl.pallas_call(attend_back_kernel, grid=(5,), out_shape=(shape((CTX_ROWS,...  13.4 us
    pallas_call x1, Pallas kernels, attend(): pl.pallas_call(attend_kernel, grid=(5,), out_shape=(shape((CTX_ROWS, QK),...  13.3 us
    reshape x7, local copies, waits for them, and re-layouts, middle(): line = lambda v: v.reshape(1, D)  8.87 us

profile of v2, /device:TPU:1, one launch (start us, length us, event | category | flops | bytes accessed | tf_op | source)
XLA Modules:
  0.0 242.8 jit_solution(4532232137853863449)
XLA Ops:
  0.7 1.3 reshape.72.bo
  1.9 1.3 reshape.73.g1
  3.2 1.3 reshape.74.s1
  4.5 1.3 reshape.75.bi
  5.7 1.3 reshape.76.bout
  7.0 1.3 reshape.77.g2
  8.3 1.3 reshape.78.s2
  9.5 1.7 copy.38.wout
  11.2 44.8 %project.1 = (bf16[640,384]{1,0:T(8,128)(2,1)}, bf16[2560,384]{1,0:T(8,128)(2,1)}, bf16[2560,384]{1,0:T(8,128)(2,1)}, bf16[640,768]{1,0:T(8,128)(2,1)}, bf16[3,8...) custom-call(bf16[160,768]{1,0:T(8,128)(2,1)} %tok.3, bf16[96,192]{1,0:T(8,128)(2,1)} %wq.1, bf16[96,192]{1,0:T(8,128)(2,1)} %wk.1, ...), custom_call_target="tpu_custom_call" | custom-call | tf_op jit(solution)/shard_map/project/pallas_call | solution.py:199
  56.0 13.3 %attend.1 = (bf16[640,192]{1,0:T(8,128)(2,1)}, bf16[5,3,128,1280]{3,2,1,0:T(8,128)(2,1)}) custom-call(s32[1,20]{1,0:T(1,128)} %parents.3, bf16[640,384]{1,0:T(8,128)(2,1)} %get-tuple-element.53.q, bf16[2560,384]{1,0:T(8,128)(2,1)} %get-tuple-element.54.k, bf16[2560,384]{1,0:T(8,128)(2,1)} %get-tuple-element.55.v, bf16[3,512,512]{2,1,0:T(8,128)(2,1)} %bitcast.7), custom_call_target="tpu_custom_call" | custom-call | flops 1258291200 | bytes 12582912 | tf_op jit(solution)/shard_map/attend/pallas_call | solution.py:277
  69.3 70.0 %middle.1 = (bf16[160,768]{1,0:T(8,128)(2,1)}, f32[160,768]{1,0:T(8,128)}, bf16[640,192]{1,0:T(8,128)(2,1)}, bf16[2,2,4,96,1536]{4,3,2,1,0:T(8,128)(2,1)}, bf16[...) custom-call(bf16[640,192]{1,0:T(8,128)(2,1)} %get-tuple-element.57.o, bf16[160,768]{1,0:T(8,128)(2,1)} %tok.3, ...), custom_call_target="tpu_custom_call" | custom-call | tf_op jit(solution)/shard_map/middle/pallas_call | solution.py:613
  139.3 13.4 %attend_back.1 = (bf16[640,192]{1,0:T(8,128)(2,1)}, bf16[192,2560]{1,0:T(8,128)(2,1)}, bf16[192,2560]{1,0:T(8,128)(2,1)}, bf16[3,512,512]{2,1,0:T(8,128)(2,1)}) custom-call(s32[1,20]{1,0:T(1,128)} %parents.3, bf16[640,384]{1,0:T(8,128)(2,1)} %get-tuple-element.53.q, bf16[2560,384]{1,0:T(8,128)(2,1)} %get-tuple-element.54.k, ...), custom_call_target="tpu_custom_call" | custom-call | flops 3145728000 | bytes 20971520 | tf_op jit(solution)/shard_map/attend_back/pallas_call | solution.py:362
  152.8 82.0 %collect.1 = (bf16[96,1536]{1,0:T(8,128)(2,1)}, f32[96,192]{1,0:T(8,128)}, f32[3,96,192]{2,1,0:T(8,128)}, bf16[3,64,512]{2,1,0:T(8,128)(2,1)}, f32[160,768]{1,0:T(8,128)}, /*index=5*/f32[16,768]{1,0:T(8,128)}) custom-call(bf16[640,192]{1,0:T(8,128)(2,1)} %get-tuple-element.60.dq, bf16[192,2560]{1,0:T(8,128)(2,1)} %get-tuple-element.61.dk_t, ...), custom_call_target="tpu_custom_call" | custom-call | tf_op jit(solution)/shard_map/collect/pallas_call | solution.py:879
  234.7 3.2 %finish.1 = (bf16[160,768]{1,0:T(8,128)(2,1)}, f32[160,768]{1,0:T(8,128)}, f32[96,192]{1,0:T(8,128)}, f32[96,192]{1,0:T(8,128)}, f32[96,192]{1,0:T(8,128)}, /*in...) custom-call(bf16[96,1536]{1,0:T(8,128)(2,1)} %get-tuple-element.70.f, ...), custom_call_target="tpu_custom_call" | custom-call | tf_op jit(solution)/shard_map/finish/pallas_call | solution.py:990
  237.9 1.3 fusion
  239.2 1.7 slice_reduce_fusion
  240.9 1.9 copy.39

commit v3 on v0

v3 whole, which is shorter than its diff:
```python
import jax
import jax.numpy as jnp
from jax import lax
from jax.experimental import pallas as pl
from jax.experimental.pallas import tpu as pltpu
from jax.sharding import PartitionSpec as P

MESH = pl.DeviceIdType.MESH
BF = jnp.bfloat16
F32 = jnp.float32
HEADS_DEV = 3
HEAD_DIM = 64
WIDE = 128
SEG = 128
SEGS = 20
OWN_SEGS = 5
PATH = 10
KEYS = PATH * SEG
D = 768
QK = 192
QKP = 256
QKW = 384
ROWS = 160
PAIR = 320
CTX_ROWS = 640
TREE = 2560
DEPTHS = 512
MIB = 2**20
SCALE = HEAD_DIM**-0.5
STEPS = (1, 2, 3)


def place():
    shard = lax.axis_index("shard")
    tp = lax.axis_index("tp")
    return {
        "x": lax.axis_index("ctx"),
        "yl": lax.div(shard, 4),
        "z": lax.rem(shard, 4),
        "yh": lax.div(tp, 2),
        "core": lax.rem(tp, 2),
    }


def ident(at, **moved):
    to = {**at, **moved}
    return {"shard": to["yl"] * 4 + to["z"], "ctx": to["x"], "tp": to["yh"] * 2 + to["core"]}


def around(value, step):
    return lax.rem(value + step, 4)


def greet(devices):
    barrier = pltpu.get_barrier_semaphore()
    for device in devices:
        pl.semaphore_signal(barrier, inc=1, device_id=device, device_id_type=MESH)
    pl.semaphore_wait(barrier, len(devices))


class Mail:
    def __init__(self, send, recv):
        self.send, self.recv, self.used, self.sent = send, recv, 0, []

    def post(self, src, dst, device):
        copy = pltpu.make_async_remote_copy(
            src_ref=src,
            dst_ref=dst,
            send_sem=self.send.at[self.used],
            recv_sem=self.recv.at[self.used],
            device_id=device,
            device_id_type=MESH,
        )
        self.used += 1
        copy.start()
        self.sent.append(copy)
        return copy

    def same(self, ref, devices):
        return [self.post(ref, ref, device) for device in devices]

    def spread(self, view, landing, devices):
        return [self.post(view(k), landing.at[k - 1], devices[k - 1]) for k in STEPS]

    def ring(self, view, ahead, behind):
        return [self.post(view(0), view(0), ahead), self.post(view(0), view(0), behind)]

    def ring_on(self, view, first, ahead, behind):
        arrived(first[:1])
        onward = [self.post(view(3, 0), view(3, 0), ahead)]
        arrived(first[1:])
        return onward + [self.post(view(1, 1), view(1, 1), behind)]

    def fold(self, view, landing, ahead, behind):
        return [
            self.post(view(2, 0), landing.at[0], ahead),
            self.post(view(2, 1), landing.at[1], behind),
            self.post(view(1, 1), landing.at[3], ahead),
            self.post(view(3, 0), landing.at[4], behind),
        ]

    def fold_on(self, view, landing, first, ahead, behind):
        out = first[2:]
        for half, k, slot, device in ((0, 1, 2, ahead), (1, 3, 5, behind)):
            arrived(first[half : half + 1])
            term = view(k, half)
            term[...] = (term[...].astype(F32) + landing[half].astype(F32)).astype(BF)
            out.append(self.post(term, landing.at[slot], device))
        return out

    def done(self, copy):
        copy.wait()
        self.sent = [kept for kept in self.sent if kept is not copy]

    def flush(self):
        for copy in self.sent:
            copy.wait_send()
        self.sent = []


def arrived(copies):
    for copy in copies:
        copy.wait_recv()


def nn(a, b):
    return jnp.dot(a, b, preferred_element_type=F32)


def nt(a, b):
    return lax.dot_general(a, b, (((1,), (1,)), ((), ())), preferred_element_type=F32)


def tn(a, b):
    return lax.dot_general(a, b, (((0,), (0,)), ((), ())), preferred_element_type=F32)


def spread_heads(kind=BF):
    rows = lax.broadcasted_iota(jnp.int32, (QK, QKW), 0)
    cols = lax.broadcasted_iota(jnp.int32, (QK, QKW), 1)
    head, lane = cols // WIDE, cols % WIDE
    return ((head * HEAD_DIM + lane == rows) & (lane < HEAD_DIM)).astype(kind)


def unit(rows_count, cols_count):
    rows = lax.broadcasted_iota(jnp.int32, (rows_count, cols_count), 0)
    cols = lax.broadcasted_iota(jnp.int32, (rows_count, cols_count), 1)
    return (rows == cols).astype(BF)


def line(ref):
    return jnp.concatenate([ref[i : i + 1, :] for i in range(6)], axis=1)


def normed(values):
    centre = jnp.mean(values, axis=1, keepdims=True)
    off = values - centre
    inverse = lax.rsqrt(jnp.mean(off * off, axis=1, keepdims=True) + 1e-5)
    return off * inverse, inverse


def normed_back(grad, gain, n, inverse):
    e = grad * gain
    return inverse * (e - jnp.mean(e, axis=1, keepdims=True) - n * jnp.mean(e * n, axis=1, keepdims=True))


def total(values):
    return jnp.sum(values, axis=0, keepdims=True)


def added(own, landing, count=3):
    out = own.astype(F32)
    for i in range(count):
        out = out + landing[i].astype(F32)
    return out


def folded(view, landing, half):
    near = landing[2 + half].astype(F32) + landing[4 + half].astype(F32)
    return view(0, half)[...].astype(F32) + near


def slots_total(slots):
    return slots[0].astype(F32) + slots[1].astype(F32) + slots[2].astype(F32) + slots[3].astype(F32)


INPUTS = (
    "parents",
    "tok",
    "cot",
    "wq",
    "wk",
    "wv",
    "qb",
    "vb",
    "logits",
    "noise",
    "wo",
    "wi",
    "wout_t",
    "bo",
    "g1",
    "s1",
    "bi",
    "bout",
    "g2",
    "s2",
)
OUTPUTS = {
    "res": ((ROWS, D), BF),
    "tg": ((ROWS, D), F32),
    "f": ((96, 2 * D), BF),
    "fo": ((96, QKP), F32),
    "fq": ((3, 96, QKP), F32),
    "ft": ((HEADS_DEV, 64, DEPTHS), BF),
    "vsum": ((16, D), F32),
}
SCRATCH = {
    "cots": ((ROWS, D), BF),
    "lines": ((7, 6, 128), F32),
    "qvb": ((2, 1, QK), F32),
    "wos": ((QK, 96), BF),
    "masks": ((2, HEADS_DEV, 64, DEPTHS), F32),
    "xs": ((4, 4, ROWS, D), BF),
    "ws": ((8, 3, 96, QK), BF),
    "wide": ((2, 4, 96, 3 * QKW), BF),
    "q": ((CTX_ROWS, QKW), BF),
    "k": ((SEGS, SEG, QKW), BF),
    "v": ((SEGS, SEG, QKW), BF),
    "tab": ((HEADS_DEV, 2, 4, 64, DEPTHS), BF),
    "kp": ((KEYS, QKW), BF),
    "vp": ((KEYS, QKW), BF),
    "p": ((OWN_SEGS, HEADS_DEV, SEG, KEYS), BF),
    "o_wide": ((CTX_ROWS, QKW), BF),
    "o": ((CTX_ROWS, QK), BF),
    "w": ((2, 2, 4, 96, 2 * D), BF),
    "wt": ((2, 2, 4, 96, QKP), BF),
    "o2": ((2, PAIR, QK), BF),
    "bias": ((2, 1, D), F32),
    "part": ((PAIR, D), F32),
    "got": ((3, ROWS, D), F32),
    "rows": ((3, PAIR, D), BF),
    "act": ((2, PAIR, D), BF),
    "slope": ((CTX_ROWS, D), F32),
    "du": ((2, PAIR, D), BF),
    "y1s": ((ROWS, D), F32),
    "n1s": ((ROWS, D), F32),
    "dh2s": ((ROWS, D), F32),
    "dh1s": ((ROWS, D), F32),
    "dout": ((CTX_ROWS, QK), BF),
    "parts": ((2, PATH, HEAD_DIM, SEG), F32),
    "dtab": ((HEADS_DEV, DEPTHS, DEPTHS), F32),
    "dq_wide": ((CTX_ROWS, QKW), BF),
    "tgp": ((CTX_ROWS, D), F32),
    "r_dkv": ((6, HEADS_DEV, 64, CTX_ROWS), BF),
    "r0z": ((6, 1, 2, 96, 512), BF),
    "s0z": ((2, 2, 96, 512), BF),
    "r0y": ((3, 96, 512), BF),
    "s0y": ((96, 512), BF),
    "r0x": ((3, 96, 128), BF),
    "r1y": ((6, 2, 96, 512), BF),
    "s1y": ((4, 96, 512), BF),
    "r1x": ((3, 4, 96, 128), BF),
    "s1x": ((4, 96, 128), BF),
    "r1z": ((3, 96, 128), BF),
    "r2x": ((6, 1, 2, 4, 96, 128), BF),
    "s2x": ((2, 2, 4, 96, 128), BF),
    "r2z": ((3, 2, 2, 96, 128), BF),
    "s2z": ((2, 2, 96, 128), BF),
    "r2y": ((3, 96, 128), BF),
    "t0z": ((3, 2, 64, 512), BF),
    "u0z": ((2, 64, 512), BF),
    "t0y": ((64, 512), BF),
    "u0y": ((64, 512), BF),
    "t0x": ((3, 64, 128), BF),
    "t1y": ((4, 64, 512), BF),
    "u1y": ((4, 64, 512), BF),
    "t1x": ((3, 4, 64, 128), BF),
    "u1x": ((4, 64, 128), BF),
    "t1z": ((3, 64, 128), BF),
    "t2y": ((4, 64, 512), BF),
    "u2y": ((4, 64, 512), BF),
    "t2z": ((3, 64, 512), BF),
    "u2z": ((64, 512), BF),
    "t2x": ((3, 64, 128), BF),
    "roz": ((3, 2, 2, 96, QKP), BF),
    "soz": ((2, 2, 96, QKP), BF),
    "roy": ((3, 96, QKP), BF),
    "rox": ((4, 96, QKP), BF),
    "rqz": ((3, 3, 2, 96, QKP), BF),
    "sqz": ((3, 2, 96, QKP), BF),
    "rqy": ((3, 96, QKP), BF),
    "rqx": ((3, 4, 96, QKP), BF),
    "r_far": ((ROWS, D), BF),
    "v_own": ((16, D), F32),
    "vx": ((4, 16, D), F32),
    "vz": ((4, 16, D), F32),
    "vy": ((4, 16, D), F32),
    "vc": ((2, 16, D), F32),
}
POSTS = 260


class Names:
    pass


def layer_kernel(*refs):
    r = Names()
    names = [*INPUTS, *OUTPUTS, *SCRATCH, "trail", "depths", "fetch", "send", "recv"]
    for name, ref in zip(names, refs, strict=True):
        setattr(r, name, ref)
    at = place()
    x, yl, z, yh, core = at["x"], at["yl"], at["z"], at["yh"], at["core"]
    shard, tp, y = yl * 4 + z, yh * 2 + core, yh * 2 + yl
    sib = ident(at, core=1 - core)
    far = ident(at, yh=1 - yh)
    low = ident(at, yl=1 - yl)
    xp = [ident(at, x=around(x, k)) for k in STEPS]
    zp = [ident(at, z=around(z, k)) for k in STEPS]
    ys = [(lax.div(around(y, k), 2), lax.rem(around(y, k), 2)) for k in (0, 1, 2, 3)]
    yp = [ident(at, yh=a, yl=b) for a, b in ys[1:]]
    x_ring, y_ring, z_ring = (xp[0], xp[2]), (yp[0], yp[2]), (zp[0], zp[2])
    mail = Mail(r.send, r.recv)

    def lanes(base, k):
        return pl.ds(pl.multiple_of(base + around(x, k) * 128, 128), 128)

    def halves(size, half):
        return pl.ds(0, size) if half is None else pl.ds(half * size // 2, size // 2)

    def tok_own(k, half=None):
        return r.xs.at[around(x, k), tp, halves(ROWS, half)]

    def tok_far(k, half=None):
        return r.xs.at[around(x, k), (1 - yh) * 2 + core, halves(ROWS, half)]

    def ws_of(side):
        return lambda k, half=None: r.ws.at[side * 4 + around(z, k), :, halves(96, half)]

    def tab_of(side):
        return lambda k, half=None: r.tab.at[halves(2, half), side, around(z, k)]

    def tab_last(k, half=None):
        return r.tab.at[2, yl, around(z, k), halves(64, half)]

    def w0(k, half=None):
        return r.w.at[halves(2, half), :, around(z, k), :, pl.ds(0, 512)]

    def w1(k, half=None):
        return r.w.at[ys[k][0], ys[k][1], halves(4, half), :, pl.ds(512, 512)]

    def w2(k, half=None):
        return r.w.at[halves(2, half), :, :, :, lanes(1024, k)]

    def bring(n, src, dst):
        copy = pltpu.make_async_copy(src, dst, r.fetch.at[n])
        copy.start()
        return copy

    def brought(copies):
        for copy in copies:
            copy.wait()

    get_tok = [bring(0, r.tok, tok_own(0))]
    get_ws = [bring(1 + j, w, r.ws.at[shard, j]) for j, w in enumerate((r.wq, r.wk, r.wv))]
    get_masks = [bring(4 + j, m, r.masks.at[j]) for j, m in enumerate((r.logits, r.noise))]
    get_w = [
        bring(6, r.wout_t, r.w.at[yh, yl, z, :, pl.ds(0, D)]),
        bring(7, r.wi, r.w.at[yh, yl, z, :, pl.ds(D, D)]),
        bring(8, r.wo, r.wos),
    ]
    vectors = (r.bo, r.g1, r.s1, r.bi, r.bout, r.g2, r.s2)
    get_rest = [bring(9 + j, v, r.lines.at[j]) for j, v in enumerate(vectors)]
    get_rest += [bring(16, r.cot, r.cots), bring(17, r.qb, r.qvb.at[0]), bring(18, r.vb, r.qvb.at[1])]
    bo, g1, s1, bi, bout, g2, s2 = [r.lines.at[j] for j in range(7)]
    greet([sib, *xp, *zp, *yp])
    brought(get_tok)
    first_far = mail.same(tok_own(0), [far])
    own_x = mail.ring(tok_own, *x_ring)
    to_sib = mail.same(tok_own(0), [sib])
    brought(get_ws)
    own_low = mail.same(r.ws.at[shard], [low])
    own_z = mail.ring(ws_of(yl), *z_ring)
    brought(get_masks)
    r.tab[:, yl, z] = jax.nn.log_sigmoid(r.masks[0] + r.masks[1]).astype(BF)
    tab_low = mail.same(tab_of(yl)(0), [low])
    to_low = mail.same(tab_last(0), [low])
    tab_z = mail.ring(tab_of(yl), *z_ring)
    last_z = mail.ring(tab_last, *z_ring)
    brought(get_w + get_rest)
    r.wt[yh, yl, z] = jnp.concatenate(
        [nt(unit(96, 96), r.wos[...]).astype(BF), jnp.zeros((96, QKP - QK), BF)], axis=1
    )
    r.bias[yh] = line(bi)
    one_z = mail.same(r.w.at[yh, yl, z, :, lanes(512, 0)], zp)
    o_z = mail.same(r.wt.at[yh, yl, z], zp)
    two_y = mail.same(r.w.at[yh, yl, z, :, lanes(1024, 0)], yp)
    zero_y = mail.same(r.w.at[yh, yl, z, :, pl.ds(0, 512)], yp)
    bias_far = mail.same(r.bias.at[yh], [far])
    arrived(first_far)
    far_x = mail.ring(tok_far, *x_ring)
    to_sib += mail.same(tok_far(0), [sib])
    arrived(own_low)
    low_z = mail.ring(ws_of(1 - yl), *z_ring)
    own_z2 = mail.ring_on(ws_of(yl), own_z, *z_ring)
    own_x2 = mail.ring_on(tok_own, own_x, *x_ring)
    to_sib += mail.same(tok_own(1), [sib]) + mail.same(tok_own(3), [sib])
    arrived(tab_low)
    low_tab = mail.ring(tab_of(1 - yl), *z_ring)
    low_z2 = mail.ring_on(ws_of(1 - yl), low_z, *z_ring)
    far_x2 = mail.ring_on(tok_far, far_x, *x_ring)
    to_sib += mail.same(tok_far(1), [sib]) + mail.same(tok_far(3), [sib])
    arrived(own_x2)
    to_sib += mail.same(tok_own(2), [sib])
    tab_z2 = mail.ring_on(tab_of(yl), tab_z, *z_ring)
    last_z2 = mail.ring_on(tab_last, last_z, *z_ring)
    to_low += mail.same(tab_last(1), [low]) + mail.same(tab_last(3), [low])
    arrived(two_y)
    two_z = mail.same(r.w.at[:, :, z, :, lanes(1024, 0)], zp)
    arrived(o_z)
    o_y = mail.same(r.wt.at[yh, yl], yp)
    arrived(far_x2)
    to_sib += mail.same(tok_far(2), [sib])
    arrived(one_z)
    one_x = mail.same(r.w.at[yh, yl, :, :, lanes(512, 0)], xp)
    arrived(own_z2 + low_z2)
    low_tab2 = mail.ring_on(tab_of(1 - yl), low_tab, *z_ring)
    arrived(last_z2)
    to_low += mail.same(tab_last(2), [low])
    arrived(zero_y)
    zero_z = mail.ring(w0, *z_ring)

    hots = spread_heads()
    hots32 = spread_heads(F32)
    for j in range(3):
        full = r.ws[:, j].reshape(D, QK)
        r.wide[:, :, :, j * QKW : (j + 1) * QKW] = nn(full, hots).astype(BF).reshape(2, 4, 96, QKW)
    q_add = jnp.dot(r.qvb[0], hots32, precision=lax.Precision.HIGHEST)
    v_add = jnp.dot(r.qvb[1], hots32, precision=lax.Precision.HIGHEST)
    arrived(to_sib)

    @pl.loop(0, 4)
    def _(i):
        both = nn(r.xs[i].reshape(CTX_ROWS, D), r.wide[:, :, :, QKW:].reshape(D, 2 * QKW))
        mine = pl.ds(i * OWN_SEGS, OWN_SEGS)
        r.k[mine] = both[:, :QKW].astype(BF).reshape(OWN_SEGS, SEG, QKW)
        r.v[mine] = (both[:, QKW:] + v_add).astype(BF).reshape(OWN_SEGS, SEG, QKW)

    @pl.loop(0, 4)
    def _(i):
        wide_q = r.wide[:, :, :, :QKW].reshape(D, QKW)
        r.q[pl.ds(i * ROWS, ROWS), :] = (nn(r.xs[x, i], wide_q) + q_add).astype(BF)

    arrived(one_x)
    one_y = mail.ring(w1, *y_ring)
    arrived(two_z)
    two_x = mail.ring(w2, *x_ring)

    def climb(seg):
        r.trail[0] = seg
        depth = jnp.int32(0)
        here = seg
        for i in range(1, PATH):
            up = r.parents[0, here]
            found = up >= 0
            here = jnp.where(found, up, here)
            r.trail[i] = here
            depth = depth + found.astype(jnp.int32)
        return depth

    def on_path(depth, j):
        return r.trail[jnp.maximum(depth - j, 0)]

    def fetch_path(depth):
        for j in range(PATH):
            above = on_path(depth, j)
            r.kp[pl.ds(j * SEG, SEG), :] = r.k[above]
            r.vp[pl.ds(j * SEG, SEG), :] = r.v[above]

    arrived(tab_z2 + low_tab2 + to_low)

    def attend(a):
        depth = climb(x * OWN_SEGS + a)
        fetch_path(depth)
        mine = pl.ds(pl.multiple_of(a * SEG, SEG), SEG)
        tile = lax.rem(depth, 4) * 2
        for h in range(HEADS_DEV):
            head = slice(h * WIDE, (h + 1) * WIDE)
            low_q = r.q[mine, head] * jnp.asarray(SCALE, BF)
            flat = r.tab.at[h]
            pieces = [
                flat[lax.div(tile + i, 4), lax.rem(tile + i, 4)].astype(F32) for i in range(2)
            ]
            table = jnp.concatenate(pieces, axis=0)
            scores = nt(low_q, r.kp[:, head])
            parts = []
            for j in range(PATH):
                cols = slice((j % 4) * SEG, (j % 4 + 1) * SEG)
                score = scores[:, j * SEG : (j + 1) * SEG] + table[:, cols]
                parts.append(jnp.where(j <= depth, score, -1e30))
            scores = jnp.concatenate(parts, axis=1)
            peak = jnp.max(scores, axis=1, keepdims=True)
            raised = jnp.exp(scores - peak)
            whole = jnp.sum(raised, axis=1, keepdims=True)
            soft = (raised * (1.0 / whole)).astype(BF)
            r.p[a, h] = soft
            r.o_wide[mine, head] = nn(soft, r.vp[:, head]).astype(BF)

    pl.loop(0, 2)(attend)
    zero_z2 = mail.ring_on(w0, zero_z, *z_ring)
    pl.loop(2, 4)(attend)
    one_y2 = mail.ring_on(w1, one_y, *y_ring)
    two_x2 = mail.ring_on(w2, two_x, *x_ring)
    pl.loop(4, 5)(attend)
    r.o[...] = nt(r.o_wide[...], hots).astype(BF)
    o_far = [mail.post(r.o.at[pl.ds((1 - yh) * PAIR, PAIR)], r.o2.at[yh], far)]
    r.o2[yh] = r.o[pl.ds(yh * PAIR, PAIR), :]

    own, other = pl.ds(core * ROWS, ROWS), pl.ds((1 - core) * ROWS, ROWS)

    def trade_sum(slot):
        mail.done(mail.post(r.part.at[other], r.got.at[slot], sib))
        return r.part[own, :] + r.got[slot]

    def trade_rows(slot, values):
        r.rows[slot, own, :] = values
        arrived(mail.same(r.rows.at[slot, own], [sib]))

    def both_halves(left0, left1, weights):
        for half in range(2):
            cols = slice(half * 384, (half + 1) * 384)
            r.part[:, cols] = nt(left0, weights(0, half)) + nt(left1, weights(1, half))

    def tiles():
        return [(which, n) for which in range(2) for n in range(3)]

    def outer(which, half):
        return r.w[which, half, :, :, :D].reshape(384, D)

    def inner(which, half):
        return r.w[which, half, :, :, D:].reshape(384, D)

    arrived(o_y + o_far)
    both_halves(r.o2[0], r.o2[1], lambda a, b: r.wt[a, b, :, :, :QK].reshape(384, QK))
    n1, inv1 = normed(r.xs[x, tp].astype(F32) + trade_sum(0) + line(bo))
    r.n1s[...] = n1
    y1 = n1 * line(g1) + line(s1)
    r.y1s[...] = y1
    trade_rows(0, y1.astype(BF))
    arrived([*bias_far, *zero_z2, *one_y2, *two_x2])

    @pl.loop(0, 6)
    def _(i):
        which, col = lax.div(i, 3), pl.multiple_of(lax.rem(i, 3) * 256, 256)
        later = pl.multiple_of(col + D, 256)
        weight = r.w[which, :, :, :, pl.ds(later, 256)].reshape(D, 256)
        u = nn(r.rows[0], weight) + r.bias[which, :, pl.ds(col, 256)]
        phi = 0.5 * (1.0 + lax.erf(u * 0.7071067811865476))
        r.act[which, :, pl.ds(col, 256)] = (u * phi).astype(BF)
        slope = phi + u * (jnp.exp(-0.5 * u * u) * 0.3989422804014327)
        r.slope[pl.ds(pl.multiple_of(which * PAIR, PAIR), PAIR), pl.ds(col, 256)] = slope

    both_halves(r.act[0], r.act[1], outer)
    n2, inv2 = normed(r.y1s[...] + trade_sum(1) + line(bout))
    gain2 = line(g2)
    r.res[...] = (n2 * gain2 + line(s2)).astype(BF)
    c = r.cots[...].astype(F32)
    r.v_own[...] = jnp.zeros_like(r.v_own)
    r.v_own[4:5, :] = total(c * n2)
    r.v_own[5:6, :] = total(c)
    dh2 = normed_back(c, gain2, n2, inv2)
    r.dh2s[...] = dh2
    df = dh2.astype(BF)
    r.v_own[1:2, :] = total(df.astype(F32))
    trade_rows(1, df)

    @pl.loop(0, 6)
    def _(i):
        which, col = lax.div(i, 3), pl.multiple_of(lax.rem(i, 3) * 256, 256)
        weight = r.w[which, :, :, :, pl.ds(col, 256)].reshape(D, 256)
        slope = r.slope[pl.ds(pl.multiple_of(which * PAIR, PAIR), PAIR), pl.ds(col, 256)]
        grad = (nn(r.rows[1], weight) * slope).astype(BF)
        r.du[which, :, pl.ds(col, 256)] = grad
        r.v_own[pl.ds(6 + which, 1), pl.ds(col, 256)] = total(grad.astype(F32))

    mail.flush()
    both_halves(r.du[0], r.du[1], inner)
    c_dy = [mail.post(r.part.at[other], r.got.at[2], sib)]

    @pl.loop(0, 6)
    def _(i):
        which, col = lax.div(i, 3), pl.multiple_of(lax.rem(i, 3) * 256, 256)
        later = pl.multiple_of(col + D, 256)
        grad = tn(r.rows[1], r.act[which, :, pl.ds(col, 256)]).astype(BF)
        r.w[which, :, :, :, pl.ds(col, 256)] = grad.reshape(2, 4, 96, 256)
        grad = tn(r.rows[0], r.du[which, :, pl.ds(col, 256)]).astype(BF)
        r.w[which, :, :, :, pl.ds(later, 256)] = grad.reshape(2, 4, 96, 256)

    c0z = mail.fold(w0, r.r0z, *z_ring)
    c2x = mail.fold(w2, r.r2x, *x_ring)
    arrived(c_dy)
    dy1 = r.part[own, :] + r.got[2] + r.dh2s[...]
    n1 = r.n1s[...]
    r.v_own[2:3, :] = total(dy1 * n1)
    r.v_own[3:4, :] = total(dy1)
    dh1 = normed_back(dy1, line(g1), n1, inv1)
    r.dh1s[...] = dh1
    da = dh1.astype(BF)
    r.v_own[0:1, :] = total(da.astype(F32))
    trade_rows(2, da)
    leave = r.o.at[pl.ds(0, PAIR)]
    leave[...] = nn(r.rows[2], r.wt[1 - yh, :, :, :, :QK].reshape(D, QK)).astype(BF)
    back = [mail.post(leave, r.dout.at[pl.ds(yh * PAIR, PAIR)], far)]
    r.dout[pl.ds(yh * PAIR, PAIR), :] = nn(r.rows[2], r.wt[yh, :, :, :, :QK].reshape(D, QK)).astype(BF)
    for which in range(2):
        grad = tn(r.rows[2], r.o2[which]).astype(BF)
        r.wt[which, :, :, :, :QK] = grad.reshape(2, 4, 96, QK)
    r.slope[...] = jnp.zeros_like(r.slope)
    r.tgp[...] = jnp.zeros_like(r.tgp)
    r.dtab[...] = jnp.zeros_like(r.dtab)
    for b in range(SEGS):
        r.depths[b] = climb(jnp.int32(b))
    arrived(back)
    c1y = mail.fold(w1, r.r1y, *y_ring)
    coz = mail.spread(lambda k: r.wt.at[:, :, around(z, k)], r.roz, zp)

    def spot(h, b):
        n = h * SEGS + b
        return slice(n // 6 * 64, n // 6 * 64 + 64), slice(n % 6 * 128, n % 6 * 128 + 128)

    def attend_back(a):
        depth = climb(x * OWN_SEGS + a)
        fetch_path(depth)
        mine = pl.ds(pl.multiple_of(a * SEG, SEG), SEG)
        tile = lax.rem(depth, 4)
        grads = nn(r.dout[mine, :], hots).astype(BF)
        for h in range(HEADS_DEV):
            head = slice(h * WIDE, (h + 1) * WIDE)
            low_q, grad = r.q[mine, head], grads[:, head]
            soft = r.p[a, h]
            inside = grad.astype(F32) * r.o_wide[mine, head].astype(F32)
            ds = soft.astype(F32) * (
                nt(grad, r.vp[:, head]) - jnp.sum(inside, axis=1, keepdims=True)
            )
            ds_low = ds.astype(BF)
            r.dq_wide[mine, head] = (nn(ds_low, r.kp[:, head]) * SCALE).astype(BF)
            q_t = (low_q.astype(F32).T[:HEAD_DIM] * SCALE).astype(BF)
            grad_t = grad.astype(F32).T[:HEAD_DIM].astype(BF)
            dk_part, dv_part = nn(q_t, ds_low), nn(grad_t, soft)
            for j in range(PATH):
                r.parts[0, j] = dk_part[:, j * SEG : (j + 1) * SEG]
                r.parts[1, j] = dv_part[:, j * SEG : (j + 1) * SEG]
            for b in range(SEGS):
                down = r.depths[b]
                held = (down <= depth) & (on_path(depth, down) == b)
                rows, cols = spot(h, b)
                r.slope[rows, cols] += jnp.where(held, r.parts[0, down], 0.0)
                r.tgp[rows, cols] += jnp.where(held, r.parts[1, down], 0.0)
            fall = ds_low.astype(F32)
            left = fall[:, 0:256] + fall[:, 512:768] + fall[:, 1024:1280]
            right = fall[:, 256:512] + fall[:, 768:1024]
            for t in range(4):
                span = slice(t * SEG, (t + 1) * SEG)
                r.dtab[h, span, 0:256] += jnp.where(tile == t, left, 0.0)
                r.dtab[h, span, 256:512] += jnp.where(tile == t, right, 0.0)

    c0z = mail.fold_on(w0, r.r0z, c0z, *z_ring)
    c2x = mail.fold_on(w2, r.r2x, c2x, *x_ring)
    pl.loop(0, OWN_SEGS)(attend_back)
    c1y = mail.fold_on(w1, r.r1y, c1y, *y_ring)
    for h in range(HEADS_DEV):
        for b in range(SEGS):
            rows, cols = spot(h, b)
            into = slice(b % 5 * SEG, (b % 5 + 1) * SEG)
            r.p[b // 5, h, 0:64, into] = r.slope[rows, cols].astype(BF)
            r.p[b // 5, h, 64:128, into] = r.tgp[rows, cols].astype(BF)

    def dkv(k, half):
        return r.p.at[around(x, k), :, pl.ds(half * 64, 64), pl.ds(0, CTX_ROWS)]

    c_dkv = mail.fold(dkv, r.r_dkv, *x_ring)
    for h in range(HEADS_DEV):
        r.tab[h] = r.dtab[h].astype(BF).reshape(2, 4, 64, DEPTHS)
    d0z = mail.spread(lambda k: r.tab.at[0, :, around(z, k)], r.t0z, zp)
    d1y = mail.post(r.tab.at[1, 1 - yl], r.t1y, low)
    d2y = mail.post(r.tab.at[2, 1 - yl], r.t2y, low)

    def project_grad(j, values):
        room = slice(j * QKW, j * QKW + QK)
        parts = [tn(r.xs[x, i], values[i * ROWS : (i + 1) * ROWS, :]) for i in range(4)]
        r.wide[:, :, :, room] = (parts[0] + parts[1] + parts[2] + parts[3]).astype(BF).reshape(2, 4, 96, QK)
        send = pl.ds(j * QKW, QKP)
        return mail.spread(lambda k: r.wide.at[:, around(z, k), :, send], r.rqz.at[j], zp)

    def weight_of(j):
        return r.ws[:, j].reshape(D, QK)

    q_low = nt(r.dq_wide[...], hots).astype(BF)
    cqz = [project_grad(0, q_low)]
    r.tgp[...] = nt(q_low, weight_of(0))
    r.v_own[pl.ds(8 + yh, 1), 0:QK] = total(q_low.astype(F32))
    c_dkv = mail.fold_on(dkv, r.r_dkv, c_dkv, *x_ring)
    arrived(c0z)
    for half in range(2):
        r.s0z[half : half + 1] = folded(w0, r.r0z, half).astype(BF)
    c0y = mail.spread(lambda k: r.s0z.at[ys[k][0], ys[k][1]], r.r0y, yp)
    arrived(c2x)
    for half in range(2):
        r.s2x[half : half + 1] = folded(w2, r.r2x, half).astype(BF)
    c2z = mail.spread(lambda k: r.s2x.at[:, :, around(z, k)], r.r2z, zp)
    arrived(coz)
    r.soz[...] = added(r.wt[:, :, z], r.roz).astype(BF)
    coy = mail.spread(lambda k: r.soz.at[ys[k][0], ys[k][1]], r.roy, yp)
    arrived(c1y)
    for half in range(2):
        r.s1y[half * 2 : half * 2 + 2] = folded(w1, r.r1y, half).astype(BF)
    c1x = mail.spread(lambda k: r.s1y.at[:, :, lanes(0, k)], r.r1x, xp)
    arrived(d0z)
    r.u0z[...] = added(r.tab[0, :, z], r.t0z).astype(BF)
    d0y = mail.post(r.u0z.at[1 - yl], r.t0y, low)
    arrived([d1y])
    r.u1y[...] = (r.tab[1, yl].astype(F32) + r.t1y[...].astype(F32)).astype(BF)
    d1x = mail.spread(lambda k: r.u1y.at[:, :, lanes(0, k)], r.t1x, xp)
    arrived([d2y])
    r.u2y[...] = (r.tab[2, yl].astype(F32) + r.t2y[...].astype(F32)).astype(BF)
    d2z = mail.spread(lambda k: r.u2y.at[around(z, k)], r.t2z, zp)

    arrived(c_dkv)
    k_low = folded(dkv, r.r_dkv, 0).reshape(QK, CTX_ROWS).T.astype(BF)
    v_low = folded(dkv, r.r_dkv, 1).reshape(QK, CTX_ROWS).T.astype(BF)
    r.v_own[pl.ds(10 + yh, 1), 0:QK] = total(v_low.astype(F32))
    r.vx[x] = r.v_own[...]
    c_vx = mail.same(r.vx.at[x], xp)
    r.tgp[...] += nt(k_low, weight_of(1)) + nt(v_low, weight_of(2))

    def quarter(a, b):
        return pl.ds((a * 2 + b) * ROWS, ROWS)

    c_sib = [mail.post(r.tgp.at[quarter(a, 1 - core)], r.got.at[a], sib) for a in range(2)]
    cqz.append(project_grad(1, k_low))
    cqz.append(project_grad(2, v_low))
    arrived(c_sib)
    s_far = r.rows.at[0, pl.ds(0, ROWS)]
    s_far[...] = (r.tgp[quarter(1 - yh, core), :] + r.got[1 - yh]).astype(BF)
    c_far = [mail.post(s_far, r.r_far, far)]

    arrived(c0y)
    r.s0y[...] = added(r.s0z[yh, yl], r.r0y).astype(BF)
    c0x = mail.spread(lambda k: r.s0y.at[:, lanes(0, k)], r.r0x, xp)
    arrived(coy)
    r.rox[x] = added(r.soz[yh, yl], r.roy).astype(BF)
    cox = mail.same(r.rox.at[x], xp)
    arrived(c1x)
    r.s1x[...] = added(r.s1y[:, :, lanes(0, 0)], r.r1x).astype(BF)
    c1z = mail.spread(lambda k: r.s1x.at[around(z, k)], r.r1z, zp)
    arrived([d0y])
    r.u0y[...] = (r.u0z[yl].astype(F32) + r.t0y[...].astype(F32)).astype(BF)
    d0x = mail.spread(lambda k: r.u0y.at[:, lanes(0, k)], r.t0x, xp)
    arrived(d1x)
    r.u1x[...] = added(r.u1y[:, :, lanes(0, 0)], r.t1x).astype(BF)
    d1z = mail.spread(lambda k: r.u1x.at[around(z, k)], r.t1z, zp)
    cqy = []
    for j in range(3):
        arrived(cqz[j])
        r.sqz[j] = added(r.wide[:, z, :, j * QKW : j * QKW + QKP], r.rqz.at[j]).astype(BF)
        cqy.append(mail.post(r.sqz.at[j, 1 - yl], r.rqy.at[j], low))
    arrived(c_vx)
    r.vz[z] = slots_total(r.vx)
    c_vz = mail.same(r.vz.at[z], zp)
    arrived(d2z)
    r.u2z[...] = added(r.u2y[z], r.t2z).astype(BF)
    d2x = mail.spread(lambda k: r.u2z.at[:, lanes(0, k)], r.t2x, xp)
    arrived(c_far)
    r.tg[...] = r.tgp[quarter(yh, core), :] + r.got[yh] + r.r_far[...].astype(F32) + r.dh1s[...]
    cqx = []
    for j in range(3):
        arrived([cqy[j]])
        r.rqx[j, x] = (r.sqz[j, yl].astype(F32) + r.rqy[j].astype(F32)).astype(BF)
        cqx.append(mail.same(r.rqx.at[j, x], xp))

    late = []

    def settle(ref, base, values):
        ref[:, lanes(base, 0)] = values.astype(BF)
        late.extend(mail.same(ref.at[:, lanes(base, 0)], xp))

    arrived(c0x)
    settle(r.f, 0, added(r.s0y[:, lanes(0, 0)], r.r0x))
    arrived(c1z)
    settle(r.f, 512, added(r.s1x[z], r.r1z))
    arrived(d0x)
    settle(r.ft.at[0], 0, added(r.u0y[:, lanes(0, 0)], r.t0x))
    arrived(d1z)
    settle(r.ft.at[1], 0, added(r.u1x[z], r.t1z))
    arrived(c_vz)
    r.vy[y] = slots_total(r.vz)
    c_vy = mail.same(r.vy.at[y], yp)
    arrived(c2z)
    r.s2z[...] = added(r.s2x[:, :, z], r.r2z).astype(BF)
    c2y = mail.spread(lambda k: r.s2z.at[ys[k][0], ys[k][1]], r.r2y, yp)
    arrived(d2x)
    settle(r.ft.at[2], 0, added(r.u2z[:, lanes(0, 0)], r.t2x))
    arrived(c_vy)
    r.vc[0] = slots_total(r.vy)
    c_vc = mail.post(r.vc.at[0], r.vc.at[1], sib)
    arrived(c2y)
    settle(r.f, 1024, added(r.s2z[yh, yl], r.r2y))
    arrived(cox)
    r.fo[...] = slots_total(r.rox)
    for j in range(3):
        arrived(cqx[j])
        r.fq[j] = slots_total(r.rqx.at[j])
    arrived([c_vc])
    r.vsum[...] = r.vc[0]
    r.vsum[0:6, :] = r.vc[0, 0:6, :] + r.vc[1, 0:6, :]
    arrived(late)
    mail.flush()
    assert mail.used <= POSTS


def layer(*arrays):
    vm = pl.BlockSpec(memory_space=pltpu.VMEM)
    hbm = pl.BlockSpec(memory_space=pltpu.HBM)
    return pl.pallas_call(
        layer_kernel,
        out_shape=tuple(jax.ShapeDtypeStruct(*entry) for entry in OUTPUTS.values()),
        in_specs=[pl.BlockSpec(memory_space=pltpu.SMEM)] + [hbm] * (len(INPUTS) - 1),
        out_specs=[vm] * len(OUTPUTS),
        scratch_shapes=[
            *(pltpu.VMEM(*entry) for entry in SCRATCH.values()),
            pltpu.SMEM((PATH,), jnp.int32),
            pltpu.SMEM((SEGS,), jnp.int32),
            pltpu.SemaphoreType.DMA((20,)),
            pltpu.SemaphoreType.DMA((POSTS,)),
            pltpu.SemaphoreType.DMA((POSTS,)),
        ],
        compiler_params=pltpu.CompilerParams(
            collective_id=1, has_side_effects=True, vmem_limit_bytes=60 * MIB
        ),
        name="layer",
    )(*arrays)


def finish_kernel(*refs):
    f_in, fo_in, fq_in, ft_in, tg, vsum_in, res, logits_in, noise_in = refs[:9]
    res_out, tg_out, gwq, gwk, gwv, gwo, gwi, gwout_t, mask, gbq, gbv, *lines = refs[9:-8]
    f, fo, fq, ft, vsum, logits, noise, sem = refs[-8:]
    pairs = [
        (res, res_out),
        (tg, tg_out),
        (f_in, f),
        (fo_in, fo),
        (fq_in, fq),
        (ft_in, ft),
        (vsum_in, vsum),
        (logits_in, logits),
        (noise_in, noise),
    ]
    copies = [pltpu.make_async_copy(src, dst, sem.at[n]) for n, (src, dst) in enumerate(pairs)]
    for copy in copies:
        copy.start()
    for copy in copies[2:]:
        copy.wait()
    gwq[...], gwk[...], gwv[...] = fq[0, :, :QK], fq[1, :, :QK], fq[2, :, :QK]
    gwo[...] = fo[...].T[:QK]
    gwout_t[...] = f[:, :D].astype(F32)
    gwi[...] = f[:, D:].astype(F32)
    mask[...] = ft[...].astype(F32) * jax.nn.sigmoid(-(logits[...] + noise[...]))
    yh = lax.div(lax.axis_index("tp"), 2)
    gbq[...] = vsum[pl.ds(8 + yh, 1), 0:QK]
    gbv[...] = vsum[pl.ds(10 + yh, 1), 0:QK]
    for n, out in enumerate(lines):
        row = vsum[pl.ds(6 + yh, 1), :] if n == 6 else vsum[n : n + 1, :]
        for i in range(6):
            out[i : i + 1, :] = row[:, i * 128 : (i + 1) * 128]
    for copy in copies[:2]:
        copy.wait()


def finish(f, fo, fq, ft, tg, vsum, res, logits, noise):
    shape = jax.ShapeDtypeStruct
    vm = pl.BlockSpec(memory_space=pltpu.VMEM)
    hbm = pl.BlockSpec(memory_space=pltpu.HBM)
    outs = (
        shape((ROWS, D), BF),
        shape((ROWS, D), F32),
        shape((96, QK), F32),
        shape((96, QK), F32),
        shape((96, QK), F32),
        shape((QK, 96), F32),
        shape((96, D), F32),
        shape((96, D), F32),
        shape((HEADS_DEV, 64, DEPTHS), F32),
        shape((1, QK), F32),
        shape((1, QK), F32),
        *[shape((6, 128), F32)] * 7,
    )
    held = (f, fo, fq, ft, vsum, logits, noise)
    return pl.pallas_call(
        finish_kernel,
        out_shape=outs,
        in_specs=[hbm] * 9,
        out_specs=[hbm] * 2 + [vm] * (len(outs) - 2),
        scratch_shapes=[
            *(pltpu.VMEM(entry.shape, entry.dtype) for entry in held),
            pltpu.SemaphoreType.DMA((9,)),
        ],
        compiler_params=pltpu.CompilerParams(vmem_limit_bytes=60 * MIB),
        name="finish",
    )(f, fo, fq, ft, tg, vsum, res, logits, noise)


def shards(
    tokens,
    parents,
    query_weight,
    query_bias,
    key_weight,
    value_weight,
    value_bias,
    output_weight,
    output_bias,
    first_gain,
    first_shift,
    inner_weight,
    inner_bias,
    outer_weight,
    outer_bias,
    second_gain,
    second_shift,
    mask_logits,
    mask_noise,
    cotangent,
):
    def lined(vector):
        return vector.reshape(6, 128)

    res, tg, f, fo, fq, ft, vsum = layer(
        parents,
        tokens,
        cotangent,
        query_weight,
        key_weight,
        value_weight,
        query_bias.reshape(1, QK),
        value_bias.reshape(1, QK),
        mask_logits,
        mask_noise,
        output_weight,
        inner_weight,
        outer_weight.T,
        lined(output_bias),
        lined(first_gain),
        lined(first_shift),
        lined(inner_bias),
        lined(outer_bias),
        lined(second_gain),
        lined(second_shift),
    )
    result, tg, gwq, gwk, gwv, gwo, gwi, gwout_t, mask, gbq, gbv, *lines = finish(
        f, fo, fq, ft, tg, vsum, res, mask_logits, mask_noise
    )
    bo, bout, g1, s1, g2, s2, bi = [entry.reshape(D) for entry in lines]
    return (
        result,
        tg,
        gwq,
        gbq.reshape(QK),
        gwk,
        gwv,
        gbv.reshape(QK),
        gwo,
        bo,
        g1,
        s1,
        gwi,
        bi,
        gwout_t.T,
        bout,
        g2,
        s2,
        mask,
    )


def solution(mesh):
    in_specs = (
        P(("shard", "ctx", "tp"), None),
        P("shard", None),
        P("shard", "tp"),
        P("tp"),
        P("shard", "tp"),
        P("shard", "tp"),
        P("tp"),
        P("tp", "shard"),
        P(),
        P(),
        P(),
        P("shard", "tp"),
        P("tp"),
        P("tp", "shard"),
        P(),
        P(),
        P(),
        P("tp", "shard", None),
        P("tp", "shard", None),
        P(("shard", "ctx", "tp"), None),
    )
    out_specs = (
        P(("shard", "ctx", "tp"), None),
        P(("shard", "ctx", "tp"), None),
        P("shard", "tp"),
        P("tp"),
        P("shard", "tp"),
        P("shard", "tp"),
        P("tp"),
        P("tp", "shard"),
        P(),
        P(),
        P(),
        P("shard", "tp"),
        P("tp"),
        P("tp", "shard"),
        P(),
        P(),
        P(),
        P("tp", "shard", None),
    )
    return jax.shard_map(shards, mesh=mesh, in_specs=in_specs, out_specs=out_specs, check_vma=False)
```

time: 1090 us -> 175 us (0.16)
  the two profiles are of different devices: /device:TPU:8 before, /device:TPU:1 now
where the time goes in v3:
time: 175 us
  Pallas kernels  174 us (99%)
    pallas_call x1, Pallas kernels, layer(): pl.pallas_call(layer_kernel, out_shape=tuple((jax.ShapeDtypeStruct(*entry...  150 us
    pallas_call x1, Pallas kernels, finish(): pl.pallas_call(finish_kernel, out_shape=outs, in_specs=[hbm] * 9, out_spe...  24.6 us

profile of v3, /device:TPU:1, one launch (start us, length us, event | category | flops | bytes accessed | tf_op | source)
XLA Modules:
  0.0 175.0 jit_solution(4101541693433767021)
XLA Ops:
  0.7 149.6 %layer.1 = (bf16[160,768]{1,0:T(8,128)(2,1)}, f32[160,768]{1,0:T(8,128)}, bf16[96,1536]{1,0:T(8,128)(2,1)}, f32[96,256]{1,0:T(8,128)}, f32[3,96,256]{2,1,0:T(8,1...) custom-call(s32[1,20]{1,0:T(1,128)} %refs_0_.1, bf16[160,768]{1,0:T(8,128)(2,1)} %refs_1_.1, ...), custom_call_target="tpu_custom_call" | custom-call | tf_op jit(solution)/shard_map/layer/pallas_call | solution.py:825
  150.3 24.6 %finish.1 = (bf16[160,768]{1,0:T(8,128)(2,1)}, f32[160,768]{1,0:T(8,128)}, f32[96,192]{1,0:T(8,128)}, f32[96,192]{1,0:T(8,128)}, f32[96,192]{1,0:T(8,128)}, /*in...) custom-call(bf16[96,1536]{1,0:T(8,128)(2,1)} %get-tuple-element.43.r, ...), custom_call_target="tpu_custom_call" | custom-call | tf_op jit(solution)/shard_map/finish/pallas_call | solution.py:900

commit v4 on v3

--- a/solution.py
+++ b/solution.py
@@ -20,6 +20,7 @@
 QK = 192
 QKP = 256
 QKW = 384
+QKV = QKP + QKW
 ROWS = 160
 PAIR = 320
 CTX_ROWS = 640
@@ -211,7 +212,7 @@
     "tg": ((ROWS, D), F32),
     "f": ((96, 2 * D), BF),
     "fo": ((96, QKP), F32),
-    "fq": ((3, 96, QKP), F32),
+    "fq": ((96, QKV), F32),
     "ft": ((HEADS_DEV, 64, DEPTHS), BF),
     "vsum": ((16, D), F32),
 }
@@ -252,7 +253,9 @@
     "dtab": ((HEADS_DEV, DEPTHS, DEPTHS), F32),
     "dq_wide": ((CTX_ROWS, QKW), BF),
     "tgp": ((CTX_ROWS, D), F32),
-    "r_dkv": ((6, HEADS_DEV, 64, CTX_ROWS), BF),
+    "r_dka": ((6, 2, 64, CTX_ROWS), BF),
+    "r_dkb": ((6, 1, 64, CTX_ROWS), BF),
+    "kv_t": ((2 * QK, D), F32),
     "r0z": ((6, 1, 2, 96, 512), BF),
     "s0z": ((2, 2, 96, 512), BF),
     "r0y": ((3, 96, 512), BF),
@@ -287,10 +290,10 @@
     "soz": ((2, 2, 96, QKP), BF),
     "roy": ((3, 96, QKP), BF),
     "rox": ((4, 96, QKP), BF),
-    "rqz": ((3, 3, 2, 96, QKP), BF),
-    "sqz": ((3, 2, 96, QKP), BF),
-    "rqy": ((3, 96, QKP), BF),
-    "rqx": ((3, 4, 96, QKP), BF),
+    "rqz": ((3, 2, 96, QKV), BF),
+    "sqz": ((2, 96, QKV), BF),
+    "rqy": ((96, QKV), BF),
+    "rqx": ((4, 96, QKV), BF),
     "r_far": ((ROWS, D), BF),
     "v_own": ((16, D), F32),
     "vx": ((4, 16, D), F32),
@@ -612,6 +615,7 @@
     leave = r.o.at[pl.ds(0, PAIR)]
     leave[...] = nn(r.rows[2], r.wt[1 - yh, :, :, :, :QK].reshape(D, QK)).astype(BF)
     back = [mail.post(leave, r.dout.at[pl.ds(yh * PAIR, PAIR)], far)]
+    c1y = mail.fold(w1, r.r1y, *y_ring)
     r.dout[pl.ds(yh * PAIR, PAIR), :] = nn(r.rows[2], r.wt[yh, :, :, :, :QK].reshape(D, QK)).astype(BF)
     for which in range(2):
         grad = tn(r.rows[2], r.o2[which]).astype(BF)
@@ -622,20 +626,19 @@
     for b in range(SEGS):
         r.depths[b] = climb(jnp.int32(b))
     arrived(back)
-    c1y = mail.fold(w1, r.r1y, *y_ring)
     coz = mail.spread(lambda k: r.wt.at[:, :, around(z, k)], r.roz, zp)
 
     def spot(h, b):
         n = h * SEGS + b
         return slice(n // 6 * 64, n // 6 * 64 + 64), slice(n % 6 * 128, n % 6 * 128 + 128)
 
-    def attend_back(a):
+    def attend_back(a, heads):
         depth = climb(x * OWN_SEGS + a)
         fetch_path(depth)
         mine = pl.ds(pl.multiple_of(a * SEG, SEG), SEG)
         tile = lax.rem(depth, 4)
         grads = nn(r.dout[mine, :], hots).astype(BF)
-        for h in range(HEADS_DEV):
+        for h in heads:
             head = slice(h * WIDE, (h + 1) * WIDE)
             low_q, grad = r.q[mine, head], grads[:, head]
             soft = r.p[a, h]
@@ -665,42 +668,63 @@
                 r.dtab[h, span, 0:256] += jnp.where(tile == t, left, 0.0)
                 r.dtab[h, span, 256:512] += jnp.where(tile == t, right, 0.0)
 
+    def settle_heads(heads):
+        for h in heads:
+            for b in range(SEGS):
+                rows, cols = spot(h, b)
+                into = slice(b % 5 * SEG, (b % 5 + 1) * SEG)
+                r.p[b // 5, h, 0:64, into] = r.slope[rows, cols].astype(BF)
+                r.p[b // 5, h, 64:128, into] = r.tgp[rows, cols].astype(BF)
+            r.tab[h] = r.dtab[h].astype(BF).reshape(2, 4, 64, DEPTHS)
+
+    def dkv(first, count):
+        def view(k, half):
+            span = (pl.ds(half * 64, 64), pl.ds(0, CTX_ROWS))
+            return r.p.at[around(x, k), pl.ds(first, count), *span]
+
+        return view
+
     c0z = mail.fold_on(w0, r.r0z, c0z, *z_ring)
     c2x = mail.fold_on(w2, r.r2x, c2x, *x_ring)
-    pl.loop(0, OWN_SEGS)(attend_back)
-    c1y = mail.fold_on(w1, r.r1y, c1y, *y_ring)
-    for h in range(HEADS_DEV):
-        for b in range(SEGS):
-            rows, cols = spot(h, b)
-            into = slice(b % 5 * SEG, (b % 5 + 1) * SEG)
-            r.p[b // 5, h, 0:64, into] = r.slope[rows, cols].astype(BF)
-            r.p[b // 5, h, 64:128, into] = r.tgp[rows, cols].astype(BF)
-
-    def dkv(k, half):
-        return r.p.at[around(x, k), :, pl.ds(half * 64, 64), pl.ds(0, CTX_ROWS)]
-
-    c_dkv = mail.fold(dkv, r.r_dkv, *x_ring)
-    for h in range(HEADS_DEV):
-        r.tab[h] = r.dtab[h].astype(BF).reshape(2, 4, 64, DEPTHS)
+    pl.loop(0, OWN_SEGS)(lambda a: attend_back(a, (0, 1)))
+    settle_heads((0, 1))
+    c_dka = mail.fold(dkv(0, 2), r.r_dka, *x_ring)
     d0z = mail.spread(lambda k: r.tab.at[0, :, around(z, k)], r.t0z, zp)
     d1y = mail.post(r.tab.at[1, 1 - yl], r.t1y, low)
+    pl.loop(0, OWN_SEGS)(lambda a: attend_back(a, (2,)))
+    settle_heads((2,))
+    c_dkb = mail.fold(dkv(2, 1), r.r_dkb, *x_ring)
     d2y = mail.post(r.tab.at[2, 1 - yl], r.t2y, low)
-
-    def project_grad(j, values):
-        room = slice(j * QKW, j * QKW + QK)
-        parts = [tn(r.xs[x, i], values[i * ROWS : (i + 1) * ROWS, :]) for i in range(4)]
-        r.wide[:, :, :, room] = (parts[0] + parts[1] + parts[2] + parts[3]).astype(BF).reshape(2, 4, 96, QK)
-        send = pl.ds(j * QKW, QKP)
-        return mail.spread(lambda k: r.wide.at[:, around(z, k), :, send], r.rqz.at[j], zp)
 
     def weight_of(j):
         return r.ws[:, j].reshape(D, QK)
 
+    def quarter(a, b):
+        return pl.ds((a * 2 + b) * ROWS, ROWS)
+
+    late = []
+
+    def settle(ref, base, values):
+        ref[:, lanes(base, 0)] = values.astype(BF)
+        late.extend(mail.same(ref.at[:, lanes(base, 0)], xp))
+
     q_low = nt(r.dq_wide[...], hots).astype(BF)
-    cqz = [project_grad(0, q_low)]
-    r.tgp[...] = nt(q_low, weight_of(0))
+    grad = tn(r.xs[x].reshape(CTX_ROWS, D), q_low).astype(BF)
+    r.wide[:, :, :, 0:QK] = grad.reshape(2, 4, 96, QK)
+    for i in range(4):
+        both = r.p[i, :, :, 0:CTX_ROWS].reshape(2 * QK, CTX_ROWS)
+        term = nn(both, r.xs[i].reshape(CTX_ROWS, D))
+        r.kv_t[...] = term if i == 0 else r.kv_t[...] + term
+    r.wide[:, :, :, QKP : QKP + QKW] = r.kv_t[...].T.astype(BF).reshape(2, 4, 96, QKW)
+    cqz = mail.spread(lambda k: r.wide.at[:, around(z, k), :, pl.ds(0, QKV)], r.rqz, zp)
     r.v_own[pl.ds(8 + yh, 1), 0:QK] = total(q_low.astype(F32))
-    c_dkv = mail.fold_on(dkv, r.r_dkv, c_dkv, *x_ring)
+    ones = jnp.ones((8, CTX_ROWS), BF)
+    sums = [nt(ones, r.p[i, :, 64:128, 0:CTX_ROWS].reshape(QK, CTX_ROWS)) for i in range(4)]
+    r.v_own[pl.ds(10 + yh, 1), 0:QK] = (sums[0] + sums[1] + sums[2] + sums[3])[0:1]
+    c_dka = mail.fold_on(dkv(0, 2), r.r_dka, c_dka, *x_ring)
+    r.vx[x] = r.v_own[...]
+    c_vx = mail.same(r.vx.at[x], xp)
+    c1y = mail.fold_on(w1, r.r1y, c1y, *y_ring)
     arrived(c0z)
     for half in range(2):
         r.s0z[half : half + 1] = folded(w0, r.r0z, half).astype(BF)
@@ -712,105 +736,95 @@
     arrived(coz)
     r.soz[...] = added(r.wt[:, :, z], r.roz).astype(BF)
     coy = mail.spread(lambda k: r.soz.at[ys[k][0], ys[k][1]], r.roy, yp)
-    arrived(c1y)
-    for half in range(2):
-        r.s1y[half * 2 : half * 2 + 2] = folded(w1, r.r1y, half).astype(BF)
-    c1x = mail.spread(lambda k: r.s1y.at[:, :, lanes(0, k)], r.r1x, xp)
     arrived(d0z)
     r.u0z[...] = added(r.tab[0, :, z], r.t0z).astype(BF)
     d0y = mail.post(r.u0z.at[1 - yl], r.t0y, low)
     arrived([d1y])
     r.u1y[...] = (r.tab[1, yl].astype(F32) + r.t1y[...].astype(F32)).astype(BF)
     d1x = mail.spread(lambda k: r.u1y.at[:, :, lanes(0, k)], r.t1x, xp)
+    r.tgp[...] = nt(q_low, weight_of(0))
+    c_dkb = mail.fold_on(dkv(2, 1), r.r_dkb, c_dkb, *x_ring)
+    arrived(c_vx)
+    r.vz[z] = slots_total(r.vx)
+    c_vz = mail.same(r.vz.at[z], zp)
     arrived([d2y])
     r.u2y[...] = (r.tab[2, yl].astype(F32) + r.t2y[...].astype(F32)).astype(BF)
     d2z = mail.spread(lambda k: r.u2y.at[around(z, k)], r.t2z, zp)
-
-    arrived(c_dkv)
-    k_low = folded(dkv, r.r_dkv, 0).reshape(QK, CTX_ROWS).T.astype(BF)
-    v_low = folded(dkv, r.r_dkv, 1).reshape(QK, CTX_ROWS).T.astype(BF)
-    r.v_own[pl.ds(10 + yh, 1), 0:QK] = total(v_low.astype(F32))
-    r.vx[x] = r.v_own[...]
-    c_vx = mail.same(r.vx.at[x], xp)
+    arrived(c1y)
+    for half in range(2):
+        r.s1y[half * 2 : half * 2 + 2] = folded(w1, r.r1y, half).astype(BF)
+    c1x = mail.spread(lambda k: r.s1y.at[:, :, lanes(0, k)], r.r1x, xp)
+
+    arrived(c_dka + c_dkb)
+    k_low, v_low = (
+        jnp.concatenate(
+            [
+                folded(dkv(0, 2), r.r_dka, half).reshape(2 * 64, CTX_ROWS),
+                folded(dkv(2, 1), r.r_dkb, half).reshape(64, CTX_ROWS),
+            ],
+            axis=0,
+        ).T.astype(BF)
+        for half in range(2)
+    )
     r.tgp[...] += nt(k_low, weight_of(1)) + nt(v_low, weight_of(2))
-
-    def quarter(a, b):
-        return pl.ds((a * 2 + b) * ROWS, ROWS)
-
     c_sib = [mail.post(r.tgp.at[quarter(a, 1 - core)], r.got.at[a], sib) for a in range(2)]
-    cqz.append(project_grad(1, k_low))
-    cqz.append(project_grad(2, v_low))
+    arrived(coy)
+    r.rox[x] = added(r.soz[yh, yl], r.roy).astype(BF)
+    cox = mail.same(r.rox.at[x], xp)
+    arrived(c0y)
+    r.s0y[...] = added(r.s0z[yh, yl], r.r0y).astype(BF)
+    c0x = mail.spread(lambda k: r.s0y.at[:, lanes(0, k)], r.r0x, xp)
+    arrived([d0y])
+    r.u0y[...] = (r.u0z[yl].astype(F32) + r.t0y[...].astype(F32)).astype(BF)
+    d0x = mail.spread(lambda k: r.u0y.at[:, lanes(0, k)], r.t0x, xp)
     arrived(c_sib)
     s_far = r.rows.at[0, pl.ds(0, ROWS)]
     s_far[...] = (r.tgp[quarter(1 - yh, core), :] + r.got[1 - yh]).astype(BF)
     c_far = [mail.post(s_far, r.r_far, far)]
 
-    arrived(c0y)
-    r.s0y[...] = added(r.s0z[yh, yl], r.r0y).astype(BF)
-    c0x = mail.spread(lambda k: r.s0y.at[:, lanes(0, k)], r.r0x, xp)
-    arrived(coy)
-    r.rox[x] = added(r.soz[yh, yl], r.roy).astype(BF)
-    cox = mail.same(r.rox.at[x], xp)
+    arrived(cqz)
+    r.sqz[...] = added(r.wide[:, z, :, 0:QKV], r.rqz).astype(BF)
+    cqy = mail.post(r.sqz.at[1 - yl], r.rqy, low)
+    arrived(d1x)
+    r.u1x[...] = added(r.u1y[:, :, lanes(0, 0)], r.t1x).astype(BF)
+    d1z = mail.spread(lambda k: r.u1x.at[around(z, k)], r.t1z, zp)
+    arrived(c2z)
+    r.s2z[...] = added(r.s2x[:, :, z], r.r2z).astype(BF)
+    c2y = mail.spread(lambda k: r.s2z.at[ys[k][0], ys[k][1]], r.r2y, yp)
+    arrived(c_vz)
+    r.vy[y] = slots_total(r.vz)
+    c_vy = mail.same(r.vy.at[y], yp)
     arrived(c1x)
     r.s1x[...] = added(r.s1y[:, :, lanes(0, 0)], r.r1x).astype(BF)
     c1z = mail.spread(lambda k: r.s1x.at[around(z, k)], r.r1z, zp)
-    arrived([d0y])
-    r.u0y[...] = (r.u0z[yl].astype(F32) + r.t0y[...].astype(F32)).astype(BF)
-    d0x = mail.spread(lambda k: r.u0y.at[:, lanes(0, k)], r.t0x, xp)
-    arrived(d1x)
-    r.u1x[...] = added(r.u1y[:, :, lanes(0, 0)], r.t1x).astype(BF)
-    d1z = mail.spread(lambda k: r.u1x.at[around(z, k)], r.t1z, zp)
-    cqy = []
-    for j in range(3):
-        arrived(cqz[j])
-        r.sqz[j] = added(r.wide[:, z, :, j * QKW : j * QKW + QKP], r.rqz.at[j]).astype(BF)
-        cqy.append(mail.post(r.sqz.at[j, 1 - yl], r.rqy.at[j], low))
-    arrived(c_vx)
-    r.vz[z] = slots_total(r.vx)
-    c_vz = mail.same(r.vz.at[z], zp)
     arrived(d2z)
     r.u2z[...] = added(r.u2y[z], r.t2z).astype(BF)
     d2x = mail.spread(lambda k: r.u2z.at[:, lanes(0, k)], r.t2x, xp)
-    arrived(c_far)
-    r.tg[...] = r.tgp[quarter(yh, core), :] + r.got[yh] + r.r_far[...].astype(F32) + r.dh1s[...]
-    cqx = []
-    for j in range(3):
-        arrived([cqy[j]])
-        r.rqx[j, x] = (r.sqz[j, yl].astype(F32) + r.rqy[j].astype(F32)).astype(BF)
-        cqx.append(mail.same(r.rqx.at[j, x], xp))
-
-    late = []
-
-    def settle(ref, base, values):
-        ref[:, lanes(base, 0)] = values.astype(BF)
-        late.extend(mail.same(ref.at[:, lanes(base, 0)], xp))
-
     arrived(c0x)
     settle(r.f, 0, added(r.s0y[:, lanes(0, 0)], r.r0x))
+    arrived(d0x)
+    settle(r.ft.at[0], 0, added(r.u0y[:, lanes(0, 0)], r.t0x))
+    arrived([cqy])
+    r.rqx[x] = (r.sqz[yl].astype(F32) + r.rqy[...].astype(F32)).astype(BF)
+    cqx = mail.same(r.rqx.at[x], xp)
+
+    arrived(d1z)
+    settle(r.ft.at[1], 0, added(r.u1x[z], r.t1z))
+    arrived(c2y)
+    settle(r.f, 1024, added(r.s2z[yh, yl], r.r2y))
     arrived(c1z)
     settle(r.f, 512, added(r.s1x[z], r.r1z))
-    arrived(d0x)
-    settle(r.ft.at[0], 0, added(r.u0y[:, lanes(0, 0)], r.t0x))
-    arrived(d1z)
-    settle(r.ft.at[1], 0, added(r.u1x[z], r.t1z))
-    arrived(c_vz)
-    r.vy[y] = slots_total(r.vz)
-    c_vy = mail.same(r.vy.at[y], yp)
-    arrived(c2z)
-    r.s2z[...] = added(r.s2x[:, :, z], r.r2z).astype(BF)
-    c2y = mail.spread(lambda k: r.s2z.at[ys[k][0], ys[k][1]], r.r2y, yp)
     arrived(d2x)
     settle(r.ft.at[2], 0, added(r.u2z[:, lanes(0, 0)], r.t2x))
     arrived(c_vy)
     r.vc[0] = slots_total(r.vy)
     c_vc = mail.post(r.vc.at[0], r.vc.at[1], sib)
-    arrived(c2y)
-    settle(r.f, 1024, added(r.s2z[yh, yl], r.r2y))
     arrived(cox)
     r.fo[...] = slots_total(r.rox)
-    for j in range(3):
-        arrived(cqx[j])
-        r.fq[j] = slots_total(r.rqx.at[j])
+    arrived(c_far)
+    r.tg[...] = r.tgp[quarter(yh, core), :] + r.got[yh] + r.r_far[...].astype(F32) + r.dh1s[...]
+    arrived(cqx)
+    r.fq[...] = slots_total(r.rqx)
     arrived([c_vc])
     r.vsum[...] = r.vc[0]
     r.vsum[0:6, :] = r.vc[0, 0:6, :] + r.vc[1, 0:6, :]
@@ -862,7 +876,13 @@
         copy.start()
     for copy in copies[2:]:
         copy.wait()
-    gwq[...], gwk[...], gwv[...] = fq[0, :, :QK], fq[1, :, :QK], fq[2, :, :QK]
+    gwq[...] = fq[:, :QK]
+    rows = lax.broadcasted_iota(jnp.int32, (QKW, QK), 0)
+    cols = lax.broadcasted_iota(jnp.int32, (QKW, QK), 1)
+    wanted = cols // HEAD_DIM * WIDE + cols % HEAD_DIM
+    for out, shift in ((gwk, 0), (gwv, HEAD_DIM)):
+        pick = (rows == wanted + shift).astype(F32)
+        out[...] = jnp.dot(fq[:, QKP:], pick, precision=lax.Precision.HIGHEST)
     gwo[...] = fo[...].T[:QK]
     gwout_t[...] = f[:, :D].astype(F32)
     gwi[...] = f[:, D:].astype(F32)
@@ -901,7 +921,7 @@
         finish_kernel,
         out_shape=outs,
         in_specs=[hbm] * 9,
-        out_specs=[hbm] * 2 + [vm] * (len(outs) - 2),
+        out_specs=[vm] * len(outs),
         scratch_shapes=[
             *(pltpu.VMEM(entry.shape, entry.dtype) for entry in held),
             pltpu.SemaphoreType.DMA((9,)),

time: 175 us -> 153 us (0.87)
  Pallas kernels: 174 us -> 152 us
    pallas_call x1, Pallas kernels: 24.6 us -> 3.92 us  [finish(): pl.pallas_call(finish_kernel, out_shape=outs, in_specs=[hbm] * 9, out_spe...]
where the time goes in v4:
time: 153 us
  Pallas kernels  152 us (99%)
    pallas_call x1, Pallas kernels, layer(): pl.pallas_call(layer_kernel, out_shape=tuple((jax.ShapeDtypeStruct(*entry...  148 us
    pallas_call x1, Pallas kernels, finish(): pl.pallas_call(finish_kernel, out_shape=outs, in_specs=[hbm] * 9, out_spe...  3.92 us

profile of v4, /device:TPU:1, one launch (start us, length us, event | category | flops | bytes accessed | tf_op | source)
XLA Modules:
  0.0 152.9 jit_solution(3240543725888665092)
XLA Ops:
  0.7 148.1 %layer.1 = (bf16[160,768]{1,0:T(8,128)(2,1)}, f32[160,768]{1,0:T(8,128)}, bf16[96,1536]{1,0:T(8,128)(2,1)}, f32[96,256]{1,0:T(8,128)}, f32[96,640]{1,0:T(8,128)}...) custom-call(s32[1,20]{1,0:T(1,128)} %refs_0_.1, bf16[160,768]{1,0:T(8,128)(2,1)} %refs_1_.1, bf16[160,768]{1,0:T(8,128)(2,1)} %refs_2_.1, ...), custom_call_target="tpu_custom_call" | custom-call | tf_op jit(solution)/shard_map/layer/pallas_call | solution.py:839
  148.8 3.9 %finish.1 = (bf16[160,768]{1,0:T(8,128)(2,1)}, f32[160,768]{1,0:T(8,128)}, f32[96,192]{1,0:T(8,128)}, f32[96,192]{1,0:T(8,128)}, f32[96,192]{1,0:T(8,128)}, /*in...) custom-call(bf16[96,1536]{1,0:T(8,128)(2,1)} %get-tuple-element.43.r, ...), custom_call_target="tpu_custom_call" | custom-call | tf_op jit(solution)/shard_map/finish/pallas_call | solution.py:920

commit v5 on v4

--- a/solution.py
+++ b/solution.py
@@ -407,10 +407,10 @@
     arrived(own_low)
     low_z = mail.ring(ws_of(1 - yl), *z_ring)
     own_z2 = mail.ring_on(ws_of(yl), own_z, *z_ring)
+    arrived(tab_low)
+    low_tab = mail.ring(tab_of(1 - yl), *z_ring)
     own_x2 = mail.ring_on(tok_own, own_x, *x_ring)
     to_sib += mail.same(tok_own(1), [sib]) + mail.same(tok_own(3), [sib])
-    arrived(tab_low)
-    low_tab = mail.ring(tab_of(1 - yl), *z_ring)
     low_z2 = mail.ring_on(ws_of(1 - yl), low_z, *z_ring)
     far_x2 = mail.ring_on(tok_far, far_x, *x_ring)
     to_sib += mail.same(tok_far(1), [sib]) + mail.same(tok_far(3), [sib])

time: 153 us -> 153 us (level)
  no operation moved by 1% of the time
where the time goes in v5:
time: 153 us
  Pallas kernels  152 us (99%)
    pallas_call x1, Pallas kernels, layer(): pl.pallas_call(layer_kernel, out_shape=tuple((jax.ShapeDtypeStruct(*entry...  148 us
    pallas_call x1, Pallas kernels, finish(): pl.pallas_call(finish_kernel, out_shape=outs, in_specs=[hbm] * 9, out_spe...  3.92 us

profile of v5, /device:TPU:1, one launch (start us, length us, event | category | flops | bytes accessed | tf_op | source)
XLA Modules:
  0.0 153.0 jit_solution(3120528974366352049)
XLA Ops:
  0.7 148.2 %layer.1 = (bf16[160,768]{1,0:T(8,128)(2,1)}, f32[160,768]{1,0:T(8,128)}, bf16[96,1536]{1,0:T(8,128)(2,1)}, f32[96,256]{1,0:T(8,128)}, f32[96,640]{1,0:T(8,128)}...) custom-call(s32[1,20]{1,0:T(1,128)} %refs_0_.1, bf16[160,768]{1,0:T(8,128)(2,1)} %refs_1_.1, bf16[160,768]{1,0:T(8,128)(2,1)} %refs_2_.1, ...), custom_call_target="tpu_custom_call" | custom-call | tf_op jit(solution)/shard_map/layer/pallas_call | solution.py:839
  148.9 3.9 %finish.1 = (bf16[160,768]{1,0:T(8,128)(2,1)}, f32[160,768]{1,0:T(8,128)}, f32[96,192]{1,0:T(8,128)}, f32[96,192]{1,0:T(8,128)}, f32[96,192]{1,0:T(8,128)}, /*in...) custom-call(bf16[96,1536]{1,0:T(8,128)(2,1)} %get-tuple-element.43.r, ...), custom_call_target="tpu_custom_call" | custom-call | tf_op jit(solution)/shard_map/finish/pallas_call | solution.py:920
